TPU v7x, 768 devices: a whole 4x8x12 slice. The times are simulated.
768 devices in a mesh: intra: 16 (over y_hi, x), inter: 48 (over z, y_lo, core).
Axes of the slice: x: 4, y: 8 (y_hi: 4, y_lo: 2; y = y_hi * 2 + y_lo), z: 12, core: 2. Of those that a mesh axis runs over, the one named last changes fastest.
Arguments:
- tokens: bfloat16 [196608, 4096], P(('intra', 'inter')), may hold values from -6 to 6
- gain: bfloat16 [4096], replicated, may hold values from 0.099609375 to 1.8984375
- codes: bfloat16 [528, 4096], P('inter', 'intra'), may hold values from -127 to 127, as said below
- scales: bfloat16 [528, 32], P('inter', 'intra'), may hold values from 4.9829483e-05 to 0.00049972534
- cotangent: bfloat16 [196608, 528], P(('intra', 'inter')), may hold values from -12 to 12
Outputs:
- keys: bfloat16 [196608, 528], P(('intra', 'inter'))
- grad_tokens: bfloat16 [196608, 4096], P(('intra', 'inter'))
- grad_weight: float32 [528, 4096], P('inter', 'intra')
Inputs may be any that keep to these rules, and one draw needn't show every extreme that they name: `codes`: whole numbers.
All inputs are finite; a program needn't handle non-finite values.
Results may differ from a plain program's by a relative error of at most 0.017.
Values may be sent and summed in bfloat16 or wider, within the bound.
No kernel may reach another device: no remote copies, remote signals or barrier semaphores. Data moves between devices by JAX's collectives and lax.ppermute only.
A program may use at most 64 MiB of HBM per device.

v0:
```python
import jax
import jax.numpy as jnp
from jax import lax
from jax.sharding import PartitionSpec as P

EPS = 1e-05


def dequantize(quant, block_scales):
    height = quant.shape[0]
    width = quant.shape[1]
    nblocks = block_scales.shape[1]
    return (
        (
            quant.astype(jnp.float32).reshape(height, nblocks, width // nblocks)
            * block_scales.astype(jnp.float32)[:, :, None]
        )
        .reshape(height, width)
        .astype(jnp.bfloat16)
    )


def per_device(tokens, gain, codes, scales, cotangent):
    gain_f = gain.astype(jnp.float32)

    def normed_rows(values):
        meansq = jnp.mean(values * values, axis=-1, keepdims=True)
        return values * lax.rsqrt(meansq + EPS) * gain_f

    normed, back = jax.vjp(normed_rows, tokens.astype(jnp.float32))
    hidden = normed.astype(jnp.bfloat16)
    n_intra = lax.axis_size("intra")
    n_inter = lax.axis_size("inter")
    outw = codes.shape[0] * n_inter
    group_codes, group_scales = (
        lax.all_gather(codes, "inter", axis=0, tiled=True),
        lax.all_gather(scales, "inter", axis=0, tiled=True),
    )
    secondary = dequantize(group_codes, group_scales)
    full_weight = lax.all_gather(secondary, "intra", axis=1, tiled=True)
    keys = lax.dot_general(
        hidden, full_weight, (((1,), (1,)), ((), ())), preferred_element_type=jnp.float32
    ).astype(jnp.bfloat16)
    grad_hidden = jnp.dot(cotangent, full_weight, preferred_element_type=jnp.float32)
    grad_tokens = back(grad_hidden)[0].astype(jnp.bfloat16)
    feature_rows = hidden.shape[1] // n_intra
    within = lax.psum_scatter(
        lax.dot_general(
            hidden, cotangent, (((0,), (0,)), ((), ())), preferred_element_type=jnp.float32
        ).astype(jnp.bfloat16),
        "intra",
        scatter_dimension=0,
        tiled=True,
    ).astype(jnp.float32)
    grouped = within.reshape(feature_rows, n_inter, outw // n_inter)
    returned = lax.all_to_all(
        grouped.astype(jnp.bfloat16), "inter", split_axis=1, concat_axis=1, tiled=True
    ).astype(grouped.dtype)
    total = jnp.transpose(jnp.sum(returned, axis=1))
    grad_weight = total / (n_intra * n_inter)
    return (keys, grad_tokens, grad_weight)


def solution(mesh):
    placed = (
        P(("intra", "inter"), None),
        P(),
        P("inter", "intra"),
        P("inter", "intra"),
        P(("intra", "inter"), None),
    )
    return jax.shard_map(
        per_device,
        mesh=mesh,
        in_specs=placed,
        out_specs=(P(("intra", "inter"), None), P(("intra", "inter"), None), P("inter", "intra")),
        check_vma=False,
    )
```

profile of v0, /device:TPU:6, one launch (start us, length us, event | category | flops | bytes accessed | tf_op | source)
XLA Modules:
  0.0 361.8 jit_solution(12650943938939339576)
XLA Ops:
  7.2 0.0 copy-start
  7.2 0.0 copy-start.1
  7.2 0.0 all-gather.4.cloned.1.call-start
  7.2 58.4 %all-gather.1 = bf16[48,11,2]{1,2,0:T(2,128)(2,1)S(1)} all-gather(bf16[1,11,2]{1,2,0:T(2,128)(2,1)} %bitcast.21), channel_id=1, replica_groups=mesh['intra'=16,'inter'=48] {'inter'}, dimensions={0}, use_global_device_ids=true | all-gather | bytes 2156 | tf_op jit(solution)/shard_map/all_gather | solution.py:37
  65.6 0.1 copy.19
  65.7 0.1 copy.20
  65.8 0.1 reshape.34
  66.0 0.2 copy.21
  66.1 46.4 %all-gather = bf16[48,11,256]{2,1,0:T(8,128)(2,1)S(1)} all-gather(bf16[1,11,256]{2,1,0:T(8,128)(2,1)} %bitcast.20), channel_id=1, replica_groups=mesh['intra'=16,'inter'=48] {'inter'}, dimensions={0}, use_global_device_ids=true | all-gather | bytes 275968 | tf_op jit(solution)/shard_map/all_gather | solution.py:36
  112.5 0.1 reshape.33
  112.6 0.6 mul.74
  113.2 0.8 fusion.8
  114.0 0.0 all-gather.4.cloned.1.call-update
  114.0 0.0 reduce-scatter.2.cloned.1.call-start
  114.1 0.0 copy-done.1
  114.1 3.3 copy.18
  117.4 81.5 %all-gather.4.cloned.1.call-done = bf16[528,4096]{1,0:T(8,128)(2,1)} async-done(((bf16[528,256]{1,0:T(8,128)(2,1)}), bf16[528,4096]{1,0:T(8,128)(2,1)}) %all-gather.4.cloned.1.call-update) | async-done | bytes 4325392 | tf_op jit(solution)/shard_map/all_gather | solution.py:40
  198.9 0.0 copy-done
  198.9 6.9 %fusion.5 = (f32[256]{0:T(256)S(1)}, f32[256]{0:T(256)S(1)}, f32[256,4096]{0,1:T(8,128)}) fusion(bf16[256,4096]{0,1:T(8,128)(2,1)S(1)} %copy.18, f32[4096]{0:T(1024)S(1)} %convert_element_type.36, bf16[528,4096]{1,0:T(8,128)(2,1)} %all-gather.4.cloned.1.call-done, bf16[256,528]{0,1:T(8,128)(2,1)S(1)} %copy-done), kind=kOutput, calls=%fused_computation.12 | convolution fusion | flops 1113587200 | bytes 10905600 | tf_op jit(solution)/shard_map/dot_general | solution.py:44
  205.8 3.2 convolution_convert_fusion
  209.0 0.0 reduce-scatter.2.cloned.1.call-update
  209.0 111.4 %reduce-scatter.2.cloned.1.call-done = bf16[256,528]{0,1:T(8,128)(2,1)} async-done(((bf16[4096,528]{0,1:T(8,128)(2,1)}), bf16[256,528]{0,1:T(8,128)(2,1)}) %reduce-scatter.2.cloned.1.call-update) | async-done | bytes 270352 | tf_op jit(solution)/shard_map/reduce_scatter | solution.py:47
  320.4 1.8 convert_element_type.44
  322.2 11.0 %all-to-all-start = ((bf16[256,48,11]{0,2,1:T(8,128)(2,1)}), bf16[256,48,11]{0,2,1:T(8,128)(2,1)S(1)}, u32[]{:S(2)}, u32[]{:S(2)}) async-start(bf16[256,48,11]{0,2,1:T(8,128)(2,1)} %convert_element_type.44), calls=%async_computation.1 | async-start | bytes 786432 | tf_op jit(solution)/shard_map/all_to_all | solution.py:56
  333.2 4.4 %fusion.1 = bf16[256,4096]{0,1:T(8,128)(2,1)} fusion(bf16[256,4096]{0,1:T(8,128)(2,1)S(1)} %copy.18, f32[256,4096]{0,1:T(8,128)} %get-tuple-element.19, f32[256]{0:T(256)S(1)} %get-tuple-element.17, f32[256]{0:T(256)S(1)} %get-tuple-element.18), kind=kLoop, calls=%fused_computation.8 | loop fusion | flops 6291456 | bytes 8390656 | tf_op jit(solution)/shard_map/convert_element_type | solution.py:45
  337.6 4.1 %copy.22 = bf16[256,4096]{1,0:T(8,128)(2,1)} copy(bf16[256,4096]{0,1:T(8,128)(2,1)} %fusion.1) | data formatting | bytes 4194304
  341.7 4.4 %convolution_convert_fusion.1 = bf16[256,528]{0,1:T(8,128)(2,1)} fusion(bf16[528,4096]{1,0:T(8,128)(2,1)} %all-gather.4.cloned.1.call-done, bf16[256,4096]{0,1:T(8,128)(2,1)S(1)} %copy.18, f32[4096]{0:T(1024)S(1)} %convert_element_type.36, f32[256]{0:T(256)S(1)} %get-tuple-element.18), kind=kOutput, calls=%fused_computation.13 | convolution fusion | flops 1111625728 | bytes 6710272 | tf_op jit(solution)/shard_map/dot_general | solution.py:41
  346.1 8.2 %all-to-all-done = bf16[256,48,11]{0,2,1:T(8,128)(2,1)S(1)} async-done(((bf16[256,48,11]{0,2,1:T(8,128)(2,1)}), bf16[256,48,11]{0,2,1:T(8,128)(2,1)S(1)}, u32[]{:S(2)}, u32[]{:S(2)}) %all-to-all-start) | async-done | bytes 270368 | tf_op jit(solution)/shard_map/all_to_all | solution.py:56
  354.2 0.1 convert_reduce_fusion
  354.3 0.6 multiply_bitcast_fusion
  (2 shorter events, 0.0 us)
Async XLA Ops:
  7.2 191.7 %copy-start = (bf16[256,528]{0,1:T(8,128)(2,1)S(1)}, bf16[256,528]{0,1:T(8,128)(2,1)}, u32[]{:S(2)}) copy-start(bf16[256,528]{0,1:T(8,128)(2,1)} %param.9) | copy-start | bytes 811012
  7.2 106.9 %copy-start.1 = (bf16[4096]{0:T(1024)(128)(2,1)S(1)}, bf16[4096]{0:T(1024)(128)(2,1)}, u32[]{:S(2)}) copy-start(bf16[4096]{0:T(1024)(128)(2,1)} %param.6) | copy-start | bytes 24580
  7.2 191.7 %all-gather.4.cloned.1.call-start = ((), (), s32[]{:S(2)}) async-start(), calls=%async_computation.2 | async-start | bytes 4595712 | tf_op jit(solution)/shard_map/all_gather | solution.py:40
  114.0 206.4 %reduce-scatter.2.cloned.1.call-start = ((), (), s32[]{:S(2)}) async-start(), calls=%async_computation.3 | async-start | bytes 4595712 | tf_op jit(solution)/shard_map/reduce_scatter | solution.py:47
  322.2 32.0 %all-to-all-start = ((bf16[256,48,11]{0,2,1:T(8,128)(2,1)}), bf16[256,48,11]{0,2,1:T(8,128)(2,1)S(1)}, u32[]{:S(2)}, u32[]{:S(2)}) async-start(bf16[256,48,11]{0,2,1:T(8,128)(2,1)} %convert_element_type.44), calls=%async_computation.1 | async-start | bytes 786432 | tf_op jit(solution)/shard_map/all_to_all | solution.py:56
Sparse Core Ops, SparseCore 0:
  114.2 84.6 all-gather.3
  209.1 111.2 reduce-scatter.1
where the time goes:
time: 364 us; the launch traced here: 362 us
  waiting for transfers between devices  201 us (55%)
  blocking collectives  105 us (29%)
  matrix products  14.5 us (4%)
  between operations  14.1 us (4%)
  starting transfers between devices  11.1 us (3%)
  local copies, waits for them, and re-layouts  10.4 us (3%)
  other arithmetic  5.87 us (2%)
    reduce_scatter x1, waiting for transfers between devices, per_device(): lax.psum_scatter(lax.dot_general(hidden, cotangent, (((0,), (0,)), ((), (...  111 us
    all_gather x1, waiting for transfers between devices, per_device(): full_weight = lax.all_gather(secondary, 'intra', axis=1, tiled=True)  81.5 us
    all_gather x1, blocking collectives, per_device(): lax.all_gather(scales, 'inter', axis=0, tiled=True)  58.4 us
    all_gather x1, blocking collectives, per_device(): lax.all_gather(codes, 'inter', axis=0, tiled=True)  46.4 us
    all_to_all x1, starting transfers between devices, per_device(): lax.all_to_all(grouped.astype(jnp.bfloat16), 'inter', split_axis=1, conca...  11 us
    all_to_all x1, waiting for transfers between devices, per_device(): lax.all_to_all(grouped.astype(jnp.bfloat16), 'inter', split_axis=1, conca...  8.15 us
    unnamed x6, local copies, waits for them, and re-layouts  7.36 us
  transfers between devices with their start and end apart: 3, of which 3 were waited for; matrix products, arithmetic and copies ran while one was open for 4% of the time, Pallas kernels for 0%

commit v1 on v0

v1 whole, which is shorter than its diff:
```python
import numpy as np
import jax
import jax.numpy as jnp
from jax import lax
from jax.experimental import pallas as pl
from jax.experimental.pallas import tpu as pltpu
from jax.sharding import Mesh, PartitionSpec as P

EPS = 1e-05
COL = 256
VMEM = pl.BlockSpec(memory_space=pltpu.VMEM)
PARAMS = pltpu.CompilerParams(vmem_limit_bytes=48 * 1024 * 1024)


def row_orders(n_z, rows):
    group = -(-n_z * rows // 8) * 8
    grouped = np.full((4 * group, 1), -1, np.int32)
    natural = np.zeros((n_z * 4 * rows, 1), np.int32)
    for z in range(n_z):
        for y in range(2):
            for c in range(2):
                for r in range(rows):
                    o = ((z * 2 + y) * 2 + c) * rows + r
                    p = (c * 2 + y) * group + z * rows + r
                    grouped[p, 0] = o
                    natural[o, 0] = p
    return group, grouped, natural


def pick(index, width):
    lanes = lax.broadcasted_iota(jnp.int32, (index.shape[0], width), 1)
    return jnp.where(lanes == index, 1.0, 0.0).astype(jnp.bfloat16)


def dot(a, b, ca, cb):
    return lax.dot_general(a, b, (((ca,), (cb,)), ((), ())), preferred_element_type=jnp.float32)


def term_kernel(tokens, gain, cot, order, term, cot_grouped, inv):
    feats = tokens.shape[1]
    n_x, half = term.shape[1], term.shape[2]
    total = jnp.zeros((tokens.shape[0], COL), jnp.float32)
    for f in range(0, feats, COL):
        v = tokens[:, f : f + COL].astype(jnp.float32)
        total = total + v * v
    r = lax.rsqrt(jnp.sum(total, axis=1, keepdims=True) / feats + EPS)
    inv[...] = jnp.broadcast_to(r, inv.shape)
    for c in range(2):
        chosen = pick(order[c * half : (c + 1) * half, :], cot.shape[0])
        cot_grouped[c] = dot(chosen, cot[...], 1, 0).astype(jnp.bfloat16)
    for f in range(0, feats, COL):
        v = tokens[:, f : f + COL].astype(jnp.float32)
        hid = (v * r * gain[:, f : f + COL].astype(jnp.float32)).astype(jnp.bfloat16)
        y, x = divmod(f // COL, n_x)
        for c in range(2):
            term[c, x, :, y * COL : (y + 1) * COL] = dot(cot_grouped[c], hid, 1, 0).astype(jnp.bfloat16)


def main_kernel(tokens, gain, cot_grouped, inv, order, w, keys, grad, keys_acc, gh, dots):
    i = pl.program_id(0)
    n_x = pl.num_programs(0)
    toks, feats = tokens.shape
    half = w.shape[2]
    r = inv[:, :1]

    @pl.when(i == 0)
    def _():
        keys_acc[...] = jnp.zeros_like(keys_acc)
        dots[...] = jnp.zeros_like(dots)

    for y in range(w.shape[3] // COL):
        at = pl.ds(pl.multiple_of((y * n_x + i) * COL, COL), COL)
        cols = slice(y * COL, (y + 1) * COL)
        v = tokens[:, at].astype(jnp.float32)
        g = gain[:, at].astype(jnp.float32)
        hid = (v * r * g).astype(jnp.bfloat16)
        for c in range(2):
            keys_acc[c * half : (c + 1) * half, :] += dot(w[0, c, :, cols], hid, 1, 1)
        part = dot(cot_grouped[0], w[0, 0, :, cols], 0, 0) + dot(cot_grouped[1], w[0, 1, :, cols], 0, 0)
        part = part * g
        gh[:, at] = part
        dots[...] += v * part

    @pl.when(i == n_x - 1)
    def _():
        keys[...] = dot(pick(order[...], keys_acc.shape[0]), keys_acc[...].astype(jnp.bfloat16), 1, 0).astype(jnp.bfloat16)
        k = r * r * r * (jnp.sum(dots[...], axis=1, keepdims=True) / feats)
        for f in range(0, feats, COL):
            v = tokens[:, f : f + COL].astype(jnp.float32)
            grad[:, f : f + COL] = (r * gh[:, f : f + COL] - v * k).astype(jnp.bfloat16)


def per_device(tokens, gain, codes, scales, cotangent):
    n_y, n_x, n_z = (lax.axis_size(a) for a in ("y_hi", "x", "z"))
    rows, width = codes.shape
    toks, feats = tokens.shape
    outw = cotangent.shape[1]
    group, grouped, natural = row_orders(n_z, rows)
    half = 2 * group
    far = ("y_lo", "z", "y_hi")
    n_far = 2 * n_z * n_y

    with jax.named_scope("weight_far"):
        scale = jnp.repeat(scales.astype(jnp.float32), width // scales.shape[1], axis=1)
        own = (codes.astype(jnp.float32) * scale).astype(jnp.bfloat16)
        spread = jnp.broadcast_to(own[None], (n_far, rows, width))
        spread = lax.all_to_all(spread, far, split_axis=0, concat_axis=0, tiled=True)
        slab = spread.reshape(2, n_z, n_y, rows, width).transpose(0, 1, 3, 2, 4).reshape(2, n_z * rows, n_y * width)
        slab = jnp.pad(slab, ((0, 0), (0, group - n_z * rows), (0, 0))).reshape(half, n_y * width)
    with jax.named_scope("weight_near"):
        w = lax.all_gather(slab, ("x", "core"), axis=0, tiled=False).reshape(n_x, 2, half, n_y * width)

    gain_row = gain.reshape(1, feats)
    cot_t = cotangent.T
    with jax.named_scope("term"):
        term, cot_grouped, inv = pl.pallas_call(
            term_kernel,
            out_shape=(
                jax.ShapeDtypeStruct((2, n_x, half, n_y * width), jnp.bfloat16),
                jax.ShapeDtypeStruct((2, half, toks), jnp.bfloat16),
                jax.ShapeDtypeStruct((toks, 128), jnp.float32),
            ),
            in_specs=[VMEM] * 4,
            out_specs=(VMEM,) * 3,
            compiler_params=PARAMS,
        )(tokens, gain_row, cot_t, jnp.asarray(grouped))
    with jax.named_scope("reduce_core"):
        term, _ = lax.optimization_barrier((term, slab))
        core = lax.axis_index("core")
        mine = lax.dynamic_index_in_dim(term, core, 0, keepdims=False)
        theirs = lax.dynamic_index_in_dim(term, 1 - core, 0, keepdims=False)
        came = lax.ppermute(theirs, "core", ((0, 1), (1, 0)))
        pair = (mine.astype(jnp.float32) + came.astype(jnp.float32)).astype(jnp.bfloat16)
    with jax.named_scope("reduce_x"):
        parts = lax.all_to_all(pair, "x", split_axis=0, concat_axis=0, tiled=True)
        part = jnp.sum(parts.astype(jnp.float32), axis=0).astype(jnp.bfloat16)
    with jax.named_scope("reduce_far"):
        part = part.reshape(2, group, n_y, width)[:, : n_z * rows].reshape(2, n_z, rows, n_y, width)
        part = part.transpose(0, 1, 3, 2, 4).reshape(n_far, rows, width)
        last = lax.all_to_all(part, far, split_axis=0, concat_axis=0, tiled=True)
        grad_weight = jnp.sum(last.astype(jnp.float32), axis=0) / (n_y * n_x * n_z * 4)

    with jax.named_scope("main"):
        whole = lambda *shape: pl.BlockSpec(shape, lambda i: (0,) * len(shape))
        keys_t, grad_tokens = pl.pallas_call(
            main_kernel,
            grid=(n_x,),
            out_shape=(
                jax.ShapeDtypeStruct((outw, toks), jnp.bfloat16),
                jax.ShapeDtypeStruct((toks, feats), jnp.bfloat16),
            ),
            in_specs=[
                whole(toks, feats),
                whole(1, feats),
                whole(2, half, toks),
                whole(toks, 128),
                whole(outw, 1),
                pl.BlockSpec((1, 2, half, n_y * width), lambda i: (i, 0, 0, 0)),
            ],
            out_specs=(whole(outw, toks), whole(toks, feats)),
            scratch_shapes=[
                pltpu.VMEM((2 * half, toks), jnp.float32),
                pltpu.VMEM((toks, feats), jnp.float32),
                pltpu.VMEM((toks, COL), jnp.float32),
            ],
            compiler_params=PARAMS,
        )(tokens, gain_row, cot_grouped, inv, jnp.asarray(natural), w)
    return keys_t.T, grad_tokens, grad_weight


def solution(mesh):
    n_intra, n_inter = mesh.devices.shape
    fine = Mesh(mesh.devices.reshape(4, n_intra // 4, n_inter // 4, 2, 2), ("y_hi", "x", "z", "y_lo", "core"))
    intra, inter = ("y_hi", "x"), ("z", "y_lo", "core")
    placed = (P(intra + inter, None), P(), P(inter, intra), P(inter, intra), P(intra + inter, None))
    return jax.shard_map(
        per_device,
        mesh=fine,
        in_specs=placed,
        out_specs=(P(intra + inter, None), P(intra + inter, None), P(inter, intra)),
        check_vma=False,
    )
```

time: 364 us -> 200 us (0.55)
  waiting for transfers between devices: 201 us -> 4.67 us
  blocking collectives: 105 us -> 146 us
  matrix products: 14.5 us -> 0 us
  Pallas kernels: 0 us -> 12.6 us
  starting transfers between devices: 11.1 us -> 1.95 us
    all_to_all x0 -> x3, blocking collectives: none -> 146 us  [the longest x1 58.6 us: per_device(): lax.all_to_all(spread, far, split_axis=0, concat_axis=0, tiled=True)]
    reduce_scatter x1 -> x0, waiting for transfers between devices: 111 us -> none  [per_device(): lax.psum_scatter(lax.dot_general(hidden, cotangent, (((0,), (0,)), ((), (...]
    all_gather x2 -> x0, blocking collectives: 105 us -> none  [the longest x1 58.4 us: per_device(): lax.all_gather(scales, 'inter', axis=0, tiled=True)]
    all_gather x1, waiting for transfers between devices: 81.5 us -> 0.01 us  [per_device(): lax.all_gather(slab, ('x', 'core'), axis=0, tiled=False)]
    dot_general x3 -> x0, matrix products: 14.5 us -> none  [the longest x1 6.91 us: per_device(): jnp.dot(cotangent, full_weight, preferred_element_type=jnp.float32)]
    pallas_call x0 -> x2, Pallas kernels: none -> 12.6 us  [the longest x1 8.47 us: per_device(): pl.pallas_call(main_kernel, grid=(n_x,), out_shape=(jax.ShapeDtypeStruct(...]
    all_to_all x1 -> x0, starting transfers between devices: 11 us -> none  [per_device(): lax.all_to_all(grouped.astype(jnp.bfloat16), 'inter', split_axis=1, conca...]
    all_to_all x1 -> x0, waiting for transfers between devices: 8.15 us -> none  [per_device(): lax.all_to_all(grouped.astype(jnp.bfloat16), 'inter', split_axis=1, conca...]
  transfers between devices with their start and end apart: 3 -> 2, of which waited for: 3 -> 1; matrix products, arithmetic and copies ran while one was open for 4% -> 6% of each run, Pallas kernels for 0% -> 2%
where the time goes in v1:
time: 200 us; the launch traced here: 199 us
  blocking collectives  146 us (73%)
  between operations  14.1 us (7%)
  Pallas kernels  12.6 us (6%)
  local copies, waits for them, and re-layouts  12 us (6%)
  other arithmetic  7.08 us (4%)
  waiting for transfers between devices  4.67 us (2%)
    all_to_all x1, blocking collectives, per_device(): lax.all_to_all(spread, far, split_axis=0, concat_axis=0, tiled=True)  58.6 us
    all_to_all x1, blocking collectives, per_device(): last = lax.all_to_all(part, far, split_axis=0, concat_axis=0, tiled=True)  52.8 us
    all_to_all x1, blocking collectives, per_device(): parts = lax.all_to_all(pair, 'x', split_axis=0, concat_axis=0, tiled=True)  35.1 us
    pallas_call x1, Pallas kernels, per_device(): pl.pallas_call(main_kernel, grid=(n_x,), out_shape=(jax.ShapeDtypeStruct(...  8.47 us
    ppermute x1, waiting for transfers between devices, per_device(): came = lax.ppermute(theirs, 'core', ((0, 1), (1, 0)))  4.65 us
    pallas_call x1, Pallas kernels, per_device(): pl.pallas_call(term_kernel, out_shape=(jax.ShapeDtypeStruct((2, n_x, half...  4.09 us
  transfers between devices with their start and end apart: 2, of which 1 were waited for; matrix products, arithmetic and copies ran while one was open for 6% of the time, Pallas kernels for 2%

profile of v1, /device:TPU:6, one launch (start us, length us, event | category | flops | bytes accessed | tf_op | source)
XLA Modules:
  0.0 198.9 jit_solution(12518136058217865287)
XLA Ops:
  7.2 0.0 all-gather.2.cloned.1.call-start
  7.2 0.8 copy.16
  8.0 0.1 broadcast_in_dim.4
  8.1 0.7 multiply_convert_fusion
  8.8 0.1 broadcast_in_dim.10
  8.8 58.6 %all_to_all.15 = bf16[96,11,256]{2,1,0:T(8,128)(2,1)S(1)} all-to-all(bf16[96,11,256]{2,1,0:T(8,128)(2,1)S(1)} %broadcast_in_dim.10), channel_id=1, replica_groups=mesh['y_hi'=4,'x'=4,'z'=12,'y_lo'=2,'core'=2] {'y_lo','z','y_hi'}, dimensions={0} | all-to-all | bytes 1081344 | tf_op jit(solution)/shard_map/weight_far/all_to_all | solution.py:107
  67.4 0.0 copy-start.4
  67.4 0.0 copy-start
  67.4 0.0 copy-start.1
  67.4 0.0 copy-start.3
  67.4 1.1 copy.27
  68.5 2.2 %reshape.40 = bf16[2,132,1024]{2,1,0:T(8,128)(2,1)} reshape(bf16[2,12,11,4,256]{4,3,2,1,0:T(4,128)(2,1)} %bitcast.26) | data formatting | bytes 1081344 | tf_op jit(solution)/shard_map/weight_far/reshape | solution.py:108
  70.7 1.9 pad.4
  72.6 0.0 all-gather.2.cloned.1.call-update
  72.6 0.0 copy-done.4
  72.6 0.0 copy-done
  72.6 0.0 copy-done.1
  72.7 0.0 copy-done.3
  72.7 4.1 %term.1 = (bf16[2,4,272,1024]{3,2,1,0:T(8,128)(2,1)}, bf16[2,272,256]{2,1,0:T(8,128)(2,1)S(1)}, f32[256,128]{1,0:T(8,128)S(1)}) custom-call(bf16[256,4096]{1,0:T(8,128)(2,1)S(1)} %copy-done, bf16[1,4096]{1,0:T(2,128)(2,1)S(1)} %reshape.37.gain, bf16[528,256]{1,0:T(8,128)(2,1)S(1)} %bitcast.21, s32[544,1]{1,0:T(8,128)S(1)} %copy-done.1), custom_call_target="tpu_custom_call" | custom-call | tf_op jit(solution)/shard_map/term/pallas_call | solution.py:116
  76.8 3.3 %dynamic-slice_bitcast_fusion = bf16[4,272,1024]{2,1,0:T(8,128)(2,1)} fusion(bf16[2,4,272,1024]{3,2,1,0:T(8,128)(2,1)} %get-tuple-element.12, s32[]{:T(128)S(6)} %select_n.8), kind=kLoop, calls=%fused_computation.2 | loop fusion | bytes 4456452 | tf_op jit(solution)/shard_map/reduce_core/jit(dynamic_index_in_dim)/squeeze | solution.py:131
  80.0 1.9 collective-permute-start
  82.0 4.7 %collective-permute-done = bf16[4,272,1024]{2,1,0:T(8,128)(2,1)} collective-permute-done((bf16[4,272,1024]{2,1,0:T(8,128)(2,1)}, bf16[4,272,1024]{2,1,0:T(8,128)(2,1)}, u32[]{:S(2)}, u32[]{:S(2)}) %collective-permute-start) | collective-permute-done | bytes 2228256 | tf_op jit(solution)/shard_map/reduce_core/ppermute | solution.py:132
  86.6 3.5 %fusion = bf16[4,272,1024]{2,1,0:T(8,128)(2,1)S(1)} fusion(bf16[4,272,1024]{2,1,0:T(8,128)(2,1)} %collective-permute-done, bf16[2,4,272,1024]{3,2,1,0:T(8,128)(2,1)} %get-tuple-element.12, s32[]{:T(128)S(6)} %select_n.7), kind=kLoop, calls=%fused_computation.1 | loop fusion | flops 4456448 | bytes 6684676 | tf_op jit(solution)/shard_map/reduce_core/convert_element_type | solution.py:133
  90.1 35.1 %all_to_all.16 = bf16[4,272,1024]{2,1,0:T(8,128)(2,1)} all-to-all(bf16[4,272,1024]{2,1,0:T(8,128)(2,1)S(1)} %fusion), channel_id=1, replica_groups=mesh['y_hi'=4,'x'=4,'z'=12,'y_lo'=2,'core'=2] {'x'}, dimensions={0} | all-to-all | bytes 4456448 | tf_op jit(solution)/shard_map/reduce_x/all_to_all | solution.py:135
  125.2 2.1 %reduce_sum.21 = bf16[272,1024]{1,0:T(8,128)(2,1)S(1)} reduce(bf16[4,272,1024]{2,1,0:T(8,128)(2,1)} %all_to_all.16, bf16[]{:T(256)} %constant.21.clone.1), dimensions={0}, to_apply=%region_0.1 | reduce | flops 835584 | bytes 2785282 | tf_op jit(solution)/shard_map/reduce_x/reduce_sum | solution.py:136
  127.3 1.2 reshape.43
  128.5 0.0 copy-start.2
  128.5 1.3 slice.4
  129.8 0.1 copy.23
  129.9 52.8 %all_to_all.17 = bf16[96,11,256]{2,1,0:T(8,128)(2,1)S(1)} all-to-all(bf16[96,11,256]{2,1,0:T(8,128)(2,1)S(1)} %bitcast.24), channel_id=1, replica_groups=mesh['y_hi'=4,'x'=4,'z'=12,'y_lo'=2,'core'=2] {'y_lo','z','y_hi'}, dimensions={0} | all-to-all | bytes 1081344 | tf_op jit(solution)/shard_map/reduce_far/all_to_all | solution.py:140
  182.8 0.2 convert_reduce_fusion
  182.9 0.6 broadcast_multiply_fusion
  183.5 0.0 all-gather.2.cloned.1.call-done
  183.5 0.0 copy-done.2
  183.5 8.5 %main.1 = (bf16[528,256]{1,0:T(8,128)(2,1)}, bf16[256,4096]{1,0:T(8,128)(2,1)}) custom-call(bf16[256,4096]{1,0:T(8,128)(2,1)S(1)} %copy-done, bf16[1,4096]{1,0:T(2,128)(2,1)S(1)} %reshape.37.gain, bf16[2,272,256]{2,1,0:T(8,128)(2,1)S(1)} %get-tuple-element.8.cot_grouped, f32[256,128]{1,0:T(8,128)S(1)} %get-tuple-element.9.inv, s32[528,1]{1,0:T(8,128)S(1)} %copy-done.2, ...), custom_call_target="tpu_custom_call" | custom-call | tf_op jit(solution)/shard_map/main/pallas_call | solution.py:145
  (3 shorter events, 0.0 us)
Async XLA Ops:
  7.2 176.4 %all-gather.2.cloned.1.call-start = ((), (), s32[]{:S(2)}) async-start(), calls=%async_computation.3 | async-start | bytes 5013504 | tf_op jit(solution)/shard_map/weight_near/all_gather | solution.py:111
  67.4 5.2 %copy-start.4 = (bf16[4096]{0:T(1024)(128)(2,1)S(1)}, bf16[4096]{0:T(1024)(128)(2,1)}, u32[]{:S(2)}) copy-start(bf16[4096]{0:T(1024)(128)(2,1)} %param.8) | copy-start | bytes 24580
  67.4 5.2 %copy-start = (bf16[256,4096]{1,0:T(8,128)(2,1)S(1)}, bf16[256,4096]{1,0:T(8,128)(2,1)}, u32[]{:S(2)}) copy-start(bf16[256,4096]{1,0:T(8,128)(2,1)} %tokens.3) | copy-start | bytes 6291460
  67.4 5.2 %copy-start.1 = (s32[544,1]{1,0:T(8,128)S(1)}, s32[544,1]{1,0:T(8,128)}, u32[]{:S(2)}) copy-start(s32[544,1]{1,0:T(8,128)} %constant.29.clone.order) | copy-start | bytes 6532
  67.4 5.3 %copy-start.3 = (bf16[256,528]{0,1:T(8,128)(2,1)S(1)}, bf16[256,528]{0,1:T(8,128)(2,1)}, u32[]{:S(2)}) copy-start(bf16[256,528]{0,1:T(8,128)(2,1)} %param.11) | copy-start | bytes 811012
  80.0 6.6 %collective-permute-start = (bf16[4,272,1024]{2,1,0:T(8,128)(2,1)}, bf16[4,272,1024]{2,1,0:T(8,128)(2,1)}, u32[]{:S(2)}, u32[]{:S(2)}) collective-permute-start(bf16[4,272,1024]{2,1,0:T(8,128)(2,1)} %dynamic-slice_bitcast_fusion), channel_id=1, source_target_pairs={{0,1},{1,0},{2,3},{3,2},{4,5},{5,4},{6,7},{7,6},{8,9},{9,8},{10,11... | collective-permute-start | bytes 6684680 | tf_op jit(solution)/shard_map/reduce_core/ppermute | solution.py:132
  128.5 55.1 %copy-start.2 = (s32[528,1]{1,0:T(8,128)S(1)}, s32[528,1]{1,0:T(8,128)}, u32[]{:S(2)}) copy-start(s32[528,1]{1,0:T(8,128)} %constant.30.clone.order) | copy-start | bytes 6340
Sparse Core Ops, SparseCore 0:
  72.7 37.8 all-gather.1

commit v2 on v1

v2 whole, which is shorter than its diff:
```python
import jax
import jax.numpy as jnp
from jax import lax
from jax.experimental import pallas as pl
from jax.experimental.pallas import tpu as pltpu
from jax.sharding import Mesh, PartitionSpec as P

EPS = 1e-05
COL = 256
LANE = 128
VMEM = pl.BlockSpec(memory_space=pltpu.VMEM)
SMEM = pl.BlockSpec(memory_space=pltpu.SMEM)
PARAMS = pltpu.CompilerParams(vmem_limit_bytes=48 * 1024 * 1024)


def dot(a, b, ca, cb):
    return lax.dot_general(a, b, (((ca,), (cb,)), ((), ())), preferred_element_type=jnp.float32)


def term_kernel(n_y, n_x, place, tokens, gain, cot, mine, theirs, inv):
    feats = tokens.shape[1]
    total = jnp.zeros((tokens.shape[0], COL), jnp.float32)
    for f in range(0, feats, COL):
        v = tokens[:, f : f + COL].astype(jnp.float32)
        total = total + v * v
    r = lax.rsqrt(jnp.sum(total, axis=1, keepdims=True) / feats + EPS)
    inv[...] = jnp.broadcast_to(r, inv.shape)
    second = place[2] == 1
    for f in range(0, feats, COL):
        v = tokens[:, f : f + COL].astype(jnp.float32)
        hid = (v * r * gain[:, f : f + COL].astype(jnp.float32)).astype(jnp.bfloat16)
        y, x = divmod(f // COL, n_x)
        part = dot(cot[...], hid, 1, 0).astype(jnp.bfloat16)
        low, high = part[:, :LANE], part[:, LANE:]
        a, b = lax.rem(x + n_x - place[1], n_x), lax.rem(y + n_y - place[0], n_y)
        mine[a, b] = jnp.where(second, high, low)
        theirs[a, b] = jnp.where(second, low, high)


def main_kernel(n_y, place, tokens, gain, cot, inv, w, keys, grad, keys_acc, gh, dots):
    i = pl.program_id(0)
    n_x = pl.num_programs(0)
    toks, feats = tokens.shape
    r = inv[:, :1]

    @pl.when(i == 0)
    def _():
        keys_acc[...] = jnp.zeros_like(keys_acc)
        dots[...] = jnp.zeros_like(dots)

    for s in range(n_y):
        y = lax.rem(place[0] + n_y - s, n_y)
        at = pl.ds(pl.multiple_of((y * n_x + i) * COL, COL), COL)
        v = tokens[:, at].astype(jnp.float32)
        g = gain[:, at].astype(jnp.float32)
        hid = (v * r * g).astype(jnp.bfloat16)
        weight = jnp.concatenate([w[0, 0, s], w[0, 1, s]], axis=1)
        keys_acc[...] += dot(weight, hid, 1, 1)
        part = dot(cot[...], weight, 0, 0) * g
        gh[:, at] = part
        dots[...] += v * part

    @pl.when(i == n_x - 1)
    def _():
        keys[...] = keys_acc[...].astype(jnp.bfloat16)
        k = r * r * r * (jnp.sum(dots[...], axis=1, keepdims=True) / feats)
        for f in range(0, feats, COL):
            v = tokens[:, f : f + COL].astype(jnp.float32)
            grad[:, f : f + COL] = (r * gh[:, f : f + COL] - v * k).astype(jnp.bfloat16)


def shifted(value, axis, s):
    n = lax.axis_size(axis)
    return lax.ppermute(value, axis, [(j, (j + s) % n) for j in range(n)])


def add(values):
    total = values[0].astype(jnp.float32)
    for value in values[1:]:
        total = total + value.astype(jnp.float32)
    return total


def per_device(tokens, gain, codes, scales, cotangent):
    n_y, n_x, n_z = (lax.axis_size(a) for a in ("y_hi", "x", "z"))
    rows, width = codes.shape
    toks, feats = tokens.shape
    outw = cotangent.shape[1]
    inter = ("z", "y_lo", "core")
    n_inter = 4 * n_z
    place = jnp.stack([lax.axis_index(a) for a in ("y_hi", "x", "core")]).astype(jnp.int32)
    gain_row = gain.reshape(1, feats)
    cot_t = cotangent.T

    with jax.named_scope("term"):
        near = jax.ShapeDtypeStruct((n_x, n_y, outw, LANE), jnp.bfloat16)
        mine, theirs, inv = pl.pallas_call(
            lambda *refs: term_kernel(n_y, n_x, *refs),
            out_shape=(near, near, jax.ShapeDtypeStruct((toks, LANE), jnp.float32)),
            in_specs=[SMEM] + [VMEM] * 3,
            out_specs=(VMEM,) * 3,
            compiler_params=PARAMS,
        )(place, tokens, gain_row, cot_t)
    with jax.named_scope("reduce_core"):
        came = lax.ppermute(theirs, "core", ((0, 1), (1, 0)))

    with jax.named_scope("weight_far"):
        scale = jnp.repeat(scales.astype(jnp.float32), width // scales.shape[1], axis=1)
        own = (codes.astype(jnp.float32) * scale).astype(jnp.bfloat16)
        own, _ = lax.optimization_barrier((own, theirs))
        halves = jnp.stack([own[:, :LANE], own[:, LANE:]])
        spread = jnp.broadcast_to(halves[None], (n_inter // 2, 2, rows, LANE)).reshape(n_inter, rows, LANE)
        spread = lax.all_to_all(spread, inter, split_axis=0, concat_axis=0, tiled=True)
        strip = spread.reshape(outw, LANE)
    with jax.named_scope("weight_y"):
        slab = jnp.stack([strip] + [shifted(strip, "y_hi", s) for s in range(1, n_y)])
    with jax.named_scope("weight_near"):
        w = lax.all_gather(slab, ("x", "core"), axis=0, tiled=False).reshape(n_x, 2, n_y, outw, LANE)

    with jax.named_scope("reduce_x"):
        pairs = [add([mine[s], came[s]]).astype(jnp.bfloat16) for s in range(n_x)]
        part = add([pairs[0]] + [shifted(pairs[s], "x", s) for s in range(1, n_x)]).astype(jnp.bfloat16)
    with jax.named_scope("reduce_y"):
        part = add([part[0]] + [shifted(part[s], "y_hi", s) for s in range(1, n_y)]).astype(jnp.bfloat16)
    with jax.named_scope("reduce_far"):
        last = lax.all_to_all(part.reshape(n_inter, rows, LANE), inter, split_axis=0, concat_axis=0, tiled=True)
        last = jnp.sum(last.reshape(n_inter // 2, 2, rows, LANE).astype(jnp.float32), axis=0)
        grad_weight = jnp.concatenate([last[0], last[1]], axis=1) / (n_y * n_x * n_inter)

    with jax.named_scope("main"):
        whole = lambda *shape: pl.BlockSpec(shape, lambda i: (0,) * len(shape))
        keys_t, grad_tokens = pl.pallas_call(
            lambda *refs: main_kernel(n_y, *refs),
            grid=(n_x,),
            out_shape=(
                jax.ShapeDtypeStruct((outw, toks), jnp.bfloat16),
                jax.ShapeDtypeStruct((toks, feats), jnp.bfloat16),
            ),
            in_specs=[
                SMEM,
                whole(toks, feats),
                whole(1, feats),
                whole(outw, toks),
                whole(toks, LANE),
                pl.BlockSpec((1, 2, n_y, outw, LANE), lambda i: (i, 0, 0, 0, 0)),
            ],
            out_specs=(whole(outw, toks), whole(toks, feats)),
            scratch_shapes=[
                pltpu.VMEM((outw, toks), jnp.float32),
                pltpu.VMEM((toks, feats), jnp.float32),
                pltpu.VMEM((toks, COL), jnp.float32),
            ],
            compiler_params=PARAMS,
        )(place, tokens, gain_row, cot_t, inv, w)
    return keys_t.T, grad_tokens, grad_weight


def solution(mesh):
    n_intra, n_inter = mesh.devices.shape
    fine = Mesh(mesh.devices.reshape(4, n_intra // 4, n_inter // 4, 2, 2), ("y_hi", "x", "z", "y_lo", "core"))
    intra, inter = ("y_hi", "x"), ("z", "y_lo", "core")
    placed = (P(intra + inter, None), P(), P(inter, intra), P(inter, intra), P(intra + inter, None))
    return jax.shard_map(
        per_device,
        mesh=fine,
        in_specs=placed,
        out_specs=(P(intra + inter, None), P(intra + inter, None), P(inter, intra)),
        check_vma=False,
    )
```

time: 200 us -> 181 us (0.905)
  blocking collectives: 146 us -> 50.7 us
  waiting for transfers between devices: 4.67 us -> 53.7 us
  starting transfers between devices: 1.95 us -> 40.3 us
  local copies, waits for them, and re-layouts: 12 us -> 4.36 us
  other arithmetic: 7.08 us -> 3.2 us
    all_to_all x3 -> x2, blocking collectives: 146 us -> 50.7 us  [the longest x1 31.8 us: per_device(): lax.all_to_all(spread, inter, split_axis=0, concat_axis=0, tiled=True)]
    ppermute x0 -> x9, waiting for transfers between devices: none -> 49.3 us  [shifted(): return lax.ppermute(value, axis, [(j, (j + s) % n) for j in range(n)])]
    ppermute x0 -> x9, starting transfers between devices: none -> 38.3 us  [shifted(): return lax.ppermute(value, axis, [(j, (j + s) % n) for j in range(n)])]
    reshape x3, local copies, waits for them, and re-layouts: 3.51 us -> 0.19 us  [the longest x1 0.07 us: per_device(): jnp.stack([strip] + [shifted(strip, 'y_hi', s) for s in range(1, n_y)])]
    squeeze x1 -> x2, local copies, waits for them, and re-layouts: 3.28 us -> 0.03 us  [the longest x1 0.03 us: per_device(): part[s]]
    convert_element_type x1 -> x3, other arithmetic: 3.51 us -> 0.88 us  [the longest x1 0.42 us: per_device(): pairs = [add([mine[s], came[s]]).astype(jnp.bfloat16) for s in range(n_x)]]
    unnamed x12 -> x10, local copies, waits for them, and re-layouts: 0.03 us -> 2.57 us
    reduce_sum x2 -> x1, other arithmetic: 2.26 us -> 0.04 us  [per_device(): jnp.sum(last.reshape(n_inter // 2, 2, rows, LANE).astype(jnp.float32), ax...]
  transfers between devices with their start and end apart: 2 -> 11, of which waited for: 1 -> 8; matrix products, arithmetic and copies ran while one was open for 6% -> 1% of each run, Pallas kernels for 2% -> 0%
where the time goes in v2:
time: 181 us; the launch traced here: 178 us
  waiting for transfers between devices  53.7 us (30%)
  blocking collectives  50.7 us (28%)
  starting transfers between devices  40.3 us (22%)
  between operations  14.2 us (8%)
  Pallas kernels  12 us (7%)
  local copies, waits for them, and re-layouts  4.36 us (2%)
  other arithmetic  3.2 us (2%)
    ppermute x9, waiting for transfers between devices, shifted(): return lax.ppermute(value, axis, [(j, (j + s) % n) for j in range(n)])  49.3 us
    ppermute x9, starting transfers between devices, shifted(): return lax.ppermute(value, axis, [(j, (j + s) % n) for j in range(n)])  38.3 us
    all_to_all x1, blocking collectives, per_device(): lax.all_to_all(spread, inter, split_axis=0, concat_axis=0, tiled=True)  31.8 us
    all_to_all x1, blocking collectives, per_device(): lax.all_to_all(part.reshape(n_inter, rows, LANE), inter, split_axis=0, co...  18.9 us
    pallas_call x1, Pallas kernels, per_device(): pl.pallas_call(lambda *refs: main_kernel(n_y, *refs), grid=(n_x,), out_sh...  7.9 us
    ppermute x1, waiting for transfers between devices, per_device(): came = lax.ppermute(theirs, 'core', ((0, 1), (1, 0)))  4.43 us
    pallas_call x1, Pallas kernels, per_device(): pl.pallas_call(lambda *refs: term_kernel(n_y, n_x, *refs), out_shape=(nea...  4.09 us
  transfers between devices with their start and end apart: 11, of which 8 were waited for; matrix products, arithmetic and copies ran while one was open for 1% of the time, Pallas kernels for 0%

profile of v2, /device:TPU:6, one launch (start us, length us, event | category | flops | bytes accessed | tf_op | source)
XLA Modules:
  0.0 178.5 jit_solution(17385600134518824306)
XLA Ops:
  7.2 0.0 all-gather.3.cloned.1.call-start
  7.2 0.7 reshape.51.refs_2_
  7.9 0.8 copy.10
  8.7 0.1 broadcast_in_dim.4
  8.8 0.7 multiply_convert_fusion
  9.5 0.1 pad_add_fusion.refs_0_
  9.6 0.0 copy-start
  9.6 1.6 copy-done
  11.2 0.0 copy-start.2
  11.2 1.0 copy-done.2
  12.1 4.1 %term.1 = (bf16[4,4,528,128]{3,2,1,0:T(8,128)(2,1)S(1)}, bf16[4,4,528,128]{3,2,1,0:T(8,128)(2,1)}, f32[256,128]{1,0:T(8,128)S(1)}) custom-call(s32[3]{0:T(128)S(1)} %pad_add_fusion.refs_0_, bf16[256,4096]{1,0:T(8,128)(2,1)S(1)} %copy-done, bf16[1,4096]{1,0:T(2,128)(2,1)S(1)} %reshape.51.refs_2_, bf16[528,256]{1,0:T(8,128)(2,1)S(1)} %bitcast.45), custom_call_target="tpu_custom_call" | custom-call | tf_op jit(solution)/shard_map/term/pallas_call | solution.py:97
  16.2 31.8 %all_to_all.10 = bf16[48,11,128]{2,1,0:T(8,128)(2,1)S(1)} all-to-all(bf16[48,11,128]{2,1,0:T(8,128)(2,1)S(1)} %bitcast.48), channel_id=1, replica_groups=mesh['y_hi'=4,'x'=4,'z'=12,'y_lo'=2,'core'=2] {'z','y_lo','core'}, dimensions={0} | all-to-all | bytes 270336 | tf_op jit(solution)/shard_map/weight_far/all_to_all | solution.py:113
  48.0 0.1 reshape.55
  48.1 4.5 %collective-permute-start = (bf16[528,128]{1,0:T(8,128)(2,1)S(1)}, bf16[528,128]{1,0:T(8,128)(2,1)S(1)}, u32[]{:S(2)}, u32[]{:S(2)}) collective-permute-start(bf16[528,128]{1,0:T(8,128)(2,1)S(1)} %reshape.55), channel_id=1, source_target_pairs={{0,192},{192,384},{384,576},{576,0},{1,193},{193,385},{385,577},{5... | collective-permute-start | bytes 405512 | tf_op jit(solution)/shard_map/weight_y/ppermute | solution.py:74
  52.6 5.0 %collective-permute-start.1 = (bf16[528,128]{1,0:T(8,128)(2,1)S(1)}, bf16[528,128]{1,0:T(8,128)(2,1)S(1)}, u32[]{:S(2)}, u32[]{:S(2)}) collective-permute-start(bf16[528,128]{1,0:T(8,128)(2,1)S(1)} %reshape.55), channel_id=1, source_target_pairs={{0,384},{192,576},{384,0},{576,192},{1,385},{193,577},{385,1},{577... | collective-permute-start | bytes 405512 | tf_op jit(solution)/shard_map/weight_y/ppermute | solution.py:74
  57.7 5.3 %collective-permute-start.2 = (bf16[528,128]{1,0:T(8,128)(2,1)S(1)}, bf16[528,128]{1,0:T(8,128)(2,1)S(1)}, u32[]{:S(2)}, u32[]{:S(2)}) collective-permute-start(bf16[528,128]{1,0:T(8,128)(2,1)S(1)} %reshape.55), channel_id=1, source_target_pairs={{0,576},{192,0},{384,192},{576,384},{1,577},{193,1},{385,193},{577... | collective-permute-start | bytes 405512 | tf_op jit(solution)/shard_map/weight_y/ppermute | solution.py:74
  62.9 0.1 reshape.54
  63.0 0.0 collective-permute-done
  63.0 2.8 %collective-permute-done.1 = bf16[528,128]{1,0:T(8,128)(2,1)S(1)} collective-permute-done((bf16[528,128]{1,0:T(8,128)(2,1)S(1)}, bf16[528,128]{1,0:T(8,128)(2,1)S(1)}, u32[]{:S(2)}, u32[]{:S(2)}) %collective-permute-start.1) | collective-permute-done | bytes 135200 | tf_op jit(solution)/shard_map/weight_y/ppermute | solution.py:74
  65.8 3.9 %collective-permute-done.2 = bf16[528,128]{1,0:T(8,128)(2,1)S(1)} collective-permute-done((bf16[528,128]{1,0:T(8,128)(2,1)S(1)}, bf16[528,128]{1,0:T(8,128)(2,1)S(1)}, u32[]{:S(2)}, u32[]{:S(2)}) %collective-permute-start.2) | collective-permute-done | bytes 135200 | tf_op jit(solution)/shard_map/weight_y/ppermute | solution.py:74
  69.8 0.9 pad_maximum_fusion
  70.6 0.0 all-gather.3.cloned.1.call-update
  70.7 1.9 %collective-permute-start.3 = (bf16[4,4,528,128]{3,2,1,0:T(8,128)(2,1)}, bf16[4,4,528,128]{3,2,1,0:T(8,128)(2,1)S(1)}, u32[]{:S(2)}, u32[]{:S(2)}) collective-permute-start(bf16[4,4,528,128]{3,2,1,0:T(8,128)(2,1)} %get-tuple-element.10), channel_id=1, source_target_pairs={{0,1},{1,0},{2,3},{3,2},{4,5},{5,4},{6,7},{7,6},{8,9},{9,8},{10,11... | collective-permute-start | bytes 6488072 | tf_op jit(solution)/shard_map/reduce_core/ppermute | solution.py:105
  72.6 4.4 %collective-permute-done.3 = bf16[4,4,528,128]{3,2,1,0:T(8,128)(2,1)S(1)} collective-permute-done((bf16[4,4,528,128]{3,2,1,0:T(8,128)(2,1)}, bf16[4,4,528,128]{3,2,1,0:T(8,128)(2,1)S(1)}, u32[]{:S(2)}, u32[]{:S(2)}) %collective-permute-start.3) | collective-permute-done | bytes 2162720 | tf_op jit(solution)/shard_map/reduce_core/ppermute | solution.py:105
  77.0 0.4 fusion.4
  77.4 2.4 %collective-permute-start.4 = (bf16[4,528,128]{2,1,0:T(8,128)(2,1)S(1)}, bf16[4,528,128]{2,1,0:T(8,128)(2,1)S(1)}, u32[]{:S(2)}, u32[]{:S(2)}) collective-permute-start(bf16[4,528,128]{2,1,0:T(8,128)(2,1)S(1)} %get-tuple-element.15), channel_id=1, source_target_pairs={{0,48},{48,96},{96,144},{144,0},{1,49},{49,97},{97,145},{145,1},{2... | collective-permute-start | bytes 1622024 | tf_op jit(solution)/shard_map/reduce_x/ppermute | solution.py:74
  79.9 4.3 %collective-permute-start.5 = (bf16[4,528,128]{2,1,0:T(8,128)(2,1)S(1)}, bf16[4,528,128]{2,1,0:T(8,128)(2,1)S(1)}, u32[]{:S(2)}, u32[]{:S(2)}) collective-permute-start(bf16[4,528,128]{2,1,0:T(8,128)(2,1)S(1)} %get-tuple-element.17), channel_id=1, source_target_pairs={{0,96},{48,144},{96,0},{144,48},{1,97},{49,145},{97,1},{145,49},{2... | collective-permute-start | bytes 1622024 | tf_op jit(solution)/shard_map/reduce_x/ppermute | solution.py:74
  84.2 1.9 %collective-permute-start.6 = (bf16[4,528,128]{2,1,0:T(8,128)(2,1)S(1)}, bf16[4,528,128]{2,1,0:T(8,128)(2,1)S(1)}, u32[]{:S(2)}, u32[]{:S(2)}) collective-permute-start(bf16[4,528,128]{2,1,0:T(8,128)(2,1)S(1)} %get-tuple-element.16), channel_id=1, source_target_pairs={{0,144},{48,0},{96,48},{144,96},{1,145},{49,1},{97,49},{145,97},{2... | collective-permute-start | bytes 1622024 | tf_op jit(solution)/shard_map/reduce_x/ppermute | solution.py:74
  86.1 17.5 %collective-permute-done.4 = bf16[4,528,128]{2,1,0:T(8,128)(2,1)S(1)} collective-permute-done((bf16[4,528,128]{2,1,0:T(8,128)(2,1)S(1)}, bf16[4,528,128]{2,1,0:T(8,128)(2,1)S(1)}, u32[]{:S(2)}, u32[]{:S(2)}) %collective-permute-start.4) | collective-permute-done | bytes 540704 | tf_op jit(solution)/shard_map/reduce_x/ppermute | solution.py:74
  103.6 4.2 %collective-permute-done.5 = bf16[4,528,128]{2,1,0:T(8,128)(2,1)S(1)} collective-permute-done((bf16[4,528,128]{2,1,0:T(8,128)(2,1)S(1)}, bf16[4,528,128]{2,1,0:T(8,128)(2,1)S(1)}, u32[]{:S(2)}, u32[]{:S(2)}) %collective-permute-start.5) | collective-permute-done | bytes 540704 | tf_op jit(solution)/shard_map/reduce_x/ppermute | solution.py:74
  107.8 16.8 %collective-permute-done.6 = bf16[4,528,128]{2,1,0:T(8,128)(2,1)S(1)} collective-permute-done((bf16[4,528,128]{2,1,0:T(8,128)(2,1)S(1)}, bf16[4,528,128]{2,1,0:T(8,128)(2,1)S(1)}, u32[]{:S(2)}, u32[]{:S(2)}) %collective-permute-start.6) | collective-permute-done | bytes 540704 | tf_op jit(solution)/shard_map/reduce_x/ppermute | solution.py:74
  124.7 0.4 fusion.2
  125.1 0.0 copy-start.1
  125.1 0.0 copy-start.3
  125.1 4.5 %collective-permute-start.7 = (bf16[528,128]{1,0:T(8,128)(2,1)S(1)}, bf16[528,128]{1,0:T(8,128)(2,1)S(1)}, u32[]{:S(2)}, u32[]{:S(2)}) collective-permute-start(bf16[528,128]{1,0:T(8,128)(2,1)S(1)} %get-tuple-element.18), channel_id=1, source_target_pairs={{0,192},{192,384},{384,576},{576,0},{1,193},{193,385},{385,577},{5... | collective-permute-start | bytes 405512 | tf_op jit(solution)/shard_map/reduce_y/ppermute | solution.py:74
  129.7 5.2 %collective-permute-start.8 = (bf16[528,128]{1,0:T(8,128)(2,1)S(1)}, bf16[528,128]{1,0:T(8,128)(2,1)S(1)}, u32[]{:S(2)}, u32[]{:S(2)}) collective-permute-start(bf16[528,128]{1,0:T(8,128)(2,1)S(1)} %get-tuple-element.20), channel_id=1, source_target_pairs={{0,384},{192,576},{384,0},{576,192},{1,385},{193,577},{385,1},{577... | collective-permute-start | bytes 405512 | tf_op jit(solution)/shard_map/reduce_y/ppermute | solution.py:74
  134.9 5.2 %collective-permute-start.9 = (bf16[528,128]{1,0:T(8,128)(2,1)S(1)}, bf16[528,128]{1,0:T(8,128)(2,1)S(1)}, u32[]{:S(2)}, u32[]{:S(2)}) collective-permute-start(bf16[528,128]{1,0:T(8,128)(2,1)S(1)} %get-tuple-element.19), channel_id=1, source_target_pairs={{0,576},{192,0},{384,192},{576,384},{1,577},{193,1},{385,193},{577... | collective-permute-start | bytes 405512 | tf_op jit(solution)/shard_map/reduce_y/ppermute | solution.py:74
  140.0 0.0 collective-permute-done.7
  140.0 2.2 %collective-permute-done.8 = bf16[528,128]{1,0:T(8,128)(2,1)S(1)} collective-permute-done((bf16[528,128]{1,0:T(8,128)(2,1)S(1)}, bf16[528,128]{1,0:T(8,128)(2,1)S(1)}, u32[]{:S(2)}, u32[]{:S(2)}) %collective-permute-start.8) | collective-permute-done | bytes 135200 | tf_op jit(solution)/shard_map/reduce_y/ppermute | solution.py:74
  142.2 1.7 collective-permute-done.9
  144.0 0.1 fusion.9
  144.0 0.1 reshape.57
  144.1 18.9 %all_to_all.11 = bf16[48,11,128]{2,1,0:T(8,128)(2,1)S(1)} all-to-all(bf16[48,11,128]{2,1,0:T(8,128)(2,1)S(1)} %reshape.57), channel_id=1, replica_groups=mesh['y_hi'=4,'x'=4,'z'=12,'y_lo'=2,'core'=2] {'z','y_lo','core'}, dimensions={0} | all-to-all | bytes 270336 | tf_op jit(solution)/shard_map/reduce_far/all_to_all | solution.py:126
  163.1 0.6 maximum_multiply_fusion
  163.7 0.0 all-gather.3.cloned.1.call-done
  163.7 0.0 copy-done.1
  163.7 0.0 copy-done.3
  163.7 7.9 %main.1 = (bf16[528,256]{1,0:T(8,128)(2,1)}, bf16[256,4096]{1,0:T(8,128)(2,1)}) custom-call(s32[3]{0:T(128)S(1)} %pad_add_fusion.refs_0_, bf16[256,4096]{1,0:T(8,128)(2,1)S(1)} %copy-done.1, bf16[1,4096]{1,0:T(2,128)(2,1)S(1)} %reshape.51.refs_2_, bf16[528,256]{1,0:T(8,128)(2,1)S(1)} %bitcast.46, f32[256,128]{1,0:T(8,128)S(1)} %get-tuple-element.9.refs_4_, ...), custom_call_target="tpu_custom_call" | custom-call | tf_op jit(solution)/shard_map/main/pallas_call | solution.py:132
  (8 shorter events, 0.1 us)
Async XLA Ops:
  7.2 156.6 %all-gather.3.cloned.1.call-start = ((), (), s32[]{:S(2)}) async-start(), calls=%async_computation.2 | async-start | bytes 4866048 | tf_op jit(solution)/shard_map/weight_near/all_gather | solution.py:118
  9.6 1.6 copy-start
  11.2 1.0 copy-start.2
  48.1 14.9 %collective-permute-start = (bf16[528,128]{1,0:T(8,128)(2,1)S(1)}, bf16[528,128]{1,0:T(8,128)(2,1)S(1)}, u32[]{:S(2)}, u32[]{:S(2)}) collective-permute-start(bf16[528,128]{1,0:T(8,128)(2,1)S(1)} %reshape.55), channel_id=1, source_target_pairs={{0,192},{192,384},{384,576},{576,0},{1,193},{193,385},{385,577},{5... | collective-permute-start | bytes 405512 | tf_op jit(solution)/shard_map/weight_y/ppermute | solution.py:74
  52.6 13.2 %collective-permute-start.1 = (bf16[528,128]{1,0:T(8,128)(2,1)S(1)}, bf16[528,128]{1,0:T(8,128)(2,1)S(1)}, u32[]{:S(2)}, u32[]{:S(2)}) collective-permute-start(bf16[528,128]{1,0:T(8,128)(2,1)S(1)} %reshape.55), channel_id=1, source_target_pairs={{0,384},{192,576},{384,0},{576,192},{1,385},{193,577},{385,1},{577... | collective-permute-start | bytes 405512 | tf_op jit(solution)/shard_map/weight_y/ppermute | solution.py:74
  57.7 12.1 %collective-permute-start.2 = (bf16[528,128]{1,0:T(8,128)(2,1)S(1)}, bf16[528,128]{1,0:T(8,128)(2,1)S(1)}, u32[]{:S(2)}, u32[]{:S(2)}) collective-permute-start(bf16[528,128]{1,0:T(8,128)(2,1)S(1)} %reshape.55), channel_id=1, source_target_pairs={{0,576},{192,0},{384,192},{576,384},{1,577},{193,1},{385,193},{577... | collective-permute-start | bytes 405512 | tf_op jit(solution)/shard_map/weight_y/ppermute | solution.py:74
  70.7 6.4 %collective-permute-start.3 = (bf16[4,4,528,128]{3,2,1,0:T(8,128)(2,1)}, bf16[4,4,528,128]{3,2,1,0:T(8,128)(2,1)S(1)}, u32[]{:S(2)}, u32[]{:S(2)}) collective-permute-start(bf16[4,4,528,128]{3,2,1,0:T(8,128)(2,1)} %get-tuple-element.10), channel_id=1, source_target_pairs={{0,1},{1,0},{2,3},{3,2},{4,5},{5,4},{6,7},{7,6},{8,9},{9,8},{10,11... | collective-permute-start | bytes 6488072 | tf_op jit(solution)/shard_map/reduce_core/ppermute | solution.py:105
  77.4 26.2 %collective-permute-start.4 = (bf16[4,528,128]{2,1,0:T(8,128)(2,1)S(1)}, bf16[4,528,128]{2,1,0:T(8,128)(2,1)S(1)}, u32[]{:S(2)}, u32[]{:S(2)}) collective-permute-start(bf16[4,528,128]{2,1,0:T(8,128)(2,1)S(1)} %get-tuple-element.15), channel_id=1, source_target_pairs={{0,48},{48,96},{96,144},{144,0},{1,49},{49,97},{97,145},{145,1},{2... | collective-permute-start | bytes 1622024 | tf_op jit(solution)/shard_map/reduce_x/ppermute | solution.py:74
  79.9 28.0 %collective-permute-start.5 = (bf16[4,528,128]{2,1,0:T(8,128)(2,1)S(1)}, bf16[4,528,128]{2,1,0:T(8,128)(2,1)S(1)}, u32[]{:S(2)}, u32[]{:S(2)}) collective-permute-start(bf16[4,528,128]{2,1,0:T(8,128)(2,1)S(1)} %get-tuple-element.17), channel_id=1, source_target_pairs={{0,96},{48,144},{96,0},{144,48},{1,97},{49,145},{97,1},{145,49},{2... | collective-permute-start | bytes 1622024 | tf_op jit(solution)/shard_map/reduce_x/ppermute | solution.py:74
  84.2 40.5 %collective-permute-start.6 = (bf16[4,528,128]{2,1,0:T(8,128)(2,1)S(1)}, bf16[4,528,128]{2,1,0:T(8,128)(2,1)S(1)}, u32[]{:S(2)}, u32[]{:S(2)}) collective-permute-start(bf16[4,528,128]{2,1,0:T(8,128)(2,1)S(1)} %get-tuple-element.16), channel_id=1, source_target_pairs={{0,144},{48,0},{96,48},{144,96},{1,145},{49,1},{97,49},{145,97},{2... | collective-permute-start | bytes 1622024 | tf_op jit(solution)/shard_map/reduce_x/ppermute | solution.py:74
  125.1 38.7 %copy-start.1 = (bf16[256,4096]{1,0:T(8,128)(2,1)S(1)}, bf16[256,4096]{1,0:T(8,128)(2,1)}, u32[]{:S(2)}) copy-start(bf16[256,4096]{1,0:T(8,128)(2,1)} %refs_1_.3) | copy-start | bytes 6291460
  125.1 38.6 %copy-start.3 = (bf16[256,528]{0,1:T(8,128)(2,1)S(1)}, bf16[256,528]{0,1:T(8,128)(2,1)}, u32[]{:S(2)}) copy-start(bf16[256,528]{0,1:T(8,128)(2,1)} %param.9) | copy-start | bytes 811012
  125.1 14.9 %collective-permute-start.7 = (bf16[528,128]{1,0:T(8,128)(2,1)S(1)}, bf16[528,128]{1,0:T(8,128)(2,1)S(1)}, u32[]{:S(2)}, u32[]{:S(2)}) collective-permute-start(bf16[528,128]{1,0:T(8,128)(2,1)S(1)} %get-tuple-element.18), channel_id=1, source_target_pairs={{0,192},{192,384},{384,576},{576,0},{1,193},{193,385},{385,577},{5... | collective-permute-start | bytes 405512 | tf_op jit(solution)/shard_map/reduce_y/ppermute | solution.py:74
  129.7 12.6 %collective-permute-start.8 = (bf16[528,128]{1,0:T(8,128)(2,1)S(1)}, bf16[528,128]{1,0:T(8,128)(2,1)S(1)}, u32[]{:S(2)}, u32[]{:S(2)}) collective-permute-start(bf16[528,128]{1,0:T(8,128)(2,1)S(1)} %get-tuple-element.20), channel_id=1, source_target_pairs={{0,384},{192,576},{384,0},{576,192},{1,385},{193,577},{385,1},{577... | collective-permute-start | bytes 405512 | tf_op jit(solution)/shard_map/reduce_y/ppermute | solution.py:74
  134.9 9.1 %collective-permute-start.9 = (bf16[528,128]{1,0:T(8,128)(2,1)S(1)}, bf16[528,128]{1,0:T(8,128)(2,1)S(1)}, u32[]{:S(2)}, u32[]{:S(2)}) collective-permute-start(bf16[528,128]{1,0:T(8,128)(2,1)S(1)} %get-tuple-element.19), channel_id=1, source_target_pairs={{0,576},{192,0},{384,192},{576,384},{1,577},{193,1},{385,193},{577... | collective-permute-start | bytes 405512 | tf_op jit(solution)/shard_map/reduce_y/ppermute | solution.py:74
Sparse Core Ops, SparseCore 0:
  70.8 56.2 all-gather.2

commit v3 on v1

v3 whole, which is shorter than its diff:
```python
import numpy as np
import jax
import jax.numpy as jnp
from jax import lax
from jax.experimental import pallas as pl
from jax.experimental.pallas import tpu as pltpu
from jax.sharding import Mesh, PartitionSpec as P

EPS = 1e-05
COL = 256
LANE = 128
VMEM = pl.BlockSpec(memory_space=pltpu.VMEM)
SMEM = pl.BlockSpec(memory_space=pltpu.SMEM)
PARAMS = pltpu.CompilerParams(vmem_limit_bytes=48 * 1024 * 1024)


def row_orders(n_z, rows):
    group = -(-n_z * rows // 8) * 8
    grouped = np.full((4 * group, 1), -1, np.int32)
    natural = np.zeros((n_z * 4 * rows, 1), np.int32)
    for z in range(n_z):
        for y in range(2):
            for c in range(2):
                for r in range(rows):
                    o = ((z * 2 + y) * 2 + c) * rows + r
                    p = (c * 2 + y) * group + z * rows + r
                    grouped[p, 0] = o
                    natural[o, 0] = p
    return group, grouped, natural


def pick(index, width):
    lanes = lax.broadcasted_iota(jnp.int32, (index.shape[0], width), 1)
    return jnp.where(lanes == index, 1.0, 0.0).astype(jnp.bfloat16)


def dot(a, b, ca, cb):
    return lax.dot_general(a, b, (((ca,), (cb,)), ((), ())), preferred_element_type=jnp.float32)


def term_kernel(n_x, place, tokens, gain, cot, order, mine, theirs, cot_grouped, inv):
    feats = tokens.shape[1]
    half, group = order.shape[0] // 2, order.shape[0] // 4
    total = jnp.zeros((tokens.shape[0], COL), jnp.float32)
    for f in range(0, feats, COL):
        v = tokens[:, f : f + COL].astype(jnp.float32)
        total = total + v * v
    r = lax.rsqrt(jnp.sum(total, axis=1, keepdims=True) / feats + EPS)
    inv[...] = jnp.broadcast_to(r, inv.shape)
    for c in range(2):
        chosen = pick(order[c * half : (c + 1) * half, :], cot.shape[0])
        cot_grouped[c] = dot(chosen, cot[...], 1, 0).astype(jnp.bfloat16)
    for f in range(0, feats, COL):
        v = tokens[:, f : f + COL].astype(jnp.float32)
        hid = (v * r * gain[:, f : f + COL].astype(jnp.float32)).astype(jnp.bfloat16)
        y, x = divmod(f // COL, n_x)
        for out, c in ((theirs, 1 - place[0]), (mine, place[0])):
            part = dot(cot_grouped[c], hid, 1, 0)
            out[x, 2 * y] = part[:group].astype(jnp.bfloat16)
            out[x, 2 * y + 1] = part[group:].astype(jnp.bfloat16)


def main_kernel(tokens, gain, cot_grouped, inv, order, w, keys, grad, keys_acc, gh, dots):
    i = pl.program_id(0)
    toks, feats = tokens.shape
    n_x = w.shape[3]
    r = inv[:, :1]

    @pl.when(i == 0)
    def _():
        keys_acc[...] = jnp.zeros_like(keys_acc)
        dots[...] = jnp.zeros_like(dots)

    for x in range(n_x):
        at = pl.ds(pl.multiple_of((i * n_x + x) * COL, COL), COL)
        v = tokens[:, at].astype(jnp.float32)
        g = gain[:, at].astype(jnp.float32)
        hid = (v * r * g).astype(jnp.bfloat16)
        weight = jnp.concatenate([w[0, y, c, x] for c in range(2) for y in range(2)], axis=0)
        keys_acc[...] += dot(weight, hid, 1, 1)
        part = dot(cot_grouped[...], weight, 0, 0) * g
        gh[:, at] = part
        dots[...] += v * part

    @pl.when(i == pl.num_programs(0) - 1)
    def _():
        keys[...] = dot(pick(order[...], keys_acc.shape[0]), keys_acc[...].astype(jnp.bfloat16), 1, 0).astype(jnp.bfloat16)
        k = r * r * r * (jnp.sum(dots[...], axis=1, keepdims=True) / feats)
        for f in range(0, feats, COL):
            v = tokens[:, f : f + COL].astype(jnp.float32)
            grad[:, f : f + COL] = (r * gh[:, f : f + COL] - v * k).astype(jnp.bfloat16)


def per_device(tokens, gain, codes, scales, cotangent):
    n_y, n_x, n_z = (lax.axis_size(a) for a in ("y_hi", "x", "z"))
    rows, width = codes.shape
    toks, feats = tokens.shape
    outw = cotangent.shape[1]
    group, grouped, natural = row_orders(n_z, rows)
    place = lax.axis_index("core").astype(jnp.int32).reshape(1)
    gain_row = gain.reshape(1, feats)
    cot_t = cotangent.T

    with jax.named_scope("weight_far"):
        scale = jnp.repeat(scales.astype(jnp.float32), width // scales.shape[1], axis=1)
        own = (codes.astype(jnp.float32) * scale).astype(jnp.bfloat16)
        spread = jnp.broadcast_to(own[None], (n_x * n_z, rows, width))
        spread = lax.all_to_all(spread, ("x", "z"), split_axis=0, concat_axis=0, tiled=True)
        slab = jnp.pad(spread.reshape(n_x, n_z * rows, width), ((0, 0), (0, group - n_z * rows), (0, 0)))
    with jax.named_scope("weight_near"):
        w = lax.all_gather(slab, ("y_hi", "y_lo", "core"), axis=0, tiled=False).reshape(n_y, 2, 2, n_x, group, width)

    with jax.named_scope("term"):
        near = jax.ShapeDtypeStruct((n_x, 2 * n_y, group, width), jnp.bfloat16)
        mine, theirs, cot_grouped, inv = pl.pallas_call(
            lambda *refs: term_kernel(n_x, *refs),
            out_shape=(
                near,
                near,
                jax.ShapeDtypeStruct((2, 2 * group, toks), jnp.bfloat16),
                jax.ShapeDtypeStruct((toks, LANE), jnp.float32),
            ),
            in_specs=[SMEM] + [VMEM] * 4,
            out_specs=(VMEM,) * 4,
            compiler_params=PARAMS,
            cost_estimate=pl.CostEstimate(flops=3 * toks * outw * feats, bytes_accessed=4 * toks * feats, transcendentals=0),
        )(place, tokens, gain_row, cot_t, jnp.asarray(grouped))
        cot_grouped = cot_grouped.reshape(4 * group, toks)
    with jax.named_scope("reduce_core"):
        came = lax.ppermute(theirs, "core", ((0, 1), (1, 0)))
        came, _ = lax.optimization_barrier((came, slab))
        pair = (mine.astype(jnp.float32) + came.astype(jnp.float32)).astype(jnp.bfloat16)
    with jax.named_scope("reduce_x"):
        parts = lax.all_to_all(pair, "x", split_axis=0, concat_axis=0, tiled=True)
        part = jnp.sum(parts.astype(jnp.float32), axis=0).astype(jnp.bfloat16)
    with jax.named_scope("reduce_y"):
        parts = lax.all_to_all(part, ("y_hi", "y_lo"), split_axis=0, concat_axis=0, tiled=True)
        part = jnp.sum(parts.astype(jnp.float32), axis=0).astype(jnp.bfloat16)
    with jax.named_scope("reduce_z"):
        last = lax.all_to_all(part[: n_z * rows].reshape(n_z, rows, width), "z", split_axis=0, concat_axis=0, tiled=True)
        grad_weight = jnp.sum(last.astype(jnp.float32), axis=0) / (n_y * n_x * n_z * 4)

    with jax.named_scope("main"):
        whole = lambda *shape: pl.BlockSpec(shape, lambda i: (0,) * len(shape))
        keys_t, grad_tokens = pl.pallas_call(
            main_kernel,
            grid=(n_y,),
            out_shape=(
                jax.ShapeDtypeStruct((outw, toks), jnp.bfloat16),
                jax.ShapeDtypeStruct((toks, feats), jnp.bfloat16),
            ),
            in_specs=[
                whole(toks, feats),
                whole(1, feats),
                whole(4 * group, toks),
                whole(toks, LANE),
                whole(outw, 1),
                pl.BlockSpec((1, 2, 2, n_x, group, width), lambda i: (i, 0, 0, 0, 0, 0)),
            ],
            out_specs=(whole(outw, toks), whole(toks, feats)),
            scratch_shapes=[
                pltpu.VMEM((4 * group, toks), jnp.float32),
                pltpu.VMEM((toks, feats), jnp.float32),
                pltpu.VMEM((toks, COL), jnp.float32),
            ],
            compiler_params=PARAMS,
            cost_estimate=pl.CostEstimate(flops=5 * toks * outw * feats, bytes_accessed=10 * toks * feats, transcendentals=0),
        )(tokens, gain_row, cot_grouped, inv, jnp.asarray(natural), w)
    return keys_t.T, grad_tokens, grad_weight


def solution(mesh):
    n_intra, n_inter = mesh.devices.shape
    fine = Mesh(mesh.devices.reshape(4, n_intra // 4, n_inter // 4, 2, 2), ("y_hi", "x", "z", "y_lo", "core"))
    intra, inter = ("y_hi", "x"), ("z", "y_lo", "core")
    placed = (P(intra + inter, None), P(), P(inter, intra), P(inter, intra), P(intra + inter, None))
    return jax.shard_map(
        per_device,
        mesh=fine,
        in_specs=placed,
        out_specs=(P(intra + inter, None), P(intra + inter, None), P(inter, intra)),
        check_vma=False,
    )
```

time: 200 us -> 151 us (0.76)
  blocking collectives: 146 us -> 110 us
  local copies, waits for them, and re-layouts: 12 us -> 1.93 us
    all_to_all x2 -> x3, blocking collectives: 111 us -> 79.4 us  [the longest x1 38.9 us: per_device(): lax.all_to_all(spread, ('x', 'z'), split_axis=0, concat_axis=0, tiled=True)]
    all_to_all x1, blocking collectives: 35.1 us -> 30.6 us  [per_device(): parts = lax.all_to_all(pair, 'x', split_axis=0, concat_axis=0, tiled=True)]
    reshape x3 -> x2, local copies, waits for them, and re-layouts: 3.51 us -> 0.15 us  [the longest x1 0.11 us: per_device(): spread.reshape(n_x, n_z * rows, width)]
    squeeze x1 -> x0, local copies, waits for them, and re-layouts: 3.28 us -> none  [per_device(): theirs = lax.dynamic_index_in_dim(term, 1 - core, 0, keepdims=False)]
    convert_element_type x1, other arithmetic: 3.51 us -> 0.53 us  [per_device(): (mine.astype(jnp.float32) + came.astype(jnp.float32)).astype(jnp.bfloat16)]
    reduce_sum x1 -> x2, other arithmetic: 2.09 us -> 4.07 us  [per_device(): part = jnp.sum(parts.astype(jnp.float32), axis=0).astype(jnp.bfloat16)]
  transfers between devices with their start and end apart: 2 -> 2, of which waited for: 1 -> 1; matrix products, arithmetic and copies ran while one was open for 6% -> 4% of each run, Pallas kernels for 2% -> 2%
where the time goes in v3:
time: 151 us; the launch traced here: 150 us
  blocking collectives  110 us (73%)
  between operations  14.2 us (9%)
  Pallas kernels  11.6 us (8%)
  other arithmetic  5.94 us (4%)
  waiting for transfers between devices  4.54 us (3%)
  starting transfers between devices  1.95 us (1%)
  local copies, waits for them, and re-layouts  1.93 us (1%)
    all_to_all x1, blocking collectives, per_device(): lax.all_to_all(spread, ('x', 'z'), split_axis=0, concat_axis=0, tiled=True)  38.9 us
    all_to_all x1, blocking collectives, per_device(): parts = lax.all_to_all(pair, 'x', split_axis=0, concat_axis=0, tiled=True)  30.6 us
    all_to_all x1, blocking collectives, per_device(): lax.all_to_all(part, ('y_hi', 'y_lo'), split_axis=0, concat_axis=0, tiled...  24.3 us
    all_to_all x1, blocking collectives, per_device(): lax.all_to_all(part[:n_z * rows].reshape(n_z, rows, width), 'z', split_ax...  16.2 us
    pallas_call x1, Pallas kernels, per_device(): pl.pallas_call(main_kernel, grid=(n_y,), out_shape=(jax.ShapeDtypeStruct(...  8.08 us
    ppermute x1, waiting for transfers between devices, per_device(): came = lax.ppermute(theirs, 'core', ((0, 1), (1, 0)))  4.52 us
    reduce_sum x2, other arithmetic, per_device(): part = jnp.sum(parts.astype(jnp.float32), axis=0).astype(jnp.bfloat16)  4.07 us
    pallas_call x1, Pallas kernels, per_device(): pl.pallas_call(lambda *refs: term_kernel(n_x, *refs), out_shape=(near, ne...  3.52 us
  transfers between devices with their start and end apart: 2, of which 1 were waited for; matrix products, arithmetic and copies ran while one was open for 4% of the time, Pallas kernels for 2%

profile of v3, /device:TPU:6, one launch (start us, length us, event | category | flops | bytes accessed | tf_op | source)
XLA Modules:
  0.0 150.1 jit_solution(7461244205422670799)
XLA Ops:
  7.2 0.0 copy-start.2
  7.2 0.0 copy-start.4
  7.2 0.0 copy-start
  7.2 0.0 copy-start.1
  7.2 0.0 all-gather.3.cloned.1.call-start
  7.3 0.9 copy.13
  8.2 0.1 broadcast_in_dim.4
  8.3 0.7 multiply_convert_fusion
  9.0 38.9 %all_to_all.20 = bf16[48,11,256]{2,1,0:T(8,128)(2,1)S(1)} all-to-all(bf16[48,11,256]{2,1,0:T(8,128)(2,1)S(1)} %broadcast_in_dim.10), channel_id=1, replica_groups=mesh['y_hi'=4,'x'=4,'z'=12,'y_lo'=2,'core'=2] {'x','z'}, dimensions={0} | all-to-all | bytes 540672 | tf_op jit(solution)/shard_map/weight_far/all_to_all | solution.py:108
  47.9 0.1 reshape.32
  48.0 0.7 pad.4
  48.8 0.0 all-gather.3.cloned.1.call-update
  48.8 0.0 copy-done.4
  48.8 0.0 copy-done.2
  48.9 0.0 copy-done
  48.9 0.0 copy-done.1
  48.9 3.5 %term.1 = (bf16[4,8,136,256]{3,2,1,0:T(8,128)(2,1)S(1)}, bf16[4,8,136,256]{3,2,1,0:T(8,128)(2,1)}, bf16[2,272,256]{2,1,0:T(8,128)(2,1)S(1)}, f32[256,128]{1,0:T(8,128)S(1)}) custom-call(s32[1]{0:T(128)} %bitcast.refs_0_, bf16[256,4096]{1,0:T(8,128)(2,1)S(1)} %copy-done, bf16[1,4096]{1,0:T(2,128)(2,1)S(1)} %reshape.28.refs_2_.gain, ...), custom_call_target="tpu_custom_call" | custom-call | flops 1660944384 | bytes 4194304 | tf_op jit(solution)/shard_map/term/pallas_call | solution.py:115
  52.4 1.9 %collective-permute-start = (bf16[4,8,136,256]{3,2,1,0:T(8,128)(2,1)}, bf16[4,8,136,256]{3,2,1,0:T(8,128)(2,1)S(1)}, u32[]{:S(2)}, u32[]{:S(2)}) collective-permute-start(bf16[4,8,136,256]{3,2,1,0:T(8,128)(2,1)} %get-tuple-element.15), channel_id=1, source_target_pairs={{0,1},{1,0},{2,3},{3,2},{4,5},{5,4},{6,7},{7,6},{8,9},{9,8},{10,11... | collective-permute-start | bytes 6684680 | tf_op jit(solution)/shard_map/reduce_core/ppermute | solution.py:130
  54.3 4.5 %collective-permute-done = bf16[4,8,136,256]{3,2,1,0:T(8,128)(2,1)S(1)} collective-permute-done((bf16[4,8,136,256]{3,2,1,0:T(8,128)(2,1)}, bf16[4,8,136,256]{3,2,1,0:T(8,128)(2,1)S(1)}, u32[]{:S(2)}, u32[]{:S(2)}) %collective-permute-start) | collective-permute-done | bytes 2228256 | tf_op jit(solution)/shard_map/reduce_core/ppermute | solution.py:130
  58.8 0.5 add_convert_fusion
  59.4 30.6 %all_to_all.21 = bf16[4,8,136,256]{3,2,1,0:T(8,128)(2,1)} all-to-all(bf16[4,8,136,256]{3,2,1,0:T(8,128)(2,1)S(1)} %add_convert_fusion), channel_id=1, replica_groups=mesh['y_hi'=4,'x'=4,'z'=12,'y_lo'=2,'core'=2] {'x'}, dimensions={0} | all-to-all | bytes 4456448 | tf_op jit(solution)/shard_map/reduce_x/all_to_all | solution.py:134
  90.0 0.0 copy-start.3
  90.0 2.9 %reduce_sum.33 = bf16[8,136,256]{2,1,0:T(8,128)(2,1)} reduce(bf16[4,8,136,256]{3,2,1,0:T(8,128)(2,1)} %all_to_all.21, bf16[]{:T(256)} %constant.15.clone.1), dimensions={0}, to_apply=%region_0.1 | reduce | flops 835584 | bytes 2785282 | tf_op jit(solution)/shard_map/reduce_x/reduce_sum | solution.py:135
  92.9 24.3 %all_to_all.22 = bf16[8,136,256]{2,1,0:T(8,128)(2,1)} all-to-all(bf16[8,136,256]{2,1,0:T(8,128)(2,1)} %reduce_sum.33), channel_id=1, replica_groups=mesh['y_hi'=4,'x'=4,'z'=12,'y_lo'=2,'core'=2] {'y_hi','y_lo'}, dimensions={0} | all-to-all | bytes 1114112 | tf_op jit(solution)/shard_map/reduce_y/all_to_all | solution.py:137
  117.2 1.1 reduce_sum.34
  118.3 16.2 %all_to_all.23 = bf16[12,11,256]{2,1,0:T(8,128)(2,1)S(1)} all-to-all(bf16[12,11,256]{2,1,0:T(8,128)(2,1)S(1)} %reshape.34), channel_id=1, replica_groups=mesh['y_hi'=4,'x'=4,'z'=12,'y_lo'=2,'core'=2] {'z'}, dimensions={0} | all-to-all | bytes 135168 | tf_op jit(solution)/shard_map/reduce_z/all_to_all | solution.py:140
  134.5 0.6 broadcast_multiply_fusion
  135.1 0.0 all-gather.3.cloned.1.call-done
  135.1 0.0 copy-done.3
  135.1 8.1 %main.1 = (bf16[528,256]{1,0:T(8,128)(2,1)}, bf16[256,4096]{1,0:T(8,128)(2,1)}) custom-call(bf16[256,4096]{1,0:T(8,128)(2,1)S(1)} %copy-done, bf16[1,4096]{1,0:T(2,128)(2,1)S(1)} %reshape.28.refs_2_.gain, bf16[544,256]{1,0:T(8,128)(2,1)S(1)} %bitcast.10, f32[256,128]{1,0:T(8,128)S(1)} %get-tuple-element.11.inv, s32[528,1]{1,0:T(8,128)S(1)} %copy-done.3, ...), custom_call_target="tpu_custom_call" | custom-call | flops 2768240640 | bytes 10485760 | tf_op jit(solution)/shard_map/main/pallas_call | solution.py:145
  (6 shorter events, 0.1 us)
Async XLA Ops:
  7.2 41.7 %copy-start.2 = (s32[544,1]{1,0:T(8,128)S(1)}, s32[544,1]{1,0:T(8,128)}, u32[]{:S(2)}) copy-start(s32[544,1]{1,0:T(8,128)} %constant.18.clone.refs_4_) | copy-start | bytes 6532
  7.2 41.6 %copy-start.4 = (bf16[4096]{0:T(1024)(128)(2,1)S(1)}, bf16[4096]{0:T(1024)(128)(2,1)}, u32[]{:S(2)}) copy-start(bf16[4096]{0:T(1024)(128)(2,1)} %param.8) | copy-start | bytes 24580
  7.2 41.7 %copy-start = (bf16[256,4096]{1,0:T(8,128)(2,1)S(1)}, bf16[256,4096]{1,0:T(8,128)(2,1)}, u32[]{:S(2)}) copy-start(bf16[256,4096]{1,0:T(8,128)(2,1)} %tokens.1) | copy-start | bytes 6291460
  7.2 41.7 %copy-start.1 = (bf16[256,528]{0,1:T(8,128)(2,1)S(1)}, bf16[256,528]{0,1:T(8,128)(2,1)}, u32[]{:S(2)}) copy-start(bf16[256,528]{0,1:T(8,128)(2,1)} %param.11) | copy-start | bytes 811012
  7.2 127.9 %all-gather.3.cloned.1.call-start = ((), (), s32[]{:S(2)}) async-start(), calls=%async_computation.4 | async-start | bytes 4734976 | tf_op jit(solution)/shard_map/weight_near/all_gather | solution.py:111
  52.4 6.4 %collective-permute-start = (bf16[4,8,136,256]{3,2,1,0:T(8,128)(2,1)}, bf16[4,8,136,256]{3,2,1,0:T(8,128)(2,1)S(1)}, u32[]{:S(2)}, u32[]{:S(2)}) collective-permute-start(bf16[4,8,136,256]{3,2,1,0:T(8,128)(2,1)} %get-tuple-element.15), channel_id=1, source_target_pairs={{0,1},{1,0},{2,3},{3,2},{4,5},{5,4},{6,7},{7,6},{8,9},{9,8},{10,11... | collective-permute-start | bytes 6684680 | tf_op jit(solution)/shard_map/reduce_core/ppermute | solution.py:130
  90.0 45.2 %copy-start.3 = (s32[528,1]{1,0:T(8,128)S(1)}, s32[528,1]{1,0:T(8,128)}, u32[]{:S(2)}) copy-start(s32[528,1]{1,0:T(8,128)} %constant.19.clone.order) | copy-start | bytes 6340
Sparse Core Ops, SparseCore 0:
  48.9 42.1 all-gather.2

commit v4 on v3

--- a/solution.py
+++ b/solution.py
@@ -60,7 +60,15 @@
             out[x, 2 * y + 1] = part[group:].astype(jnp.bfloat16)
 
 
-def main_kernel(tokens, gain, cot_grouped, inv, order, w, keys, grad, keys_acc, gh, dots):
+def prep_kernel(tokens, gain, cot_grouped, inv, hid, cot):
+    r = inv[:, :1]
+    for f in range(0, tokens.shape[1], COL):
+        v = tokens[:, f : f + COL].astype(jnp.float32)
+        hid[:, f : f + COL] = (v * r * gain[:, f : f + COL].astype(jnp.float32)).astype(jnp.bfloat16)
+    cot[...] = cot_grouped[...].T
+
+
+def main_kernel(tokens, gain, hid, cot, inv, back, w, keys, grad, keys_acc, gh, dots):
     i = pl.program_id(0)
     toks, feats = tokens.shape
     n_x = w.shape[3]
@@ -74,21 +82,30 @@
     for x in range(n_x):
         at = pl.ds(pl.multiple_of((i * n_x + x) * COL, COL), COL)
         v = tokens[:, at].astype(jnp.float32)
-        g = gain[:, at].astype(jnp.float32)
-        hid = (v * r * g).astype(jnp.bfloat16)
         weight = jnp.concatenate([w[0, y, c, x] for c in range(2) for y in range(2)], axis=0)
-        keys_acc[...] += dot(weight, hid, 1, 1)
-        part = dot(cot_grouped[...], weight, 0, 0) * g
+        keys_acc[...] += dot(weight, hid[:, at], 1, 1)
+        part = dot(cot[...], weight, 1, 0) * gain[:, at].astype(jnp.float32)
         gh[:, at] = part
         dots[...] += v * part
 
     @pl.when(i == pl.num_programs(0) - 1)
     def _():
-        keys[...] = dot(pick(order[...], keys_acc.shape[0]), keys_acc[...].astype(jnp.bfloat16), 1, 0).astype(jnp.bfloat16)
+        keys[...] = dot(back[...], keys_acc[...].astype(jnp.bfloat16), 1, 0).astype(jnp.bfloat16)
         k = r * r * r * (jnp.sum(dots[...], axis=1, keepdims=True) / feats)
         for f in range(0, feats, COL):
             v = tokens[:, f : f + COL].astype(jnp.float32)
             grad[:, f : f + COL] = (r * gh[:, f : f + COL] - v * k).astype(jnp.bfloat16)
+
+
+def add(values):
+    total = values[0].astype(jnp.float32)
+    for i in range(1, values.shape[0]):
+        total = total + values[i].astype(jnp.float32)
+    return total
+
+
+def together(*values):
+    return lax.optimization_barrier(values)
 
 
 def per_device(tokens, gain, codes, scales, cotangent):
@@ -105,11 +122,8 @@
         scale = jnp.repeat(scales.astype(jnp.float32), width // scales.shape[1], axis=1)
         own = (codes.astype(jnp.float32) * scale).astype(jnp.bfloat16)
         spread = jnp.broadcast_to(own[None], (n_x * n_z, rows, width))
+        spread, tokens_after = together(spread, tokens)
         spread = lax.all_to_all(spread, ("x", "z"), split_axis=0, concat_axis=0, tiled=True)
-        slab = jnp.pad(spread.reshape(n_x, n_z * rows, width), ((0, 0), (0, group - n_z * rows), (0, 0)))
-    with jax.named_scope("weight_near"):
-        w = lax.all_gather(slab, ("y_hi", "y_lo", "core"), axis=0, tiled=False).reshape(n_y, 2, 2, n_x, group, width)
-
     with jax.named_scope("term"):
         near = jax.ShapeDtypeStruct((n_x, 2 * n_y, group, width), jnp.bfloat16)
         mine, theirs, cot_grouped, inv = pl.pallas_call(
@@ -124,22 +138,41 @@
             out_specs=(VMEM,) * 4,
             compiler_params=PARAMS,
             cost_estimate=pl.CostEstimate(flops=3 * toks * outw * feats, bytes_accessed=4 * toks * feats, transcendentals=0),
-        )(place, tokens, gain_row, cot_t, jnp.asarray(grouped))
+        )(place, tokens_after, gain_row, cot_t, jnp.asarray(grouped))
         cot_grouped = cot_grouped.reshape(4 * group, toks)
+    with jax.named_scope("weight_near"):
+        came = lax.ppermute(theirs, "core", ((0, 1), (1, 0)))
+        spread, came = together(spread, came)
+        slab = jnp.pad(spread.reshape(n_x, n_z * rows, width), ((0, 0), (0, group - n_z * rows), (0, 0)))
+        w = lax.all_gather(slab, ("y_hi", "y_lo", "core"), axis=0, tiled=False).reshape(n_y, 2, 2, n_x, group, width)
     with jax.named_scope("reduce_core"):
-        came = lax.ppermute(theirs, "core", ((0, 1), (1, 0)))
-        came, _ = lax.optimization_barrier((came, slab))
+        came, _ = together(came, slab)
         pair = (mine.astype(jnp.float32) + came.astype(jnp.float32)).astype(jnp.bfloat16)
     with jax.named_scope("reduce_x"):
+        pair, inv = together(pair, inv)
         parts = lax.all_to_all(pair, "x", split_axis=0, concat_axis=0, tiled=True)
-        part = jnp.sum(parts.astype(jnp.float32), axis=0).astype(jnp.bfloat16)
+        hid, cot = pl.pallas_call(
+            prep_kernel,
+            out_shape=(
+                jax.ShapeDtypeStruct((toks, feats), jnp.bfloat16),
+                jax.ShapeDtypeStruct((toks, 4 * group), jnp.bfloat16),
+            ),
+            in_specs=[VMEM] * 4,
+            out_specs=(VMEM,) * 2,
+            compiler_params=PARAMS,
+            cost_estimate=pl.CostEstimate(flops=4 * toks * feats, bytes_accessed=4 * toks * feats, transcendentals=0),
+        )(tokens, gain_row, cot_grouped, inv)
+        parts, hid = together(parts, hid)
+        part = add(parts).astype(jnp.bfloat16)
     with jax.named_scope("reduce_y"):
+        part, order = together(part, jnp.asarray(natural))
         parts = lax.all_to_all(part, ("y_hi", "y_lo"), split_axis=0, concat_axis=0, tiled=True)
-        part = jnp.sum(parts.astype(jnp.float32), axis=0).astype(jnp.bfloat16)
+        back = pick(order, 4 * group)
+        parts, back = together(parts, back)
+        part = add(parts).astype(jnp.bfloat16)[: n_z * rows].reshape(n_z, rows, width)
     with jax.named_scope("reduce_z"):
-        last = lax.all_to_all(part[: n_z * rows].reshape(n_z, rows, width), "z", split_axis=0, concat_axis=0, tiled=True)
-        grad_weight = jnp.sum(last.astype(jnp.float32), axis=0) / (n_y * n_x * n_z * 4)
-
+        part, back = together(part, back)
+        last = lax.all_to_all(part, "z", split_axis=0, concat_axis=0, tiled=True)
     with jax.named_scope("main"):
         whole = lambda *shape: pl.BlockSpec(shape, lambda i: (0,) * len(shape))
         keys_t, grad_tokens = pl.pallas_call(
@@ -152,9 +185,10 @@
             in_specs=[
                 whole(toks, feats),
                 whole(1, feats),
-                whole(4 * group, toks),
+                whole(toks, feats),
+                whole(toks, 4 * group),
                 whole(toks, LANE),
-                whole(outw, 1),
+                whole(outw, 4 * group),
                 pl.BlockSpec((1, 2, 2, n_x, group, width), lambda i: (i, 0, 0, 0, 0, 0)),
             ],
             out_specs=(whole(outw, toks), whole(toks, feats)),
@@ -165,7 +199,10 @@
             ],
             compiler_params=PARAMS,
             cost_estimate=pl.CostEstimate(flops=5 * toks * outw * feats, bytes_accessed=10 * toks * feats, transcendentals=0),
-        )(tokens, gain_row, cot_grouped, inv, jnp.asarray(natural), w)
+        )(tokens, gain_row, hid, cot, inv, back, w)
+    with jax.named_scope("finish"):
+        last, keys_t = together(last, keys_t)
+        grad_weight = jnp.sum(last.astype(jnp.float32), axis=0) / (n_y * n_x * n_z * 4)
     return keys_t.T, grad_tokens, grad_weight
 
 

time: 151 us -> 150 us (level)
  blocking collectives: 110 us -> 39.7 us
  waiting for transfers between devices: 4.54 us -> 39.1 us
  starting transfers between devices: 1.95 us -> 23.3 us
  local copies, waits for them, and re-layouts: 1.93 us -> 10.5 us
  other arithmetic: 5.94 us -> 9.88 us
    all_to_all x3 -> x0, blocking collectives: 71 us -> none  [the longest x1 30.6 us: per_device(): parts = lax.all_to_all(pair, 'x', split_axis=0, concat_axis=0, tiled=True)]
    all_to_all x0 -> x3, waiting for transfers between devices: none -> 39.1 us  [the longest x1 22.1 us: per_device(): parts = lax.all_to_all(pair, 'x', split_axis=0, concat_axis=0, tiled=True)]
    all_to_all x0 -> x3, starting transfers between devices: none -> 21.4 us  [the longest x1 9.26 us: per_device(): last = lax.all_to_all(part, 'z', split_axis=0, concat_axis=0, tiled=True)]
    unnamed x12 -> x16, local copies, waits for them, and re-layouts: 0.03 us -> 6.41 us
    ppermute x1, waiting for transfers between devices: 4.52 us -> 0.01 us  [per_device(): came = lax.ppermute(theirs, 'core', ((0, 1), (1, 0)))]
    reduce_sum x2 -> x0, other arithmetic: 4.07 us -> none  [per_device(): part = jnp.sum(parts.astype(jnp.float32), axis=0).astype(jnp.bfloat16)]
    add x0 -> x2, other arithmetic: none -> 3.65 us  [add(): total = total + values[i].astype(jnp.float32)]
    convert_element_type x1, other arithmetic: 0.53 us -> 3.58 us  [per_device(): (mine.astype(jnp.float32) + came.astype(jnp.float32)).astype(jnp.bfloat16)]
  transfers between devices with their start and end apart: 2 -> 5, of which waited for: 1 -> 3; matrix products, arithmetic and copies ran while one was open for 4% -> 6% of each run, Pallas kernels for 2% -> 6%
where the time goes in v4:
time: 150 us; the launch traced here: 148 us
  blocking collectives  39.7 us (26%)
  waiting for transfers between devices  39.1 us (26%)
  starting transfers between devices  23.3 us (16%)
  between operations  14.2 us (9%)
  Pallas kernels  11.7 us (8%)
  local copies, waits for them, and re-layouts  10.5 us (7%)
  other arithmetic  9.88 us (7%)
    all_to_all x1, blocking collectives, per_device(): lax.all_to_all(spread, ('x', 'z'), split_axis=0, concat_axis=0, tiled=True)  39.7 us
    all_to_all x1, waiting for transfers between devices, per_device(): parts = lax.all_to_all(pair, 'x', split_axis=0, concat_axis=0, tiled=True)  22.1 us
    all_to_all x1, waiting for transfers between devices, per_device(): lax.all_to_all(part, ('y_hi', 'y_lo'), split_axis=0, concat_axis=0, tiled...  15.1 us
    all_to_all x1, starting transfers between devices, per_device(): last = lax.all_to_all(part, 'z', split_axis=0, concat_axis=0, tiled=True)  9.26 us
    pallas_call x1, Pallas kernels, per_device(): pl.pallas_call(main_kernel, grid=(n_y,), out_shape=(jax.ShapeDtypeStruct(...  7.73 us
    all_to_all x1, starting transfers between devices, per_device(): lax.all_to_all(part, ('y_hi', 'y_lo'), split_axis=0, concat_axis=0, tiled...  7.11 us
    unnamed x16, local copies, waits for them, and re-layouts  6.41 us
    all_to_all x1, starting transfers between devices, per_device(): parts = lax.all_to_all(pair, 'x', split_axis=0, concat_axis=0, tiled=True)  4.99 us
  transfers between devices with their start and end apart: 5, of which 3 were waited for; matrix products, arithmetic and copies ran while one was open for 6% of the time, Pallas kernels for 6%

profile of v4, /device:TPU:6, one launch (start us, length us, event | category | flops | bytes accessed | tf_op | source)
XLA Modules:
  0.0 148.4 jit_solution(4815879192980923122)
XLA Ops:
  7.2 0.0 all-gather.3.cloned.1.call-start
  7.2 0.8 copy.12
  8.0 0.1 broadcast_in_dim.17
  8.1 0.7 multiply_convert_fusion
  8.8 0.7 reshape.53.refs_2_.gain
  9.5 0.0 copy-start
  9.5 1.6 %copy-done = bf16[256,4096]{1,0:T(8,128)(2,1)S(1)} copy-done((bf16[256,4096]{1,0:T(8,128)(2,1)S(1)}, bf16[256,4096]{1,0:T(8,128)(2,1)}, u32[]{:S(2)}) %copy-start) | copy-done | bytes 2097176
  11.1 0.0 copy-start.4
  11.1 1.0 copy-done.4
  12.1 0.0 copy-start.5
  12.1 1.0 copy-done.5
  13.0 3.5 %term.1 = (bf16[4,8,136,256]{3,2,1,0:T(8,128)(2,1)S(1)}, bf16[4,8,136,256]{3,2,1,0:T(8,128)(2,1)}, bf16[2,272,256]{2,1,0:T(8,128)(2,1)S(1)}, f32[256,128]{1,0:T(8,128)S(1)}) custom-call(s32[1]{0:T(128)} %bitcast.refs_0_, bf16[256,4096]{1,0:T(8,128)(2,1)S(1)} %copy-done, bf16[1,4096]{1,0:T(2,128)(2,1)S(1)} %reshape.53.refs_2_.gain, ...), custom_call_target="tpu_custom_call" | custom-call | flops 1660944384 | bytes 4194304 | tf_op jit(solution)/shard_map/term/pallas_call | solution.py:129
  16.5 1.9 %collective-permute-start = (bf16[4,8,136,256]{3,2,1,0:T(8,128)(2,1)}, bf16[4,8,136,256]{3,2,1,0:T(8,128)(2,1)}, u32[]{:S(2)}, u32[]{:S(2)}) collective-permute-start(bf16[4,8,136,256]{3,2,1,0:T(8,128)(2,1)} %get-tuple-element.31), channel_id=1, source_target_pairs={{0,1},{1,0},{2,3},{3,2},{4,5},{5,4},{6,7},{7,6},{8,9},{9,8},{10,11... | collective-permute-start | bytes 6684680 | tf_op jit(solution)/shard_map/weight_near/ppermute | solution.py:144
  18.4 39.7 %all_to_all.20 = bf16[48,11,256]{2,1,0:T(8,128)(2,1)} all-to-all(bf16[48,11,256]{2,1,0:T(8,128)(2,1)S(1)} %broadcast_in_dim.18), channel_id=1, replica_groups=mesh['y_hi'=4,'x'=4,'z'=12,'y_lo'=2,'core'=2] {'x','z'}, dimensions={0} | all-to-all | bytes 540672 | tf_op jit(solution)/shard_map/weight_far/all_to_all | solution.py:126
  58.1 0.0 collective-permute-done
  58.1 1.1 reshape.54
  59.2 0.7 pad.4
  60.0 0.0 all-gather.3.cloned.1.call-update
  60.0 3.6 %add_convert_fusion = bf16[4,8,136,256]{3,2,1,0:T(8,128)(2,1)} fusion(bf16[4,8,136,256]{3,2,1,0:T(8,128)(2,1)} %collective-permute-done, bf16[4,8,136,256]{3,2,1,0:T(8,128)(2,1)S(1)} %get-tuple-element.29), kind=kLoop, calls=%fused_computation | loop fusion | flops 4456448 | bytes 6684672 | tf_op jit(solution)/shard_map/reduce_core/convert_element_type | solution.py:150
  63.6 0.0 copy-start.1
  63.6 5.0 %all-to-all-start.1 = ((bf16[4,8,136,256]{3,2,1,0:T(8,128)(2,1)}), bf16[4,8,136,256]{3,2,1,0:T(8,128)(2,1)}, u32[]{:S(2)}, u32[]{:S(2)}) async-start(bf16[4,8,136,256]{3,2,1,0:T(8,128)(2,1)} %add_convert_fusion), calls=%async_computation.1 | async-start | bytes 4456448 | tf_op jit(solution)/shard_map/reduce_x/all_to_all | solution.py:153
  68.6 0.0 copy-done.1
  68.6 0.6 reduce_x.1
  69.1 0.0 copy-start.2
  69.1 1.3 copy-done.2
  70.5 0.0 copy-start.6
  70.5 22.1 %all-to-all-done.1 = bf16[4,8,136,256]{3,2,1,0:T(8,128)(2,1)} async-done(((bf16[4,8,136,256]{3,2,1,0:T(8,128)(2,1)}), bf16[4,8,136,256]{3,2,1,0:T(8,128)(2,1)}, u32[]{:S(2)}, u32[]{:S(2)}) %all-to-all-start.1) | async-done | bytes 2228256 | tf_op jit(solution)/shard_map/reduce_x/all_to_all | solution.py:153
  92.5 2.7 %fusion = bf16[8,136,256]{2,1,0:T(8,128)(2,1)} fusion(bf16[4,8,136,256]{3,2,1,0:T(8,128)(2,1)} %all-to-all-done.1), kind=kLoop, calls=%fused_computation.4 | loop fusion | flops 2228224 | bytes 2785280 | tf_op jit(solution)/shard_map/reduce_x/add | solution.py:103
  95.2 7.1 %all-to-all-start.2 = ((bf16[8,136,256]{2,1,0:T(8,128)(2,1)}), bf16[8,136,256]{2,1,0:T(8,128)(2,1)}, u32[]{:S(2)}, u32[]{:S(2)}) async-start(bf16[8,136,256]{2,1,0:T(8,128)(2,1)} %fusion), calls=%async_computation.2 | async-start | bytes 1114112 | tf_op jit(solution)/shard_map/reduce_y/all_to_all | solution.py:169
  102.3 0.0 copy-done.6
  102.3 0.2 select_convert_fusion.back
  102.5 15.1 %all-to-all-done.2 = bf16[8,136,256]{2,1,0:T(8,128)(2,1)} async-done(((bf16[8,136,256]{2,1,0:T(8,128)(2,1)}), bf16[8,136,256]{2,1,0:T(8,128)(2,1)}, u32[]{:S(2)}, u32[]{:S(2)}) %all-to-all-start.2) | async-done | bytes 557088 | tf_op jit(solution)/shard_map/reduce_y/all_to_all | solution.py:169
  117.6 1.0 convert_add_fusion
  118.6 1.0 fusion.6
  119.7 0.1 fusion.5
  119.7 0.7 reshape.56
  120.4 9.3 %all-to-all-start.3 = ((bf16[12,11,256]{2,1,0:T(8,128)(2,1)}), bf16[12,11,256]{2,1,0:T(8,128)(2,1)S(1)}, u32[]{:S(2)}, u32[]{:S(2)}) async-start(bf16[12,11,256]{2,1,0:T(8,128)(2,1)} %reshape.56), calls=%async_computation.3 | async-start | bytes 196608 | tf_op jit(solution)/shard_map/reduce_z/all_to_all | solution.py:175
  129.7 0.0 all-gather.3.cloned.1.call-done
  129.7 0.0 copy-start.3
  129.7 1.6 %copy-done.3 = bf16[256,4096]{1,0:T(8,128)(2,1)S(1)} copy-done((bf16[256,4096]{1,0:T(8,128)(2,1)S(1)}, bf16[256,4096]{1,0:T(8,128)(2,1)}, u32[]{:S(2)}) %copy-start.3) | copy-done | bytes 2097176
  131.3 7.7 %main.1 = (bf16[528,256]{1,0:T(8,128)(2,1)}, bf16[256,4096]{1,0:T(8,128)(2,1)}) custom-call(bf16[256,4096]{1,0:T(8,128)(2,1)S(1)} %copy-done.1, bf16[1,4096]{1,0:T(2,128)(2,1)S(1)} %reshape.53.refs_2_.gain, bf16[256,4096]{1,0:T(8,128)(2,1)S(1)} %copy-done.3, bf16[256,544]{1,0:T(8,128)(2,1)S(1)} %get-tuple-element.47.cot, ...), custom_call_target="tpu_custom_call" | custom-call | flops 2768240640 | bytes 10485760 | tf_op jit(solution)/shard_map/main/pallas_call | solution.py:178
  139.0 1.9 %all-to-all-done.3 = bf16[12,11,256]{2,1,0:T(8,128)(2,1)S(1)} async-done(((bf16[12,11,256]{2,1,0:T(8,128)(2,1)}), bf16[12,11,256]{2,1,0:T(8,128)(2,1)S(1)}, u32[]{:S(2)}, u32[]{:S(2)}) %all-to-all-start.3) | async-done | bytes 67616 | tf_op jit(solution)/shard_map/reduce_z/all_to_all | solution.py:175
  140.9 0.6 broadcast_multiply_fusion
  (5 shorter events, 0.1 us)
Async XLA Ops:
  7.2 122.5 %all-gather.3.cloned.1.call-start = ((), (), s32[]{:S(2)}) async-start(), calls=%async_computation.4 | async-start | bytes 4734976 | tf_op jit(solution)/shard_map/weight_near/all_gather | solution.py:147
  9.5 1.6 %copy-start = (bf16[256,4096]{1,0:T(8,128)(2,1)S(1)}, bf16[256,4096]{1,0:T(8,128)(2,1)}, u32[]{:S(2)}) copy-start(bf16[256,4096]{1,0:T(8,128)(2,1)} %tokens.3) | copy-start | bytes 6291460
  11.1 1.0 copy-start.4
  12.1 1.0 copy-start.5
  16.5 41.6 %collective-permute-start = (bf16[4,8,136,256]{3,2,1,0:T(8,128)(2,1)}, bf16[4,8,136,256]{3,2,1,0:T(8,128)(2,1)}, u32[]{:S(2)}, u32[]{:S(2)}) collective-permute-start(bf16[4,8,136,256]{3,2,1,0:T(8,128)(2,1)} %get-tuple-element.31), channel_id=1, source_target_pairs={{0,1},{1,0},{2,3},{3,2},{4,5},{5,4},{6,7},{7,6},{8,9},{9,8},{10,11... | collective-permute-start | bytes 6684680 | tf_op jit(solution)/shard_map/weight_near/ppermute | solution.py:144
  63.6 5.0 %copy-start.1 = (bf16[256,4096]{1,0:T(8,128)(2,1)S(1)}, bf16[256,4096]{1,0:T(8,128)(2,1)}, u32[]{:S(2)}) copy-start(bf16[256,4096]{1,0:T(8,128)(2,1)} %tokens.3) | copy-start | bytes 6291460
  63.6 28.9 %all-to-all-start.1 = ((bf16[4,8,136,256]{3,2,1,0:T(8,128)(2,1)}), bf16[4,8,136,256]{3,2,1,0:T(8,128)(2,1)}, u32[]{:S(2)}, u32[]{:S(2)}) async-start(bf16[4,8,136,256]{3,2,1,0:T(8,128)(2,1)} %add_convert_fusion), calls=%async_computation.1 | async-start | bytes 4456448 | tf_op jit(solution)/shard_map/reduce_x/all_to_all | solution.py:153
  69.1 1.3 copy-start.2
  70.5 31.8 %copy-start.6 = (s32[528,1]{0,1:T(1,128)S(1)}, s32[528,1]{0,1:T(1,128)}, u32[]{:S(2)}) copy-start(s32[528,1]{0,1:T(1,128)} %constant.19.clone) | copy-start | bytes 6340
  95.2 22.4 %all-to-all-start.2 = ((bf16[8,136,256]{2,1,0:T(8,128)(2,1)}), bf16[8,136,256]{2,1,0:T(8,128)(2,1)}, u32[]{:S(2)}, u32[]{:S(2)}) async-start(bf16[8,136,256]{2,1,0:T(8,128)(2,1)} %fusion), calls=%async_computation.2 | async-start | bytes 1114112 | tf_op jit(solution)/shard_map/reduce_y/all_to_all | solution.py:169
  120.4 20.5 %all-to-all-start.3 = ((bf16[12,11,256]{2,1,0:T(8,128)(2,1)}), bf16[12,11,256]{2,1,0:T(8,128)(2,1)S(1)}, u32[]{:S(2)}, u32[]{:S(2)}) async-start(bf16[12,11,256]{2,1,0:T(8,128)(2,1)} %reshape.56), calls=%async_computation.3 | async-start | bytes 196608 | tf_op jit(solution)/shard_map/reduce_z/all_to_all | solution.py:175
  129.7 1.6 %copy-start.3 = (bf16[256,4096]{1,0:T(8,128)(2,1)S(1)}, bf16[256,4096]{1,0:T(8,128)(2,1)}, u32[]{:S(2)}) copy-start(bf16[256,4096]{1,0:T(8,128)(2,1)} %copy-done.2) | copy-start | bytes 6291460
Sparse Core Ops, SparseCore 0:
  60.1 42.1 all-gather.2

commit v5 on v4

--- a/solution.py
+++ b/solution.py
@@ -11,7 +11,10 @@
 LANE = 128
 VMEM = pl.BlockSpec(memory_space=pltpu.VMEM)
 SMEM = pl.BlockSpec(memory_space=pltpu.SMEM)
-PARAMS = pltpu.CompilerParams(vmem_limit_bytes=48 * 1024 * 1024)
+
+
+def params(mib):
+    return pltpu.CompilerParams(vmem_limit_bytes=mib * 1024 * 1024)
 
 
 def row_orders(n_z, rows):
@@ -60,15 +63,11 @@
             out[x, 2 * y + 1] = part[group:].astype(jnp.bfloat16)
 
 
-def prep_kernel(tokens, gain, cot_grouped, inv, hid, cot):
-    r = inv[:, :1]
-    for f in range(0, tokens.shape[1], COL):
-        v = tokens[:, f : f + COL].astype(jnp.float32)
-        hid[:, f : f + COL] = (v * r * gain[:, f : f + COL].astype(jnp.float32)).astype(jnp.bfloat16)
+def prep_kernel(cot_grouped, cot):
     cot[...] = cot_grouped[...].T
 
 
-def main_kernel(tokens, gain, hid, cot, inv, back, w, keys, grad, keys_acc, gh, dots):
+def main_kernel(tokens, gain, cot, inv, back, w, keys, grad, keys_acc, gh, dots):
     i = pl.program_id(0)
     toks, feats = tokens.shape
     n_x = w.shape[3]
@@ -82,9 +81,11 @@
     for x in range(n_x):
         at = pl.ds(pl.multiple_of((i * n_x + x) * COL, COL), COL)
         v = tokens[:, at].astype(jnp.float32)
+        g = gain[:, at].astype(jnp.float32)
+        hid = (v * r * g).astype(jnp.bfloat16)
         weight = jnp.concatenate([w[0, y, c, x] for c in range(2) for y in range(2)], axis=0)
-        keys_acc[...] += dot(weight, hid[:, at], 1, 1)
-        part = dot(cot[...], weight, 1, 0) * gain[:, at].astype(jnp.float32)
+        keys_acc[...] += dot(weight, hid, 1, 1)
+        part = dot(cot[...], weight, 1, 0) * g
         gh[:, at] = part
         dots[...] += v * part
 
@@ -136,33 +137,29 @@
             ),
             in_specs=[SMEM] + [VMEM] * 4,
             out_specs=(VMEM,) * 4,
-            compiler_params=PARAMS,
+            compiler_params=params(20),
             cost_estimate=pl.CostEstimate(flops=3 * toks * outw * feats, bytes_accessed=4 * toks * feats, transcendentals=0),
         )(place, tokens_after, gain_row, cot_t, jnp.asarray(grouped))
         cot_grouped = cot_grouped.reshape(4 * group, toks)
     with jax.named_scope("weight_near"):
-        came = lax.ppermute(theirs, "core", ((0, 1), (1, 0)))
-        spread, came = together(spread, came)
+        spread, theirs = together(spread, theirs)
         slab = jnp.pad(spread.reshape(n_x, n_z * rows, width), ((0, 0), (0, group - n_z * rows), (0, 0)))
         w = lax.all_gather(slab, ("y_hi", "y_lo", "core"), axis=0, tiled=False).reshape(n_y, 2, 2, n_x, group, width)
     with jax.named_scope("reduce_core"):
-        came, _ = together(came, slab)
+        theirs, _ = together(theirs, slab)
+        came = lax.ppermute(theirs, "core", ((0, 1), (1, 0)))
         pair = (mine.astype(jnp.float32) + came.astype(jnp.float32)).astype(jnp.bfloat16)
     with jax.named_scope("reduce_x"):
-        pair, inv = together(pair, inv)
+        pair, cot_after, _ = together(pair, cot_grouped, slab)
         parts = lax.all_to_all(pair, "x", split_axis=0, concat_axis=0, tiled=True)
-        hid, cot = pl.pallas_call(
+        cot = pl.pallas_call(
             prep_kernel,
-            out_shape=(
-                jax.ShapeDtypeStruct((toks, feats), jnp.bfloat16),
-                jax.ShapeDtypeStruct((toks, 4 * group), jnp.bfloat16),
-            ),
-            in_specs=[VMEM] * 4,
-            out_specs=(VMEM,) * 2,
-            compiler_params=PARAMS,
-            cost_estimate=pl.CostEstimate(flops=4 * toks * feats, bytes_accessed=4 * toks * feats, transcendentals=0),
-        )(tokens, gain_row, cot_grouped, inv)
-        parts, hid = together(parts, hid)
+            out_shape=jax.ShapeDtypeStruct((toks, 4 * group), jnp.bfloat16),
+            in_specs=[VMEM],
+            out_specs=VMEM,
+            compiler_params=params(8),
+        )(cot_after)
+        parts, cot = together(parts, cot)
         part = add(parts).astype(jnp.bfloat16)
     with jax.named_scope("reduce_y"):
         part, order = together(part, jnp.asarray(natural))
@@ -185,7 +182,6 @@
             in_specs=[
                 whole(toks, feats),
                 whole(1, feats),
-                whole(toks, feats),
                 whole(toks, 4 * group),
                 whole(toks, LANE),
                 whole(outw, 4 * group),
@@ -197,9 +193,9 @@
                 pltpu.VMEM((toks, feats), jnp.float32),
                 pltpu.VMEM((toks, COL), jnp.float32),
             ],
-            compiler_params=PARAMS,
+            compiler_params=params(60),
             cost_estimate=pl.CostEstimate(flops=5 * toks * outw * feats, bytes_accessed=10 * toks * feats, transcendentals=0),
-        )(tokens, gain_row, hid, cot, inv, back, w)
+        )(tokens, gain_row, cot, inv, back, w)
     with jax.named_scope("finish"):
         last, keys_t = together(last, keys_t)
         grad_weight = jnp.sum(last.astype(jnp.float32), axis=0) / (n_y * n_x * n_z * 4)

time: 150 us -> 140 us (0.933)
  blocking collectives: 39.7 us -> 0 us
  waiting for transfers between devices: 39.1 us -> 60.8 us
  starting transfers between devices: 23.3 us -> 36.6 us
  other arithmetic: 9.88 us -> 5.5 us
    all_to_all x1 -> x0, blocking collectives: 39.7 us -> none  [per_device(): lax.all_to_all(spread, ('x', 'z'), split_axis=0, concat_axis=0, tiled=True)]
    all_to_all x0 -> x1, starting transfers between devices: none -> 18.5 us  [per_device(): lax.all_to_all(spread, ('x', 'z'), split_axis=0, concat_axis=0, tiled=True)]
    all_to_all x0 -> x1, waiting for transfers between devices: none -> 12.1 us  [per_device(): lax.all_to_all(spread, ('x', 'z'), split_axis=0, concat_axis=0, tiled=True)]
    all_to_all x1, starting transfers between devices: 9.26 us -> 4.28 us  [per_device(): last = lax.all_to_all(part, 'z', split_axis=0, concat_axis=0, tiled=True)]
    ppermute x1, waiting for transfers between devices: 0.01 us -> 4.52 us  [per_device(): came = lax.ppermute(theirs, 'core', ((0, 1), (1, 0)))]
    all_to_all x1, waiting for transfers between devices: 22.1 us -> 25.3 us  [per_device(): parts = lax.all_to_all(pair, 'x', split_axis=0, concat_axis=0, tiled=True)]
    add x2, other arithmetic: 3.65 us -> 1.1 us  [add(): total = total + values[i].astype(jnp.float32)]
    convert_element_type x1, other arithmetic: 3.58 us -> 1.93 us  [per_device(): (mine.astype(jnp.float32) + came.astype(jnp.float32)).astype(jnp.bfloat16)]
  transfers between devices with their start and end apart: 5 -> 6, of which waited for: 3 -> 5; matrix products, arithmetic and copies ran while one was open for 6% -> 4% of each run, Pallas kernels for 6% -> 8%
where the time goes in v5:
time: 140 us; the launch traced here: 138 us
  waiting for transfers between devices  60.8 us (43%)
  starting transfers between devices  36.6 us (26%)
  between operations  14.2 us (10%)
  Pallas kernels  11.1 us (8%)
  local copies, waits for them, and re-layouts  10.1 us (7%)
  other arithmetic  5.5 us (4%)
    all_to_all x1, waiting for transfers between devices, per_device(): parts = lax.all_to_all(pair, 'x', split_axis=0, concat_axis=0, tiled=True)  25.3 us
    all_to_all x1, starting transfers between devices, per_device(): lax.all_to_all(spread, ('x', 'z'), split_axis=0, concat_axis=0, tiled=True)  18.5 us
    all_to_all x1, waiting for transfers between devices, per_device(): lax.all_to_all(part, ('y_hi', 'y_lo'), split_axis=0, concat_axis=0, tiled...  16.5 us
    all_to_all x1, waiting for transfers between devices, per_device(): lax.all_to_all(spread, ('x', 'z'), split_axis=0, concat_axis=0, tiled=True)  12.1 us
    pallas_call x1, Pallas kernels, per_device(): pl.pallas_call(main_kernel, grid=(n_y,), out_shape=(jax.ShapeDtypeStruct(...  8.84 us
    all_to_all x1, starting transfers between devices, per_device(): lax.all_to_all(part, ('y_hi', 'y_lo'), split_axis=0, concat_axis=0, tiled...  7.08 us
    unnamed x18, local copies, waits for them, and re-layouts  6.29 us
    all_to_all x1, starting transfers between devices, per_device(): parts = lax.all_to_all(pair, 'x', split_axis=0, concat_axis=0, tiled=True)  4.72 us
  transfers between devices with their start and end apart: 6, of which 5 were waited for; matrix products, arithmetic and copies ran while one was open for 4% of the time, Pallas kernels for 8%

profile of v5, /device:TPU:6, one launch (start us, length us, event | category | flops | bytes accessed | tf_op | source)
XLA Modules:
  0.0 138.3 jit_solution(9531901575381201946)
XLA Ops:
  7.2 0.8 copy.12
  7.9 0.1 broadcast_in_dim.17
  8.0 0.7 multiply_convert_fusion
  8.7 0.8 broadcast_in_dim.18
  9.5 18.5 %all-to-all-start = ((bf16[48,11,256]{2,1,0:T(8,128)(2,1)}), bf16[48,11,256]{2,1,0:T(8,128)(2,1)S(1)}, u32[]{:S(2)}, u32[]{:S(2)}) async-start(bf16[48,11,256]{2,1,0:T(8,128)(2,1)} %broadcast_in_dim.18), calls=%async_computation | async-start | bytes 786432 | tf_op jit(solution)/shard_map/weight_far/all_to_all | solution.py:127
  28.1 0.0 all-gather.3.cloned.1.call-start
  28.1 0.7 reshape.53.refs_2_.gain
  28.8 0.0 copy-start.1
  28.8 0.0 copy-start.3
  28.8 1.6 %copy-done.3 = bf16[256,4096]{1,0:T(8,128)(2,1)S(1)} copy-done((bf16[256,4096]{1,0:T(8,128)(2,1)S(1)}, bf16[256,4096]{1,0:T(8,128)(2,1)}, u32[]{:S(2)}) %copy-start.3) | copy-done | bytes 2097176
  30.4 0.0 copy-start.4
  30.4 1.0 copy-done.4
  31.4 0.0 copy-start.5
  31.4 1.0 copy-done.5
  32.3 2.1 %term.1 = (bf16[4,8,136,256]{3,2,1,0:T(8,128)(2,1)S(1)}, bf16[4,8,136,256]{3,2,1,0:T(8,128)(2,1)S(1)}, bf16[2,272,256]{2,1,0:T(8,128)(2,1)S(1)}, f32[256,128]{1,0:T(8,128)S(1)}) custom-call(s32[1]{0:T(128)} %bitcast.refs_0_, bf16[256,4096]{1,0:T(8,128)(2,1)S(1)} %copy-done.3, bf16[1,4096]{1,0:T(2,128)(2,1)S(1)} %reshape.53.refs_2_.gain, ...), custom_call_target="tpu_custom_call" | custom-call | flops 1660944384 | bytes 4194304 | tf_op jit(solution)/shard_map/term/pallas_call | solution.py:130
  34.5 0.0 copy-done.1
  34.5 0.0 copy-start.2
  34.5 1.4 %copy-done.2 = bf16[4,8,136,256]{3,2,1,0:T(8,128)(2,1)} copy-done((bf16[4,8,136,256]{3,2,1,0:T(8,128)(2,1)}, bf16[4,8,136,256]{3,2,1,0:T(8,128)(2,1)S(1)}, u32[]{:S(2)}) %copy-start.2) | copy-done | bytes 2228248
  35.9 0.0 copy-start.6
  35.9 0.6 copy-done.6
  36.5 12.1 %all-to-all-done = bf16[48,11,256]{2,1,0:T(8,128)(2,1)S(1)} async-done(((bf16[48,11,256]{2,1,0:T(8,128)(2,1)}), bf16[48,11,256]{2,1,0:T(8,128)(2,1)S(1)}, u32[]{:S(2)}, u32[]{:S(2)}) %all-to-all-start) | async-done | bytes 270368 | tf_op jit(solution)/shard_map/weight_far/all_to_all | solution.py:127
  48.6 0.1 reshape.54
  48.7 0.7 pad.4
  49.5 0.0 all-gather.3.cloned.1.call-update
  49.5 1.9 %collective-permute-start = (bf16[4,8,136,256]{3,2,1,0:T(8,128)(2,1)}, bf16[4,8,136,256]{3,2,1,0:T(8,128)(2,1)S(1)}, u32[]{:S(2)}, u32[]{:S(2)}) collective-permute-start(bf16[4,8,136,256]{3,2,1,0:T(8,128)(2,1)} %copy-done.2), channel_id=1, source_target_pairs={{0,1},{1,0},{2,3},{3,2},{4,5},{5,4},{6,7},{7,6},{8,9},{9,8},{10,11... | collective-permute-start | bytes 6684680 | tf_op jit(solution)/shard_map/reduce_core/ppermute | solution.py:150
  51.4 4.5 %collective-permute-done = bf16[4,8,136,256]{3,2,1,0:T(8,128)(2,1)S(1)} collective-permute-done((bf16[4,8,136,256]{3,2,1,0:T(8,128)(2,1)}, bf16[4,8,136,256]{3,2,1,0:T(8,128)(2,1)S(1)}, u32[]{:S(2)}, u32[]{:S(2)}) %collective-permute-start) | collective-permute-done | bytes 2228256 | tf_op jit(solution)/shard_map/reduce_core/ppermute | solution.py:150
  56.0 1.9 %add_convert_fusion = bf16[4,8,136,256]{3,2,1,0:T(8,128)(2,1)} fusion(bf16[4,8,136,256]{3,2,1,0:T(8,128)(2,1)S(1)} %collective-permute-done, bf16[4,8,136,256]{3,2,1,0:T(8,128)(2,1)S(1)} %get-tuple-element.27), kind=kLoop, calls=%fused_computation | loop fusion | flops 4456448 | bytes 6684672 | tf_op jit(solution)/shard_map/reduce_core/convert_element_type | solution.py:151
  57.9 4.7 %all-to-all-start.1 = ((bf16[4,8,136,256]{3,2,1,0:T(8,128)(2,1)}), bf16[4,8,136,256]{3,2,1,0:T(8,128)(2,1)S(1)}, u32[]{:S(2)}, u32[]{:S(2)}) async-start(bf16[4,8,136,256]{3,2,1,0:T(8,128)(2,1)} %add_convert_fusion), calls=%async_computation.1 | async-start | bytes 4456448 | tf_op jit(solution)/shard_map/reduce_x/all_to_all | solution.py:154
  62.6 0.1 reduce_x.1.cot
  62.7 0.0 copy-start
  62.8 0.7 copy-done
  63.5 0.0 copy-start.7
  63.5 25.3 %all-to-all-done.1 = bf16[4,8,136,256]{3,2,1,0:T(8,128)(2,1)S(1)} async-done(((bf16[4,8,136,256]{3,2,1,0:T(8,128)(2,1)}), bf16[4,8,136,256]{3,2,1,0:T(8,128)(2,1)S(1)}, u32[]{:S(2)}, u32[]{:S(2)}) %all-to-all-start.1) | async-done | bytes 2228256 | tf_op jit(solution)/shard_map/reduce_x/all_to_all | solution.py:154
  88.8 1.1 fusion
  89.9 7.1 %all-to-all-start.2 = ((bf16[8,136,256]{2,1,0:T(8,128)(2,1)}), bf16[8,136,256]{2,1,0:T(8,128)(2,1)S(1)}, u32[]{:S(2)}, u32[]{:S(2)}) async-start(bf16[8,136,256]{2,1,0:T(8,128)(2,1)} %fusion), calls=%async_computation.2 | async-start | bytes 1114112 | tf_op jit(solution)/shard_map/reduce_y/all_to_all | solution.py:166
  96.9 0.0 copy-done.7
  97.0 1.0 select_convert_fusion.back
  98.0 16.5 %all-to-all-done.2 = bf16[8,136,256]{2,1,0:T(8,128)(2,1)S(1)} async-done(((bf16[8,136,256]{2,1,0:T(8,128)(2,1)}), bf16[8,136,256]{2,1,0:T(8,128)(2,1)S(1)}, u32[]{:S(2)}, u32[]{:S(2)}) %all-to-all-start.2) | async-done | bytes 557088 | tf_op jit(solution)/shard_map/reduce_y/all_to_all | solution.py:166
  114.6 0.1 fusion.5
  114.6 0.7 reshape.56
  115.3 4.3 %all-to-all-start.3 = ((bf16[12,11,256]{2,1,0:T(8,128)(2,1)}), bf16[12,11,256]{2,1,0:T(8,128)(2,1)S(1)}, u32[]{:S(2)}, u32[]{:S(2)}) async-start(bf16[12,11,256]{2,1,0:T(8,128)(2,1)} %reshape.56), calls=%async_computation.3 | async-start | bytes 196608 | tf_op jit(solution)/shard_map/reduce_z/all_to_all | solution.py:172
  119.6 0.0 all-gather.3.cloned.1.call-done
  119.6 8.8 %main.1 = (bf16[528,256]{1,0:T(8,128)(2,1)}, bf16[256,4096]{1,0:T(8,128)(2,1)}) custom-call(bf16[256,4096]{1,0:T(8,128)(2,1)} %tokens.1, bf16[1,4096]{1,0:T(2,128)(2,1)} %copy-done.1, bf16[256,544]{1,0:T(8,128)(2,1)} %copy-done, f32[256,128]{1,0:T(8,128)} %copy-done.6, bf16[528,544]{1,0:T(8,128)(2,1)} %select_convert_fusion.back, ...), custom_call_target="tpu_custom_call" | custom-call | flops 2768240640 | bytes 10485760 | tf_op jit(solution)/shard_map/main/pallas_call | solution.py:175
  128.5 2.4 %all-to-all-done.3 = bf16[12,11,256]{2,1,0:T(8,128)(2,1)S(1)} async-done(((bf16[12,11,256]{2,1,0:T(8,128)(2,1)}), bf16[12,11,256]{2,1,0:T(8,128)(2,1)S(1)}, u32[]{:S(2)}, u32[]{:S(2)}) %all-to-all-start.3) | async-done | bytes 67616 | tf_op jit(solution)/shard_map/reduce_z/all_to_all | solution.py:172
  130.9 0.6 broadcast_multiply_fusion
  (6 shorter events, 0.1 us)
Async XLA Ops:
  9.5 39.1 %all-to-all-start = ((bf16[48,11,256]{2,1,0:T(8,128)(2,1)}), bf16[48,11,256]{2,1,0:T(8,128)(2,1)S(1)}, u32[]{:S(2)}, u32[]{:S(2)}) async-start(bf16[48,11,256]{2,1,0:T(8,128)(2,1)} %broadcast_in_dim.18), calls=%async_computation | async-start | bytes 786432 | tf_op jit(solution)/shard_map/weight_far/all_to_all | solution.py:127
  28.1 91.6 %all-gather.3.cloned.1.call-start = ((), (), s32[]{:S(2)}) async-start(), calls=%async_computation.4 | async-start | bytes 4734976 | tf_op jit(solution)/shard_map/weight_near/all_gather | solution.py:147
  28.8 5.6 %copy-start.1 = (bf16[1,4096]{1,0:T(2,128)(2,1)}, bf16[1,4096]{1,0:T(2,128)(2,1)S(1)}, u32[]{:S(2)}) copy-start(bf16[1,4096]{1,0:T(2,128)(2,1)S(1)} %reshape.53.refs_2_.gain) | copy-start | bytes 24580
  28.8 1.6 %copy-start.3 = (bf16[256,4096]{1,0:T(8,128)(2,1)S(1)}, bf16[256,4096]{1,0:T(8,128)(2,1)}, u32[]{:S(2)}) copy-start(bf16[256,4096]{1,0:T(8,128)(2,1)} %tokens.1) | copy-start | bytes 6291460
  30.4 1.0 copy-start.4
  31.4 1.0 copy-start.5
  34.5 1.4 %copy-start.2 = (bf16[4,8,136,256]{3,2,1,0:T(8,128)(2,1)}, bf16[4,8,136,256]{3,2,1,0:T(8,128)(2,1)S(1)}, u32[]{:S(2)}) copy-start(bf16[4,8,136,256]{3,2,1,0:T(8,128)(2,1)S(1)} %get-tuple-element.32) | copy-start | bytes 6684676
  35.9 0.7 copy-start.6
  49.5 6.5 %collective-permute-start = (bf16[4,8,136,256]{3,2,1,0:T(8,128)(2,1)}, bf16[4,8,136,256]{3,2,1,0:T(8,128)(2,1)S(1)}, u32[]{:S(2)}, u32[]{:S(2)}) collective-permute-start(bf16[4,8,136,256]{3,2,1,0:T(8,128)(2,1)} %copy-done.2), channel_id=1, source_target_pairs={{0,1},{1,0},{2,3},{3,2},{4,5},{5,4},{6,7},{7,6},{8,9},{9,8},{10,11... | collective-permute-start | bytes 6684680 | tf_op jit(solution)/shard_map/reduce_core/ppermute | solution.py:150
  57.9 30.9 %all-to-all-start.1 = ((bf16[4,8,136,256]{3,2,1,0:T(8,128)(2,1)}), bf16[4,8,136,256]{3,2,1,0:T(8,128)(2,1)S(1)}, u32[]{:S(2)}, u32[]{:S(2)}) async-start(bf16[4,8,136,256]{3,2,1,0:T(8,128)(2,1)} %add_convert_fusion), calls=%async_computation.1 | async-start | bytes 4456448 | tf_op jit(solution)/shard_map/reduce_x/all_to_all | solution.py:154
  62.7 0.7 copy-start
  63.5 33.5 %copy-start.7 = (s32[528,1]{0,1:T(1,128)S(1)}, s32[528,1]{0,1:T(1,128)}, u32[]{:S(2)}) copy-start(s32[528,1]{0,1:T(1,128)} %constant.19.clone) | copy-start | bytes 6340
  89.9 24.6 %all-to-all-start.2 = ((bf16[8,136,256]{2,1,0:T(8,128)(2,1)}), bf16[8,136,256]{2,1,0:T(8,128)(2,1)S(1)}, u32[]{:S(2)}, u32[]{:S(2)}) async-start(bf16[8,136,256]{2,1,0:T(8,128)(2,1)} %fusion), calls=%async_computation.2 | async-start | bytes 1114112 | tf_op jit(solution)/shard_map/reduce_y/all_to_all | solution.py:166
  115.3 15.5 %all-to-all-start.3 = ((bf16[12,11,256]{2,1,0:T(8,128)(2,1)}), bf16[12,11,256]{2,1,0:T(8,128)(2,1)S(1)}, u32[]{:S(2)}, u32[]{:S(2)}) async-start(bf16[12,11,256]{2,1,0:T(8,128)(2,1)} %reshape.56), calls=%async_computation.3 | async-start | bytes 196608 | tf_op jit(solution)/shard_map/reduce_z/all_to_all | solution.py:172
Sparse Core Ops, SparseCore 0:
  49.6 42.3 all-gather.2

commit v6 on v5

--- a/solution.py
+++ b/solution.py
@@ -59,8 +59,9 @@
         y, x = divmod(f // COL, n_x)
         for out, c in ((theirs, 1 - place[0]), (mine, place[0])):
             part = dot(cot_grouped[c], hid, 1, 0)
-            out[x, 2 * y] = part[:group].astype(jnp.bfloat16)
-            out[x, 2 * y + 1] = part[group:].astype(jnp.bfloat16)
+            slot = lax.rem(x + n_x - place[1], n_x)
+            out[slot, 2 * y] = part[:group].astype(jnp.bfloat16)
+            out[slot, 2 * y + 1] = part[group:].astype(jnp.bfloat16)
 
 
 def prep_kernel(cot_grouped, cot):
@@ -100,7 +101,7 @@
 
 def add(values):
     total = values[0].astype(jnp.float32)
-    for i in range(1, values.shape[0]):
+    for i in range(1, len(values)):
         total = total + values[i].astype(jnp.float32)
     return total
 
@@ -115,7 +116,7 @@
     toks, feats = tokens.shape
     outw = cotangent.shape[1]
     group, grouped, natural = row_orders(n_z, rows)
-    place = lax.axis_index("core").astype(jnp.int32).reshape(1)
+    place = jnp.stack([lax.axis_index("core"), lax.axis_index("x")]).astype(jnp.int32)
     gain_row = gain.reshape(1, feats)
     cot_t = cotangent.T
 
@@ -142,16 +143,16 @@
         )(place, tokens_after, gain_row, cot_t, jnp.asarray(grouped))
         cot_grouped = cot_grouped.reshape(4 * group, toks)
     with jax.named_scope("weight_near"):
-        spread, theirs = together(spread, theirs)
+        came = lax.ppermute(theirs, "core", ((0, 1), (1, 0)))
+        pairs = [(mine[s].astype(jnp.float32) + came[s].astype(jnp.float32)).astype(jnp.bfloat16) for s in range(n_x)]
+        parts = [pairs[0]]
+        for s in range(1, n_x):
+            parts.append(lax.ppermute(pairs[s], "x", [(j, (j + s) % n_x) for j in range(n_x)]))
+        spread, parts[1], parts[-1] = together(spread, parts[1], parts[-1])
         slab = jnp.pad(spread.reshape(n_x, n_z * rows, width), ((0, 0), (0, group - n_z * rows), (0, 0)))
         w = lax.all_gather(slab, ("y_hi", "y_lo", "core"), axis=0, tiled=False).reshape(n_y, 2, 2, n_x, group, width)
-    with jax.named_scope("reduce_core"):
-        theirs, _ = together(theirs, slab)
-        came = lax.ppermute(theirs, "core", ((0, 1), (1, 0)))
-        pair = (mine.astype(jnp.float32) + came.astype(jnp.float32)).astype(jnp.bfloat16)
     with jax.named_scope("reduce_x"):
-        pair, cot_after, _ = together(pair, cot_grouped, slab)
-        parts = lax.all_to_all(pair, "x", split_axis=0, concat_axis=0, tiled=True)
+        cot_after, _ = together(cot_grouped, slab)
         cot = pl.pallas_call(
             prep_kernel,
             out_shape=jax.ShapeDtypeStruct((toks, 4 * group), jnp.bfloat16),
@@ -159,7 +160,7 @@
             out_specs=VMEM,
             compiler_params=params(8),
         )(cot_after)
-        parts, cot = together(parts, cot)
+        cot, *parts = together(cot, *parts)
         part = add(parts).astype(jnp.bfloat16)
     with jax.named_scope("reduce_y"):
         part, order = together(part, jnp.asarray(natural))

time: 140 us -> 142 us (1.014)
  starting transfers between devices: 36.6 us -> 44.6 us
  waiting for transfers between devices: 60.8 us -> 54 us
  Pallas kernels: 11.1 us -> 13 us
    all_to_all x1 -> x0, waiting for transfers between devices: 25.3 us -> none  [per_device(): parts = lax.all_to_all(pair, 'x', split_axis=0, concat_axis=0, tiled=True)]
    ppermute x0 -> x3, waiting for transfers between devices: none -> 16.4 us  [per_device(): lax.ppermute(pairs[s], 'x', [(j, (j + s) % n_x) for j in range(n_x)])]
    ppermute x0 -> x3, starting transfers between devices: none -> 9.36 us  [per_device(): lax.ppermute(pairs[s], 'x', [(j, (j + s) % n_x) for j in range(n_x)])]
    all_to_all x1, waiting for transfers between devices: 16.5 us -> 22.7 us  [per_device(): lax.all_to_all(part, ('y_hi', 'y_lo'), split_axis=0, concat_axis=0, tiled...]
    all_to_all x1 -> x0, starting transfers between devices: 4.72 us -> none  [per_device(): parts = lax.all_to_all(pair, 'x', split_axis=0, concat_axis=0, tiled=True)]
    ppermute x1, waiting for transfers between devices: 4.52 us -> 0.01 us  [per_device(): came = lax.ppermute(theirs, 'core', ((0, 1), (1, 0)))]
    all_to_all x1, starting transfers between devices: 4.28 us -> 7.52 us  [per_device(): last = lax.all_to_all(part, 'z', split_axis=0, concat_axis=0, tiled=True)]
    convert_element_type x1 -> x2, other arithmetic: 1.93 us -> 4.16 us  [the longest x1 3.08 us: per_device(): (mine[s].astype(jnp.float32) + came[s].astype(jnp.float32)).astype(jnp.bf...]
  transfers between devices with their start and end apart: 6 -> 8, of which waited for: 5 -> 6; matrix products, arithmetic and copies ran while one was open for 4% -> 4% of each run, Pallas kernels for 8% -> 6%
where the time goes in v6:
time: 142 us; the launch traced here: 141 us
  waiting for transfers between devices  54 us (38%)
  starting transfers between devices  44.6 us (31%)
  between operations  14.2 us (10%)
  Pallas kernels  13 us (9%)
  local copies, waits for them, and re-layouts  8.78 us (6%)
  other arithmetic  6.75 us (5%)
    all_to_all x1, waiting for transfers between devices, per_device(): lax.all_to_all(part, ('y_hi', 'y_lo'), split_axis=0, concat_axis=0, tiled...  22.7 us
    all_to_all x1, starting transfers between devices, per_device(): lax.all_to_all(spread, ('x', 'z'), split_axis=0, concat_axis=0, tiled=True)  18.6 us
    ppermute x3, waiting for transfers between devices, per_device(): lax.ppermute(pairs[s], 'x', [(j, (j + s) % n_x) for j in range(n_x)])  16.4 us
    all_to_all x1, waiting for transfers between devices, per_device(): lax.all_to_all(spread, ('x', 'z'), split_axis=0, concat_axis=0, tiled=True)  12.1 us
    ppermute x3, starting transfers between devices, per_device(): lax.ppermute(pairs[s], 'x', [(j, (j + s) % n_x) for j in range(n_x)])  9.36 us
    pallas_call x1, Pallas kernels, per_device(): pl.pallas_call(main_kernel, grid=(n_y,), out_shape=(jax.ShapeDtypeStruct(...  8.84 us
    all_to_all x1, starting transfers between devices, per_device(): last = lax.all_to_all(part, 'z', split_axis=0, concat_axis=0, tiled=True)  7.52 us
    all_to_all x1, starting transfers between devices, per_device(): lax.all_to_all(part, ('y_hi', 'y_lo'), split_axis=0, concat_axis=0, tiled...  7.24 us
  transfers between devices with their start and end apart: 8, of which 6 were waited for; matrix products, arithmetic and copies ran while one was open for 4% of the time, Pallas kernels for 6%

profile of v6, /device:TPU:6, one launch (start us, length us, event | category | flops | bytes accessed | tf_op | source)
XLA Modules:
  0.0 141.3 jit_solution(3743259251069732710)
XLA Ops:
  7.2 0.8 copy.12
  7.9 0.1 broadcast_in_dim.17
  8.0 0.7 multiply_convert_fusion
  8.7 0.8 broadcast_in_dim.18
  9.5 0.7 reshape.57.refs_2_.gain
  10.2 0.0 copy-start.1
  10.2 0.1 pad_add_fusion.refs_0_
  10.3 0.0 copy-start.2
  10.3 1.6 %copy-done.2 = bf16[256,4096]{1,0:T(8,128)(2,1)S(1)} copy-done((bf16[256,4096]{1,0:T(8,128)(2,1)S(1)}, bf16[256,4096]{1,0:T(8,128)(2,1)}, u32[]{:S(2)}) %copy-start.2) | copy-done | bytes 2097176
  11.9 0.0 copy-start.3
  11.9 1.0 copy-done.3
  12.9 0.0 copy-start.4
  12.9 1.0 copy-done.4
  13.8 4.0 %term.1 = (bf16[4,8,136,256]{3,2,1,0:T(8,128)(2,1)S(1)}, bf16[4,8,136,256]{3,2,1,0:T(8,128)(2,1)}, bf16[2,272,256]{2,1,0:T(8,128)(2,1)S(1)}, f32[256,128]{1,0:T(8,128)S(1)}) custom-call(s32[2]{0:T(128)S(1)} %pad_add_fusion.refs_0_, bf16[256,4096]{1,0:T(8,128)(2,1)S(1)} %copy-done.2, bf16[1,4096]{1,0:T(2,128)(2,1)S(1)} %reshape.57.refs_2_.gain, ...), custom_call_target="tpu_custom_call" | custom-call | flops 1660944384 | bytes 4194304 | tf_op jit(solution)/shard_map/term/pallas_call | solution.py:131
  17.8 0.0 copy-done.1
  17.8 0.0 copy-start.5
  17.8 0.7 copy-done.5
  18.5 1.9 %collective-permute-start = (bf16[4,8,136,256]{3,2,1,0:T(8,128)(2,1)}, bf16[4,8,136,256]{3,2,1,0:T(8,128)(2,1)}, u32[]{:S(2)}, u32[]{:S(2)}) collective-permute-start(bf16[4,8,136,256]{3,2,1,0:T(8,128)(2,1)} %get-tuple-element.32), channel_id=1, source_target_pairs={{0,1},{1,0},{2,3},{3,2},{4,5},{5,4},{6,7},{7,6},{8,9},{9,8},{10,11... | collective-permute-start | bytes 6684680 | tf_op jit(solution)/shard_map/weight_near/ppermute | solution.py:146
  20.4 18.6 %all-to-all-start = ((bf16[48,11,256]{2,1,0:T(8,128)(2,1)}), bf16[48,11,256]{2,1,0:T(8,128)(2,1)S(1)}, u32[]{:S(2)}, u32[]{:S(2)}) async-start(bf16[48,11,256]{2,1,0:T(8,128)(2,1)} %broadcast_in_dim.18), calls=%async_computation | async-start | bytes 786432 | tf_op jit(solution)/shard_map/weight_far/all_to_all | solution.py:128
  39.0 0.0 all-gather.3.cloned.1.call-start
  39.1 0.0 collective-permute-done
  39.1 3.1 %fusion.3 = (bf16[8,136,256]{2,1,0:T(8,128)(2,1)}, bf16[8,136,256]{2,1,0:T(8,128)(2,1)S(1)}, bf16[8,136,256]{2,1,0:T(8,128)(2,1)}, bf16[8,136,256]{2,1,0:T(8,128)(2,1)}) fusion(bf16[4,8,136,256]{3,2,1,0:T(8,128)(2,1)} %collective-permute-done, bf16[4,8,136,256]{3,2,1,0:T(8,128)(2,1)S(1)} %get-tuple-element.31), kind=kLoop, calls=%fused_computation.10 | loop fusion | flops 4456448 | bytes 6684672 | tf_op jit(solution)/shard_map/weight_near/convert_element_type | solution.py:147
  42.1 0.0 copy-start.6
  42.1 2.2 %collective-permute-start.1 = (bf16[8,136,256]{2,1,0:T(8,128)(2,1)}, bf16[8,136,256]{2,1,0:T(8,128)(2,1)S(1)}, u32[]{:S(2)}, u32[]{:S(2)}) collective-permute-start(bf16[8,136,256]{2,1,0:T(8,128)(2,1)} %get-tuple-element.56), channel_id=1, source_target_pairs={{0,48},{48,96},{96,144},{144,0},{1,49},{49,97},{97,145},{145,1},{2... | collective-permute-start | bytes 1671176 | tf_op jit(solution)/shard_map/weight_near/ppermute | solution.py:150
  44.4 3.7 %collective-permute-start.2 = (bf16[8,136,256]{2,1,0:T(8,128)(2,1)}, bf16[8,136,256]{2,1,0:T(8,128)(2,1)S(1)}, u32[]{:S(2)}, u32[]{:S(2)}) collective-permute-start(bf16[8,136,256]{2,1,0:T(8,128)(2,1)} %get-tuple-element.55), channel_id=1, source_target_pairs={{0,144},{48,0},{96,48},{144,96},{1,145},{49,1},{97,49},{145,97},{2... | collective-permute-start | bytes 1671176 | tf_op jit(solution)/shard_map/weight_near/ppermute | solution.py:150
  48.1 12.1 %all-to-all-done = bf16[48,11,256]{2,1,0:T(8,128)(2,1)S(1)} async-done(((bf16[48,11,256]{2,1,0:T(8,128)(2,1)}), bf16[48,11,256]{2,1,0:T(8,128)(2,1)S(1)}, u32[]{:S(2)}, u32[]{:S(2)}) %all-to-all-start) | async-done | bytes 270368 | tf_op jit(solution)/shard_map/weight_far/all_to_all | solution.py:128
  60.2 0.6 collective-permute-done.1
  60.8 2.7 %collective-permute-done.2 = bf16[8,136,256]{2,1,0:T(8,128)(2,1)S(1)} collective-permute-done((bf16[8,136,256]{2,1,0:T(8,128)(2,1)}, bf16[8,136,256]{2,1,0:T(8,128)(2,1)S(1)}, u32[]{:S(2)}, u32[]{:S(2)}) %collective-permute-start.2) | collective-permute-done | bytes 557088 | tf_op jit(solution)/shard_map/weight_near/ppermute | solution.py:150
  63.6 0.1 reshape.59
  63.7 0.7 pad.4
  64.4 0.0 all-gather.3.cloned.1.call-update
  64.5 0.0 copy-done.6
  64.5 3.4 %collective-permute-start.3 = (bf16[8,136,256]{2,1,0:T(8,128)(2,1)S(1)}, bf16[8,136,256]{2,1,0:T(8,128)(2,1)S(1)}, u32[]{:S(2)}, u32[]{:S(2)}) collective-permute-start(bf16[8,136,256]{2,1,0:T(8,128)(2,1)S(1)} %copy-done.6), channel_id=1, source_target_pairs={{0,96},{48,144},{96,0},{144,48},{1,97},{49,145},{97,1},{145,49},{2... | collective-permute-start | bytes 1671176 | tf_op jit(solution)/shard_map/weight_near/ppermute | solution.py:150
  67.9 0.1 reduce_x.1.cot
  68.0 0.0 copy-start
  68.0 0.7 copy-done
  68.8 13.1 %collective-permute-done.3 = bf16[8,136,256]{2,1,0:T(8,128)(2,1)S(1)} collective-permute-done((bf16[8,136,256]{2,1,0:T(8,128)(2,1)S(1)}, bf16[8,136,256]{2,1,0:T(8,128)(2,1)S(1)}, u32[]{:S(2)}, u32[]{:S(2)}) %collective-permute-start.3) | collective-permute-done | bytes 557088 | tf_op jit(solution)/shard_map/weight_near/ppermute | solution.py:150
  81.8 1.1 add_convert_fusion
  82.9 0.0 copy-start.7
  82.9 7.2 %all-to-all-start.1 = ((bf16[8,136,256]{2,1,0:T(8,128)(2,1)}), bf16[8,136,256]{2,1,0:T(8,128)(2,1)S(1)}, u32[]{:S(2)}, u32[]{:S(2)}) async-start(bf16[8,136,256]{2,1,0:T(8,128)(2,1)} %add_convert_fusion), calls=%async_computation.1 | async-start | bytes 1114112 | tf_op jit(solution)/shard_map/reduce_y/all_to_all | solution.py:167
  90.1 0.0 copy-done.7
  90.2 1.0 select_convert_fusion.back
  91.2 22.7 %all-to-all-done.1 = bf16[8,136,256]{2,1,0:T(8,128)(2,1)S(1)} async-done(((bf16[8,136,256]{2,1,0:T(8,128)(2,1)}), bf16[8,136,256]{2,1,0:T(8,128)(2,1)S(1)}, u32[]{:S(2)}, u32[]{:S(2)}) %all-to-all-start.1) | async-done | bytes 557088 | tf_op jit(solution)/shard_map/reduce_y/all_to_all | solution.py:167
  114.0 0.1 fusion.8
  114.0 0.7 reshape.60
  114.7 7.5 %all-to-all-start.2 = ((bf16[12,11,256]{2,1,0:T(8,128)(2,1)}), bf16[12,11,256]{2,1,0:T(8,128)(2,1)S(1)}, u32[]{:S(2)}, u32[]{:S(2)}) async-start(bf16[12,11,256]{2,1,0:T(8,128)(2,1)} %reshape.60), calls=%async_computation.2 | async-start | bytes 196608 | tf_op jit(solution)/shard_map/reduce_z/all_to_all | solution.py:173
  122.2 0.0 all-gather.3.cloned.1.call-done
  122.3 8.8 %main.1 = (bf16[528,256]{1,0:T(8,128)(2,1)}, bf16[256,4096]{1,0:T(8,128)(2,1)}) custom-call(bf16[256,4096]{1,0:T(8,128)(2,1)} %tokens.1, bf16[1,4096]{1,0:T(2,128)(2,1)} %copy-done.1, bf16[256,544]{1,0:T(8,128)(2,1)} %copy-done, f32[256,128]{1,0:T(8,128)} %copy-done.5, bf16[528,544]{1,0:T(8,128)(2,1)} %select_convert_fusion.back, ...), custom_call_target="tpu_custom_call" | custom-call | flops 2768240640 | bytes 10485760 | tf_op jit(solution)/shard_map/main/pallas_call | solution.py:176
  131.1 2.8 %all-to-all-done.2 = bf16[12,11,256]{2,1,0:T(8,128)(2,1)S(1)} async-done(((bf16[12,11,256]{2,1,0:T(8,128)(2,1)}), bf16[12,11,256]{2,1,0:T(8,128)(2,1)S(1)}, u32[]{:S(2)}, u32[]{:S(2)}) %all-to-all-start.2) | async-done | bytes 67616 | tf_op jit(solution)/shard_map/reduce_z/all_to_all | solution.py:173
  133.9 0.6 broadcast_multiply_fusion
  (6 shorter events, 0.1 us)
Async XLA Ops:
  10.2 7.6 %copy-start.1 = (bf16[1,4096]{1,0:T(2,128)(2,1)}, bf16[1,4096]{1,0:T(2,128)(2,1)S(1)}, u32[]{:S(2)}) copy-start(bf16[1,4096]{1,0:T(2,128)(2,1)S(1)} %reshape.57.refs_2_.gain) | copy-start | bytes 24580
  10.3 1.6 %copy-start.2 = (bf16[256,4096]{1,0:T(8,128)(2,1)S(1)}, bf16[256,4096]{1,0:T(8,128)(2,1)}, u32[]{:S(2)}) copy-start(bf16[256,4096]{1,0:T(8,128)(2,1)} %tokens.1) | copy-start | bytes 6291460
  11.9 1.0 copy-start.3
  12.9 1.0 copy-start.4
  17.8 0.7 copy-start.5
  18.5 20.5 %collective-permute-start = (bf16[4,8,136,256]{3,2,1,0:T(8,128)(2,1)}, bf16[4,8,136,256]{3,2,1,0:T(8,128)(2,1)}, u32[]{:S(2)}, u32[]{:S(2)}) collective-permute-start(bf16[4,8,136,256]{3,2,1,0:T(8,128)(2,1)} %get-tuple-element.32), channel_id=1, source_target_pairs={{0,1},{1,0},{2,3},{3,2},{4,5},{5,4},{6,7},{7,6},{8,9},{9,8},{10,11... | collective-permute-start | bytes 6684680 | tf_op jit(solution)/shard_map/weight_near/ppermute | solution.py:146
  20.4 39.8 %all-to-all-start = ((bf16[48,11,256]{2,1,0:T(8,128)(2,1)}), bf16[48,11,256]{2,1,0:T(8,128)(2,1)S(1)}, u32[]{:S(2)}, u32[]{:S(2)}) async-start(bf16[48,11,256]{2,1,0:T(8,128)(2,1)} %broadcast_in_dim.18), calls=%async_computation | async-start | bytes 786432 | tf_op jit(solution)/shard_map/weight_far/all_to_all | solution.py:128
  39.0 83.2 %all-gather.3.cloned.1.call-start = ((), (), s32[]{:S(2)}) async-start(), calls=%async_computation.3 | async-start | bytes 4734976 | tf_op jit(solution)/shard_map/weight_near/all_gather | solution.py:153
  42.1 22.3 %copy-start.6 = (bf16[8,136,256]{2,1,0:T(8,128)(2,1)S(1)}, bf16[8,136,256]{2,1,0:T(8,128)(2,1)}, u32[]{:S(2)}) copy-start(bf16[8,136,256]{2,1,0:T(8,128)(2,1)} %get-tuple-element.53) | copy-start | bytes 1671172
  42.1 18.7 %collective-permute-start.1 = (bf16[8,136,256]{2,1,0:T(8,128)(2,1)}, bf16[8,136,256]{2,1,0:T(8,128)(2,1)S(1)}, u32[]{:S(2)}, u32[]{:S(2)}) collective-permute-start(bf16[8,136,256]{2,1,0:T(8,128)(2,1)} %get-tuple-element.56), channel_id=1, source_target_pairs={{0,48},{48,96},{96,144},{144,0},{1,49},{49,97},{97,145},{145,1},{2... | collective-permute-start | bytes 1671176 | tf_op jit(solution)/shard_map/weight_near/ppermute | solution.py:150
  44.4 19.2 %collective-permute-start.2 = (bf16[8,136,256]{2,1,0:T(8,128)(2,1)}, bf16[8,136,256]{2,1,0:T(8,128)(2,1)S(1)}, u32[]{:S(2)}, u32[]{:S(2)}) collective-permute-start(bf16[8,136,256]{2,1,0:T(8,128)(2,1)} %get-tuple-element.55), channel_id=1, source_target_pairs={{0,144},{48,0},{96,48},{144,96},{1,145},{49,1},{97,49},{145,97},{2... | collective-permute-start | bytes 1671176 | tf_op jit(solution)/shard_map/weight_near/ppermute | solution.py:150
  64.5 17.4 %collective-permute-start.3 = (bf16[8,136,256]{2,1,0:T(8,128)(2,1)S(1)}, bf16[8,136,256]{2,1,0:T(8,128)(2,1)S(1)}, u32[]{:S(2)}, u32[]{:S(2)}) collective-permute-start(bf16[8,136,256]{2,1,0:T(8,128)(2,1)S(1)} %copy-done.6), channel_id=1, source_target_pairs={{0,96},{48,144},{96,0},{144,48},{1,97},{49,145},{97,1},{145,49},{2... | collective-permute-start | bytes 1671176 | tf_op jit(solution)/shard_map/weight_near/ppermute | solution.py:150
  68.0 0.8 copy-start
  82.9 7.2 %copy-start.7 = (s32[528,1]{0,1:T(1,128)S(1)}, s32[528,1]{0,1:T(1,128)}, u32[]{:S(2)}) copy-start(s32[528,1]{0,1:T(1,128)} %constant.24.clone) | copy-start | bytes 6340
  82.9 31.0 %all-to-all-start.1 = ((bf16[8,136,256]{2,1,0:T(8,128)(2,1)}), bf16[8,136,256]{2,1,0:T(8,128)(2,1)S(1)}, u32[]{:S(2)}, u32[]{:S(2)}) async-start(bf16[8,136,256]{2,1,0:T(8,128)(2,1)} %add_convert_fusion), calls=%async_computation.1 | async-start | bytes 1114112 | tf_op jit(solution)/shard_map/reduce_y/all_to_all | solution.py:167
  114.7 19.2 %all-to-all-start.2 = ((bf16[12,11,256]{2,1,0:T(8,128)(2,1)}), bf16[12,11,256]{2,1,0:T(8,128)(2,1)S(1)}, u32[]{:S(2)}, u32[]{:S(2)}) async-start(bf16[12,11,256]{2,1,0:T(8,128)(2,1)} %reshape.60), calls=%async_computation.2 | async-start | bytes 196608 | tf_op jit(solution)/shard_map/reduce_z/all_to_all | solution.py:173
Sparse Core Ops, SparseCore 0:
  64.6 57.1 all-gather.2

commit v7 on v5

--- a/solution.py
+++ b/solution.py
@@ -67,7 +67,11 @@
     cot[...] = cot_grouped[...].T
 
 
-def main_kernel(tokens, gain, cot, inv, back, w, keys, grad, keys_acc, gh, dots):
+def keys_kernel(order, grouped, keys):
+    keys[...] = dot(pick(order[...], grouped.shape[0]), grouped[...], 1, 0).astype(jnp.bfloat16)
+
+
+def main_kernel(tokens, gain, cot, inv, w, keys, grad, keys_acc, gh, dots):
     i = pl.program_id(0)
     toks, feats = tokens.shape
     n_x = w.shape[3]
@@ -91,7 +95,7 @@
 
     @pl.when(i == pl.num_programs(0) - 1)
     def _():
-        keys[...] = dot(back[...], keys_acc[...].astype(jnp.bfloat16), 1, 0).astype(jnp.bfloat16)
+        keys[...] = keys_acc[...].astype(jnp.bfloat16)
         k = r * r * r * (jnp.sum(dots[...], axis=1, keepdims=True) / feats)
         for f in range(0, feats, COL):
             v = tokens[:, f : f + COL].astype(jnp.float32)
@@ -142,15 +146,13 @@
         )(place, tokens_after, gain_row, cot_t, jnp.asarray(grouped))
         cot_grouped = cot_grouped.reshape(4 * group, toks)
     with jax.named_scope("weight_near"):
-        spread, theirs = together(spread, theirs)
+        came = lax.ppermute(theirs, "core", ((0, 1), (1, 0)))
+        pair = (mine.astype(jnp.float32) + came.astype(jnp.float32)).astype(jnp.bfloat16)
+        spread, pair = together(spread, pair)
         slab = jnp.pad(spread.reshape(n_x, n_z * rows, width), ((0, 0), (0, group - n_z * rows), (0, 0)))
         w = lax.all_gather(slab, ("y_hi", "y_lo", "core"), axis=0, tiled=False).reshape(n_y, 2, 2, n_x, group, width)
-    with jax.named_scope("reduce_core"):
-        theirs, _ = together(theirs, slab)
-        came = lax.ppermute(theirs, "core", ((0, 1), (1, 0)))
-        pair = (mine.astype(jnp.float32) + came.astype(jnp.float32)).astype(jnp.bfloat16)
     with jax.named_scope("reduce_x"):
-        pair, cot_after, _ = together(pair, cot_grouped, slab)
+        cot_after, _ = together(cot_grouped, slab)
         parts = lax.all_to_all(pair, "x", split_axis=0, concat_axis=0, tiled=True)
         cot = pl.pallas_call(
             prep_kernel,
@@ -162,21 +164,15 @@
         parts, cot = together(parts, cot)
         part = add(parts).astype(jnp.bfloat16)
     with jax.named_scope("reduce_y"):
-        part, order = together(part, jnp.asarray(natural))
+        part, inv = together(part, inv)
         parts = lax.all_to_all(part, ("y_hi", "y_lo"), split_axis=0, concat_axis=0, tiled=True)
-        back = pick(order, 4 * group)
-        parts, back = together(parts, back)
-        part = add(parts).astype(jnp.bfloat16)[: n_z * rows].reshape(n_z, rows, width)
-    with jax.named_scope("reduce_z"):
-        part, back = together(part, back)
-        last = lax.all_to_all(part, "z", split_axis=0, concat_axis=0, tiled=True)
     with jax.named_scope("main"):
         whole = lambda *shape: pl.BlockSpec(shape, lambda i: (0,) * len(shape))
-        keys_t, grad_tokens = pl.pallas_call(
+        keys_grouped, grad_tokens = pl.pallas_call(
             main_kernel,
             grid=(n_y,),
             out_shape=(
-                jax.ShapeDtypeStruct((outw, toks), jnp.bfloat16),
+                jax.ShapeDtypeStruct((4 * group, toks), jnp.bfloat16),
                 jax.ShapeDtypeStruct((toks, feats), jnp.bfloat16),
             ),
             in_specs=[
@@ -184,10 +180,9 @@
                 whole(1, feats),
                 whole(toks, 4 * group),
                 whole(toks, LANE),
-                whole(outw, 4 * group),
                 pl.BlockSpec((1, 2, 2, n_x, group, width), lambda i: (i, 0, 0, 0, 0, 0)),
             ],
-            out_specs=(whole(outw, toks), whole(toks, feats)),
+            out_specs=(whole(4 * group, toks), whole(toks, feats)),
             scratch_shapes=[
                 pltpu.VMEM((4 * group, toks), jnp.float32),
                 pltpu.VMEM((toks, feats), jnp.float32),
@@ -195,8 +190,19 @@
             ],
             compiler_params=params(60),
             cost_estimate=pl.CostEstimate(flops=5 * toks * outw * feats, bytes_accessed=10 * toks * feats, transcendentals=0),
-        )(tokens, gain_row, cot, inv, back, w)
-    with jax.named_scope("finish"):
+        )(tokens, gain_row, cot, inv, w)
+    with jax.named_scope("reduce_z"):
+        parts, grad_tokens = together(parts, grad_tokens)
+        part = add(parts).astype(jnp.bfloat16)[: n_z * rows].reshape(n_z, rows, width)
+        part, keys_grouped = together(part, keys_grouped)
+        last = lax.all_to_all(part, "z", split_axis=0, concat_axis=0, tiled=True)
+        keys_t = pl.pallas_call(
+            keys_kernel,
+            out_shape=jax.ShapeDtypeStruct((outw, toks), jnp.bfloat16),
+            in_specs=[VMEM] * 2,
+            out_specs=VMEM,
+            compiler_params=params(8),
+        )(jnp.asarray(natural), keys_grouped)
         last, keys_t = together(last, keys_t)
         grad_weight = jnp.sum(last.astype(jnp.float32), axis=0) / (n_y * n_x * n_z * 4)
     return keys_t.T, grad_tokens, grad_weight

time: 140 us -> 151 us (1.079)
  starting transfers between devices: 36.6 us -> 45.5 us
  Pallas kernels: 11.1 us -> 13.3 us
  waiting for transfers between devices: 60.8 us -> 62.8 us
    all_to_all x1, waiting for transfers between devices: 16.5 us -> 0.01 us  [per_device(): lax.all_to_all(part, ('y_hi', 'y_lo'), split_axis=0, concat_axis=0, tiled...]
    all_gather x1, waiting for transfers between devices: 0.02 us -> 12.3 us  [per_device(): lax.all_gather(slab, ('y_hi', 'y_lo', 'core'), axis=0, tiled=False)]
    all_to_all x1, starting transfers between devices: 4.28 us -> 13.2 us  [per_device(): last = lax.all_to_all(part, 'z', split_axis=0, concat_axis=0, tiled=True)]
    all_to_all x1, waiting for transfers between devices: 2.38 us -> 10.6 us  [per_device(): last = lax.all_to_all(part, 'z', split_axis=0, concat_axis=0, tiled=True)]
    all_to_all x1, waiting for transfers between devices: 12.1 us -> 17.6 us  [per_device(): lax.all_to_all(spread, ('x', 'z'), split_axis=0, concat_axis=0, tiled=True)]
    ppermute x1, waiting for transfers between devices: 4.52 us -> 0.01 us  [per_device(): came = lax.ppermute(theirs, 'core', ((0, 1), (1, 0)))]
    all_to_all x1, waiting for transfers between devices: 25.3 us -> 22.3 us  [per_device(): parts = lax.all_to_all(pair, 'x', split_axis=0, concat_axis=0, tiled=True)]
    convert_element_type x1, other arithmetic: 1.93 us -> 3.56 us  [per_device(): (mine.astype(jnp.float32) + came.astype(jnp.float32)).astype(jnp.bfloat16)]
  transfers between devices with their start and end apart: 6 -> 6, of which waited for: 5 -> 4; matrix products, arithmetic and copies ran while one was open for 4% -> 3% of each run, Pallas kernels for 8% -> 6%
where the time goes in v7:
time: 151 us
  waiting for transfers between devices  62.8 us (42%)
  starting transfers between devices  45.5 us (30%)
  between operations  14.2 us (9%)
  Pallas kernels  13.3 us (9%)
  local copies, waits for them, and re-layouts  8.72 us (6%)
  other arithmetic  6.1 us (4%)
    all_to_all x1, waiting for transfers between devices, per_device(): parts = lax.all_to_all(pair, 'x', split_axis=0, concat_axis=0, tiled=True)  22.3 us
    all_to_all x1, starting transfers between devices, per_device(): lax.all_to_all(spread, ('x', 'z'), split_axis=0, concat_axis=0, tiled=True)  18.6 us
    all_to_all x1, waiting for transfers between devices, per_device(): lax.all_to_all(spread, ('x', 'z'), split_axis=0, concat_axis=0, tiled=True)  17.6 us
    all_to_all x1, starting transfers between devices, per_device(): last = lax.all_to_all(part, 'z', split_axis=0, concat_axis=0, tiled=True)  13.2 us
    all_gather x1, waiting for transfers between devices, per_device(): lax.all_gather(slab, ('y_hi', 'y_lo', 'core'), axis=0, tiled=False)  12.3 us
    all_to_all x1, waiting for transfers between devices, per_device(): last = lax.all_to_all(part, 'z', split_axis=0, concat_axis=0, tiled=True)  10.6 us
    pallas_call x1, Pallas kernels, per_device(): pl.pallas_call(main_kernel, grid=(n_y,), out_shape=(jax.ShapeDtypeStruct(...  8.48 us
    all_to_all x1, starting transfers between devices, per_device(): lax.all_to_all(part, ('y_hi', 'y_lo'), split_axis=0, concat_axis=0, tiled...  7.11 us
  transfers between devices with their start and end apart: 6, of which 4 were waited for; matrix products, arithmetic and copies ran while one was open for 3% of the time, Pallas kernels for 6%

profile of v7, /device:TPU:6, one launch (start us, length us, event | category | flops | bytes accessed | tf_op | source)
XLA Modules:
  0.0 150.6 jit_solution(6787398976232090329)
XLA Ops:
  7.2 0.8 copy.12
  7.9 0.1 broadcast_in_dim.4
  8.0 0.7 multiply_convert_fusion
  8.7 0.8 broadcast_in_dim.10
  9.5 0.7 reshape.53.refs_2_.gain
  10.2 0.0 copy-start.3
  10.2 0.0 copy-start.4
  10.2 1.6 %copy-done.4 = bf16[256,4096]{1,0:T(8,128)(2,1)S(1)} copy-done((bf16[256,4096]{1,0:T(8,128)(2,1)S(1)}, bf16[256,4096]{1,0:T(8,128)(2,1)}, u32[]{:S(2)}) %copy-start.4) | copy-done | bytes 2097176
  11.8 0.0 copy-start.5
  11.8 1.0 copy-done.5
  12.8 0.0 copy-start.6
  12.8 1.0 copy-done.6
  13.7 3.5 %term.1 = (bf16[4,8,136,256]{3,2,1,0:T(8,128)(2,1)S(1)}, bf16[4,8,136,256]{3,2,1,0:T(8,128)(2,1)}, bf16[2,272,256]{2,1,0:T(8,128)(2,1)S(1)}, f32[256,128]{1,0:T(8,128)S(1)}) custom-call(s32[1]{0:T(128)} %bitcast.refs_0_, bf16[256,4096]{1,0:T(8,128)(2,1)S(1)} %copy-done.4, bf16[1,4096]{1,0:T(2,128)(2,1)S(1)} %reshape.53.refs_2_.gain, ...), custom_call_target="tpu_custom_call" | custom-call | flops 1660944384 | bytes 4194304 | tf_op jit(solution)/shard_map/term/pallas_call | solution.py:134
  17.2 0.0 copy-done.3
  17.2 0.0 copy-start.7
  17.2 0.7 copy-done.7
  17.9 1.9 %collective-permute-start = (bf16[4,8,136,256]{3,2,1,0:T(8,128)(2,1)}, bf16[4,8,136,256]{3,2,1,0:T(8,128)(2,1)}, u32[]{:S(2)}, u32[]{:S(2)}) collective-permute-start(bf16[4,8,136,256]{3,2,1,0:T(8,128)(2,1)} %get-tuple-element.27), channel_id=1, source_target_pairs={{0,1},{1,0},{2,3},{3,2},{4,5},{5,4},{6,7},{7,6},{8,9},{9,8},{10,11... | collective-permute-start | bytes 6684680 | tf_op jit(solution)/shard_map/weight_near/ppermute | solution.py:149
  19.8 18.6 %all-to-all-start = ((bf16[48,11,256]{2,1,0:T(8,128)(2,1)}), bf16[48,11,256]{2,1,0:T(8,128)(2,1)S(1)}, u32[]{:S(2)}, u32[]{:S(2)}) async-start(bf16[48,11,256]{2,1,0:T(8,128)(2,1)} %broadcast_in_dim.10), calls=%async_computation | async-start | bytes 786432 | tf_op jit(solution)/shard_map/weight_far/all_to_all | solution.py:131
  38.4 0.0 all-gather.3.cloned.1.call-start
  38.4 0.0 collective-permute-done
  38.4 3.6 %add_convert_fusion = bf16[4,8,136,256]{3,2,1,0:T(8,128)(2,1)} fusion(bf16[4,8,136,256]{3,2,1,0:T(8,128)(2,1)} %collective-permute-done, bf16[4,8,136,256]{3,2,1,0:T(8,128)(2,1)S(1)} %get-tuple-element.26), kind=kLoop, calls=%fused_computation | loop fusion | flops 4456448 | bytes 6684672 | tf_op jit(solution)/shard_map/weight_near/convert_element_type | solution.py:150
  42.0 17.6 %all-to-all-done = bf16[48,11,256]{2,1,0:T(8,128)(2,1)S(1)} async-done(((bf16[48,11,256]{2,1,0:T(8,128)(2,1)}), bf16[48,11,256]{2,1,0:T(8,128)(2,1)S(1)}, u32[]{:S(2)}, u32[]{:S(2)}) %all-to-all-start) | async-done | bytes 270368 | tf_op jit(solution)/shard_map/weight_far/all_to_all | solution.py:131
  59.6 0.1 reshape.55
  59.7 0.7 pad.4
  60.4 0.0 all-gather.3.cloned.1.call-update
  60.5 4.7 %all-to-all-start.1 = ((bf16[4,8,136,256]{3,2,1,0:T(8,128)(2,1)}), bf16[4,8,136,256]{3,2,1,0:T(8,128)(2,1)S(1)}, u32[]{:S(2)}, u32[]{:S(2)}) async-start(bf16[4,8,136,256]{3,2,1,0:T(8,128)(2,1)} %add_convert_fusion), calls=%async_computation.1 | async-start | bytes 4456448 | tf_op jit(solution)/shard_map/reduce_x/all_to_all | solution.py:156
  65.2 0.1 reduce_x.1.cot
  65.3 0.0 copy-start
  65.3 0.7 copy-done
  66.1 22.3 %all-to-all-done.1 = bf16[4,8,136,256]{3,2,1,0:T(8,128)(2,1)S(1)} async-done(((bf16[4,8,136,256]{3,2,1,0:T(8,128)(2,1)}), bf16[4,8,136,256]{3,2,1,0:T(8,128)(2,1)S(1)}, u32[]{:S(2)}, u32[]{:S(2)}) %all-to-all-start.1) | async-done | bytes 2228256 | tf_op jit(solution)/shard_map/reduce_x/all_to_all | solution.py:156
  88.3 1.1 fusion
  89.4 7.1 %all-to-all-start.2 = ((bf16[8,136,256]{2,1,0:T(8,128)(2,1)}), bf16[8,136,256]{2,1,0:T(8,128)(2,1)S(1)}, u32[]{:S(2)}, u32[]{:S(2)}) async-start(bf16[8,136,256]{2,1,0:T(8,128)(2,1)} %fusion), calls=%async_computation.2 | async-start | bytes 1114112 | tf_op jit(solution)/shard_map/reduce_y/all_to_all | solution.py:168
  96.5 12.3 %all-gather.3.cloned.1.call-done = bf16[64,136,256]{2,1,0:T(8,128)(2,1)} async-done(((bf16[4,136,256]{2,1,0:T(8,128)(2,1)}), bf16[64,136,256]{2,1,0:T(8,128)(2,1)}) %all-gather.3.cloned.1.call-update) | async-done | bytes 4456464 | tf_op jit(solution)/shard_map/weight_near/all_gather | solution.py:153
  108.9 8.5 %main.1 = (bf16[544,256]{1,0:T(8,128)(2,1)}, bf16[256,4096]{1,0:T(8,128)(2,1)}) custom-call(bf16[256,4096]{1,0:T(8,128)(2,1)} %tokens.1, bf16[1,4096]{1,0:T(2,128)(2,1)} %copy-done.3, bf16[256,544]{1,0:T(8,128)(2,1)} %copy-done, f32[256,128]{1,0:T(8,128)} %copy-done.7, bf16[4,2,2,4,136,256]{5,4,3,2,1,0:T(8,128)(2,1)} %bitcast.15), custom_call_target="tpu_custom_call" | custom-call | flops 2768240640 | bytes 10485760 | tf_op jit(solution)/shard_map/main/pallas_call | solution.py:171
  117.3 0.0 copy-start.1
  117.4 0.0 copy-start.2
  117.4 0.0 all-to-all-done.2
  117.4 0.1 fusion.5
  117.5 0.7 reshape.57
  118.2 13.2 %all-to-all-start.3 = ((bf16[12,11,256]{2,1,0:T(8,128)(2,1)}), bf16[12,11,256]{2,1,0:T(8,128)(2,1)S(1)}, u32[]{:S(2)}, u32[]{:S(2)}) async-start(bf16[12,11,256]{2,1,0:T(8,128)(2,1)} %reshape.57), calls=%async_computation.3 | async-start | bytes 196608 | tf_op jit(solution)/shard_map/reduce_z/all_to_all | solution.py:198
  131.4 0.0 copy-done.1
  131.4 0.0 copy-done.2
  131.4 1.1 reduce_z.1
  132.5 10.6 %all-to-all-done.3 = bf16[12,11,256]{2,1,0:T(8,128)(2,1)S(1)} async-done(((bf16[12,11,256]{2,1,0:T(8,128)(2,1)}), bf16[12,11,256]{2,1,0:T(8,128)(2,1)S(1)}, u32[]{:S(2)}, u32[]{:S(2)}) %all-to-all-start.3) | async-done | bytes 67616 | tf_op jit(solution)/shard_map/reduce_z/all_to_all | solution.py:198
  143.1 0.6 broadcast_multiply_fusion
  (5 shorter events, 0.1 us)
Async XLA Ops:
  10.2 7.0 %copy-start.3 = (bf16[1,4096]{1,0:T(2,128)(2,1)}, bf16[1,4096]{1,0:T(2,128)(2,1)S(1)}, u32[]{:S(2)}) copy-start(bf16[1,4096]{1,0:T(2,128)(2,1)S(1)} %reshape.53.refs_2_.gain) | copy-start | bytes 24580
  10.2 1.6 %copy-start.4 = (bf16[256,4096]{1,0:T(8,128)(2,1)S(1)}, bf16[256,4096]{1,0:T(8,128)(2,1)}, u32[]{:S(2)}) copy-start(bf16[256,4096]{1,0:T(8,128)(2,1)} %tokens.1) | copy-start | bytes 6291460
  11.8 1.0 copy-start.5
  12.8 1.0 copy-start.6
  17.2 0.7 copy-start.7
  17.9 20.5 %collective-permute-start = (bf16[4,8,136,256]{3,2,1,0:T(8,128)(2,1)}, bf16[4,8,136,256]{3,2,1,0:T(8,128)(2,1)}, u32[]{:S(2)}, u32[]{:S(2)}) collective-permute-start(bf16[4,8,136,256]{3,2,1,0:T(8,128)(2,1)} %get-tuple-element.27), channel_id=1, source_target_pairs={{0,1},{1,0},{2,3},{3,2},{4,5},{5,4},{6,7},{7,6},{8,9},{9,8},{10,11... | collective-permute-start | bytes 6684680 | tf_op jit(solution)/shard_map/weight_near/ppermute | solution.py:149
  19.8 39.8 %all-to-all-start = ((bf16[48,11,256]{2,1,0:T(8,128)(2,1)}), bf16[48,11,256]{2,1,0:T(8,128)(2,1)S(1)}, u32[]{:S(2)}, u32[]{:S(2)}) async-start(bf16[48,11,256]{2,1,0:T(8,128)(2,1)} %broadcast_in_dim.10), calls=%async_computation | async-start | bytes 786432 | tf_op jit(solution)/shard_map/weight_far/all_to_all | solution.py:131
  38.4 70.5 %all-gather.3.cloned.1.call-start = ((), (), s32[]{:S(2)}) async-start(), calls=%async_computation.4 | async-start | bytes 4734976 | tf_op jit(solution)/shard_map/weight_near/all_gather | solution.py:153
  60.5 27.9 %all-to-all-start.1 = ((bf16[4,8,136,256]{3,2,1,0:T(8,128)(2,1)}), bf16[4,8,136,256]{3,2,1,0:T(8,128)(2,1)S(1)}, u32[]{:S(2)}, u32[]{:S(2)}) async-start(bf16[4,8,136,256]{3,2,1,0:T(8,128)(2,1)} %add_convert_fusion), calls=%async_computation.1 | async-start | bytes 4456448 | tf_op jit(solution)/shard_map/reduce_x/all_to_all | solution.py:156
  65.3 0.7 copy-start
  89.4 27.9 %all-to-all-start.2 = ((bf16[8,136,256]{2,1,0:T(8,128)(2,1)}), bf16[8,136,256]{2,1,0:T(8,128)(2,1)S(1)}, u32[]{:S(2)}, u32[]{:S(2)}) async-start(bf16[8,136,256]{2,1,0:T(8,128)(2,1)} %fusion), calls=%async_computation.2 | async-start | bytes 1114112 | tf_op jit(solution)/shard_map/reduce_y/all_to_all | solution.py:168
  117.3 14.0 %copy-start.1 = (bf16[544,256]{1,0:T(8,128)(2,1)S(1)}, bf16[544,256]{1,0:T(8,128)(2,1)}, u32[]{:S(2)}) copy-start(bf16[544,256]{1,0:T(8,128)(2,1)} %get-tuple-element.41.grouped) | copy-start | bytes 835588
  117.4 14.0 %copy-start.2 = (s32[528,1]{1,0:T(8,128)S(1)}, s32[528,1]{1,0:T(8,128)}, u32[]{:S(2)}) copy-start(s32[528,1]{1,0:T(8,128)} %constant.17.clone.order) | copy-start | bytes 6340
  118.2 24.9 %all-to-all-start.3 = ((bf16[12,11,256]{2,1,0:T(8,128)(2,1)}), bf16[12,11,256]{2,1,0:T(8,128)(2,1)S(1)}, u32[]{:S(2)}, u32[]{:S(2)}) async-start(bf16[12,11,256]{2,1,0:T(8,128)(2,1)} %reshape.57), calls=%async_computation.3 | async-start | bytes 196608 | tf_op jit(solution)/shard_map/reduce_z/all_to_all | solution.py:198
Sparse Core Ops, SparseCore 0:
  60.6 48.2 all-gather.2

commit v8 on v5

--- a/solution.py
+++ b/solution.py
@@ -122,9 +122,10 @@
     with jax.named_scope("weight_far"):
         scale = jnp.repeat(scales.astype(jnp.float32), width // scales.shape[1], axis=1)
         own = (codes.astype(jnp.float32) * scale).astype(jnp.bfloat16)
-        spread = jnp.broadcast_to(own[None], (n_x * n_z, rows, width))
+        spread = jnp.broadcast_to(own[None], (n_z, rows, width))
         spread, tokens_after = together(spread, tokens)
-        spread = lax.all_to_all(spread, ("x", "z"), split_axis=0, concat_axis=0, tiled=True)
+        spread = lax.all_to_all(spread, "z", split_axis=0, concat_axis=0, tiled=True)
+
     with jax.named_scope("term"):
         near = jax.ShapeDtypeStruct((n_x, 2 * n_y, group, width), jnp.bfloat16)
         mine, theirs, cot_grouped, inv = pl.pallas_call(
@@ -141,16 +142,19 @@
             cost_estimate=pl.CostEstimate(flops=3 * toks * outw * feats, bytes_accessed=4 * toks * feats, transcendentals=0),
         )(place, tokens_after, gain_row, cot_t, jnp.asarray(grouped))
         cot_grouped = cot_grouped.reshape(4 * group, toks)
-    with jax.named_scope("weight_near"):
+    with jax.named_scope("weight_x"):
         spread, theirs = together(spread, theirs)
-        slab = jnp.pad(spread.reshape(n_x, n_z * rows, width), ((0, 0), (0, group - n_z * rows), (0, 0)))
-        w = lax.all_gather(slab, ("y_hi", "y_lo", "core"), axis=0, tiled=False).reshape(n_y, 2, 2, n_x, group, width)
+        strip = jnp.pad(spread.reshape(n_z * rows, width), ((0, group - n_z * rows), (0, 0)))
+        slab = jnp.broadcast_to(strip[None], (n_x, group, width))
+        slab = lax.all_to_all(slab, "x", split_axis=0, concat_axis=0, tiled=True)
     with jax.named_scope("reduce_core"):
-        theirs, _ = together(theirs, slab)
         came = lax.ppermute(theirs, "core", ((0, 1), (1, 0)))
         pair = (mine.astype(jnp.float32) + came.astype(jnp.float32)).astype(jnp.bfloat16)
+    with jax.named_scope("weight_near"):
+        slab, pair = together(slab, pair)
+        w = lax.all_gather(slab, ("y_hi", "y_lo", "core"), axis=0, tiled=False).reshape(n_y, 2, 2, n_x, group, width)
     with jax.named_scope("reduce_x"):
-        pair, cot_after, _ = together(pair, cot_grouped, slab)
+        cot_after, _ = together(cot_grouped, slab)
         parts = lax.all_to_all(pair, "x", split_axis=0, concat_axis=0, tiled=True)
         cot = pl.pallas_call(
             prep_kernel,

time: 140 us -> 136 us (0.971)
  waiting for transfers between devices: 60.8 us -> 48.3 us
  starting transfers between devices: 36.6 us -> 43 us
  other arithmetic: 5.5 us -> 7.15 us
    all_to_all x1 -> x2, waiting for transfers between devices: 12.1 us -> 5.43 us  [the longest x1 3.55 us: per_device(): lax.all_to_all(spread, 'z', split_axis=0, concat_axis=0, tiled=True)]
    ppermute x1, waiting for transfers between devices: 4.52 us -> 0.01 us  [per_device(): came = lax.ppermute(theirs, 'core', ((0, 1), (1, 0)))]
    all_to_all x1, starting transfers between devices: 4.28 us -> 8.41 us  [per_device(): last = lax.all_to_all(part, 'z', split_axis=0, concat_axis=0, tiled=True)]
    convert_element_type x1, other arithmetic: 1.93 us -> 3.56 us  [per_device(): (mine.astype(jnp.float32) + came.astype(jnp.float32)).astype(jnp.bfloat16)]
    all_to_all x1 -> x2, starting transfers between devices: 18.5 us -> 19.9 us  [the longest x1 15.2 us: per_device(): lax.all_to_all(spread, 'z', split_axis=0, concat_axis=0, tiled=True)]
    unnamed x18 -> x20, local copies, waits for them, and re-layouts: 6.29 us -> 6.97 us
  transfers between devices with their start and end apart: 6 -> 7, of which waited for: 5 -> 5; matrix products, arithmetic and copies ran while one was open for 4% -> 6% of each run, Pallas kernels for 8% -> 8%
where the time goes in v8:
time: 136 us; the launch traced here: 134 us
  waiting for transfers between devices  48.3 us (36%)
  starting transfers between devices  43 us (32%)
  between operations  14.2 us (10%)
  Pallas kernels  11.1 us (8%)
  local copies, waits for them, and re-layouts  10.6 us (8%)
  other arithmetic  7.15 us (5%)
    all_to_all x1, waiting for transfers between devices, per_device(): parts = lax.all_to_all(pair, 'x', split_axis=0, concat_axis=0, tiled=True)  24.6 us
    all_to_all x1, waiting for transfers between devices, per_device(): lax.all_to_all(part, ('y_hi', 'y_lo'), split_axis=0, concat_axis=0, tiled...  15.4 us
    all_to_all x1, starting transfers between devices, per_device(): lax.all_to_all(spread, 'z', split_axis=0, concat_axis=0, tiled=True)  15.2 us
    pallas_call x1, Pallas kernels, per_device(): pl.pallas_call(main_kernel, grid=(n_y,), out_shape=(jax.ShapeDtypeStruct(...  8.84 us
    all_to_all x1, starting transfers between devices, per_device(): last = lax.all_to_all(part, 'z', split_axis=0, concat_axis=0, tiled=True)  8.41 us
    all_to_all x1, starting transfers between devices, per_device(): lax.all_to_all(part, ('y_hi', 'y_lo'), split_axis=0, concat_axis=0, tiled...  7.1 us
    unnamed x20, local copies, waits for them, and re-layouts  6.97 us
    all_to_all x1, starting transfers between devices, per_device(): parts = lax.all_to_all(pair, 'x', split_axis=0, concat_axis=0, tiled=True)  5.67 us
  transfers between devices with their start and end apart: 7, of which 5 were waited for; matrix products, arithmetic and copies ran while one was open for 6% of the time, Pallas kernels for 8%

profile of v8, /device:TPU:6, one launch (start us, length us, event | category | flops | bytes accessed | tf_op | source)
XLA Modules:
  0.0 134.3 jit_solution(5161247217453832997)
XLA Ops:
  7.2 0.8 copy.12
  7.9 0.1 broadcast_in_dim.23
  8.0 0.7 multiply_convert_fusion
  8.7 0.6 broadcast_in_dim.24
  9.4 15.2 %all-to-all-start = ((bf16[12,11,256]{2,1,0:T(8,128)(2,1)}), bf16[12,11,256]{2,1,0:T(8,128)(2,1)S(1)}, u32[]{:S(2)}, u32[]{:S(2)}) async-start(bf16[12,11,256]{2,1,0:T(8,128)(2,1)} %broadcast_in_dim.24), calls=%async_computation | async-start | bytes 196608 | tf_op jit(solution)/shard_map/weight_far/all_to_all | solution.py:127
  24.5 0.7 reshape.54.refs_2_.gain
  25.3 0.0 copy-start.1
  25.3 0.0 copy-start.3
  25.3 1.6 %copy-done.3 = bf16[256,4096]{1,0:T(8,128)(2,1)S(1)} copy-done((bf16[256,4096]{1,0:T(8,128)(2,1)S(1)}, bf16[256,4096]{1,0:T(8,128)(2,1)}, u32[]{:S(2)}) %copy-start.3) | copy-done | bytes 2097176
  26.9 0.0 copy-start.4
  26.9 1.0 copy-done.4
  27.8 0.0 copy-start.5
  27.8 1.0 copy-done.5
  28.8 2.1 %term.1 = (bf16[4,8,136,256]{3,2,1,0:T(8,128)(2,1)S(1)}, bf16[4,8,136,256]{3,2,1,0:T(8,128)(2,1)S(1)}, bf16[2,272,256]{2,1,0:T(8,128)(2,1)S(1)}, f32[256,128]{1,0:T(8,128)S(1)}) custom-call(s32[1]{0:T(128)} %bitcast.refs_0_, bf16[256,4096]{1,0:T(8,128)(2,1)S(1)} %copy-done.3, bf16[1,4096]{1,0:T(2,128)(2,1)S(1)} %reshape.54.refs_2_.gain, ...), custom_call_target="tpu_custom_call" | custom-call | flops 1660944384 | bytes 4194304 | tf_op jit(solution)/shard_map/term/pallas_call | solution.py:131
  30.9 0.0 copy-done.1
  30.9 0.0 copy-start.2
  30.9 1.4 %copy-done.2 = bf16[4,8,136,256]{3,2,1,0:T(8,128)(2,1)} copy-done((bf16[4,8,136,256]{3,2,1,0:T(8,128)(2,1)}, bf16[4,8,136,256]{3,2,1,0:T(8,128)(2,1)S(1)}, u32[]{:S(2)}) %copy-start.2) | copy-done | bytes 2228248
  32.3 0.0 copy-start.6
  32.3 0.7 copy-done.6
  32.9 3.6 %all-to-all-done = bf16[12,11,256]{2,1,0:T(8,128)(2,1)S(1)} async-done(((bf16[12,11,256]{2,1,0:T(8,128)(2,1)}), bf16[12,11,256]{2,1,0:T(8,128)(2,1)S(1)}, u32[]{:S(2)}, u32[]{:S(2)}) %all-to-all-start) | async-done | bytes 67616 | tf_op jit(solution)/shard_map/weight_far/all_to_all | solution.py:127
  36.5 1.9 %collective-permute-start = (bf16[4,8,136,256]{3,2,1,0:T(8,128)(2,1)}, bf16[4,8,136,256]{3,2,1,0:T(8,128)(2,1)}, u32[]{:S(2)}, u32[]{:S(2)}) collective-permute-start(bf16[4,8,136,256]{3,2,1,0:T(8,128)(2,1)} %copy-done.2), channel_id=1, source_target_pairs={{0,1},{1,0},{2,3},{3,2},{4,5},{5,4},{6,7},{7,6},{8,9},{9,8},{10,11... | collective-permute-start | bytes 6684680 | tf_op jit(solution)/shard_map/reduce_core/ppermute | solution.py:151
  38.5 0.7 broadcast_in_dim.25
  39.2 4.8 %all-to-all-start.1 = ((bf16[4,136,256]{2,1,0:T(8,128)(2,1)}), bf16[4,136,256]{2,1,0:T(8,128)(2,1)S(1)}, u32[]{:S(2)}, u32[]{:S(2)}) async-start(bf16[4,136,256]{2,1,0:T(8,128)(2,1)} %broadcast_in_dim.25), calls=%async_computation.1 | async-start | bytes 557056 | tf_op jit(solution)/shard_map/weight_x/all_to_all | solution.py:149
  44.0 0.0 all-gather.3.cloned.1.call-start
  44.0 0.0 collective-permute-done
  44.0 3.6 %add_convert_fusion = bf16[4,8,136,256]{3,2,1,0:T(8,128)(2,1)} fusion(bf16[4,8,136,256]{3,2,1,0:T(8,128)(2,1)} %collective-permute-done, bf16[4,8,136,256]{3,2,1,0:T(8,128)(2,1)S(1)} %get-tuple-element.30), kind=kLoop, calls=%fused_computation | loop fusion | flops 4456448 | bytes 6684672 | tf_op jit(solution)/shard_map/reduce_core/convert_element_type | solution.py:152
  47.5 1.9 %all-to-all-done.1 = bf16[4,136,256]{2,1,0:T(8,128)(2,1)S(1)} async-done(((bf16[4,136,256]{2,1,0:T(8,128)(2,1)}), bf16[4,136,256]{2,1,0:T(8,128)(2,1)S(1)}, u32[]{:S(2)}, u32[]{:S(2)}) %all-to-all-start.1) | async-done | bytes 278560 | tf_op jit(solution)/shard_map/weight_x/all_to_all | solution.py:149
  49.4 0.0 copy-start.7
  49.4 0.7 copy-done.7
  50.1 0.0 all-gather.3.cloned.1.call-update
  50.1 5.7 %all-to-all-start.2 = ((bf16[4,8,136,256]{3,2,1,0:T(8,128)(2,1)}), bf16[4,8,136,256]{3,2,1,0:T(8,128)(2,1)S(1)}, u32[]{:S(2)}, u32[]{:S(2)}) async-start(bf16[4,8,136,256]{3,2,1,0:T(8,128)(2,1)} %add_convert_fusion), calls=%async_computation.2 | async-start | bytes 4456448 | tf_op jit(solution)/shard_map/reduce_x/all_to_all | solution.py:158
  55.8 0.1 reduce_x.1.cot
  56.0 0.0 copy-start
  56.0 0.7 copy-done
  56.7 0.0 copy-start.8
  56.7 24.6 %all-to-all-done.2 = bf16[4,8,136,256]{3,2,1,0:T(8,128)(2,1)S(1)} async-done(((bf16[4,8,136,256]{3,2,1,0:T(8,128)(2,1)}), bf16[4,8,136,256]{3,2,1,0:T(8,128)(2,1)S(1)}, u32[]{:S(2)}, u32[]{:S(2)}) %all-to-all-start.2) | async-done | bytes 2228256 | tf_op jit(solution)/shard_map/reduce_x/all_to_all | solution.py:158
  81.3 1.1 fusion
  82.4 7.1 %all-to-all-start.3 = ((bf16[8,136,256]{2,1,0:T(8,128)(2,1)}), bf16[8,136,256]{2,1,0:T(8,128)(2,1)S(1)}, u32[]{:S(2)}, u32[]{:S(2)}) async-start(bf16[8,136,256]{2,1,0:T(8,128)(2,1)} %fusion), calls=%async_computation.3 | async-start | bytes 1114112 | tf_op jit(solution)/shard_map/reduce_y/all_to_all | solution.py:170
  89.5 0.0 copy-done.8
  89.5 1.0 select_convert_fusion.back
  90.6 15.4 %all-to-all-done.3 = bf16[8,136,256]{2,1,0:T(8,128)(2,1)S(1)} async-done(((bf16[8,136,256]{2,1,0:T(8,128)(2,1)}), bf16[8,136,256]{2,1,0:T(8,128)(2,1)S(1)}, u32[]{:S(2)}, u32[]{:S(2)}) %all-to-all-start.3) | async-done | bytes 557088 | tf_op jit(solution)/shard_map/reduce_y/all_to_all | solution.py:170
  106.1 0.1 fusion.5
  106.1 0.7 reshape.57
  106.8 8.4 %all-to-all-start.4 = ((bf16[12,11,256]{2,1,0:T(8,128)(2,1)}), bf16[12,11,256]{2,1,0:T(8,128)(2,1)S(1)}, u32[]{:S(2)}, u32[]{:S(2)}) async-start(bf16[12,11,256]{2,1,0:T(8,128)(2,1)} %reshape.57), calls=%async_computation.4 | async-start | bytes 196608 | tf_op jit(solution)/shard_map/reduce_z/all_to_all | solution.py:176
  115.2 0.0 all-gather.3.cloned.1.call-done
  115.3 8.8 %main.1 = (bf16[528,256]{1,0:T(8,128)(2,1)}, bf16[256,4096]{1,0:T(8,128)(2,1)}) custom-call(bf16[256,4096]{1,0:T(8,128)(2,1)} %tokens.1, bf16[1,4096]{1,0:T(2,128)(2,1)} %copy-done.1, bf16[256,544]{1,0:T(8,128)(2,1)} %copy-done, f32[256,128]{1,0:T(8,128)} %copy-done.6, bf16[528,544]{1,0:T(8,128)(2,1)} %select_convert_fusion.back, ...), custom_call_target="tpu_custom_call" | custom-call | flops 2768240640 | bytes 10485760 | tf_op jit(solution)/shard_map/main/pallas_call | solution.py:179
  124.1 2.8 %all-to-all-done.4 = bf16[12,11,256]{2,1,0:T(8,128)(2,1)S(1)} async-done(((bf16[12,11,256]{2,1,0:T(8,128)(2,1)}), bf16[12,11,256]{2,1,0:T(8,128)(2,1)S(1)}, u32[]{:S(2)}, u32[]{:S(2)}) %all-to-all-start.4) | async-done | bytes 67616 | tf_op jit(solution)/shard_map/reduce_z/all_to_all | solution.py:176
  126.9 0.6 broadcast_multiply_fusion
  (8 shorter events, 0.2 us)
Async XLA Ops:
  9.4 27.1 %all-to-all-start = ((bf16[12,11,256]{2,1,0:T(8,128)(2,1)}), bf16[12,11,256]{2,1,0:T(8,128)(2,1)S(1)}, u32[]{:S(2)}, u32[]{:S(2)}) async-start(bf16[12,11,256]{2,1,0:T(8,128)(2,1)} %broadcast_in_dim.24), calls=%async_computation | async-start | bytes 196608 | tf_op jit(solution)/shard_map/weight_far/all_to_all | solution.py:127
  25.3 5.6 %copy-start.1 = (bf16[1,4096]{1,0:T(2,128)(2,1)}, bf16[1,4096]{1,0:T(2,128)(2,1)S(1)}, u32[]{:S(2)}) copy-start(bf16[1,4096]{1,0:T(2,128)(2,1)S(1)} %reshape.54.refs_2_.gain) | copy-start | bytes 24580
  25.3 1.6 %copy-start.3 = (bf16[256,4096]{1,0:T(8,128)(2,1)S(1)}, bf16[256,4096]{1,0:T(8,128)(2,1)}, u32[]{:S(2)}) copy-start(bf16[256,4096]{1,0:T(8,128)(2,1)} %tokens.1) | copy-start | bytes 6291460
  26.9 1.0 copy-start.4
  27.8 1.0 copy-start.5
  30.9 1.4 %copy-start.2 = (bf16[4,8,136,256]{3,2,1,0:T(8,128)(2,1)}, bf16[4,8,136,256]{3,2,1,0:T(8,128)(2,1)S(1)}, u32[]{:S(2)}) copy-start(bf16[4,8,136,256]{3,2,1,0:T(8,128)(2,1)S(1)} %get-tuple-element.31) | copy-start | bytes 6684676
  32.3 0.7 copy-start.6
  36.5 7.5 %collective-permute-start = (bf16[4,8,136,256]{3,2,1,0:T(8,128)(2,1)}, bf16[4,8,136,256]{3,2,1,0:T(8,128)(2,1)}, u32[]{:S(2)}, u32[]{:S(2)}) collective-permute-start(bf16[4,8,136,256]{3,2,1,0:T(8,128)(2,1)} %copy-done.2), channel_id=1, source_target_pairs={{0,1},{1,0},{2,3},{3,2},{4,5},{5,4},{6,7},{7,6},{8,9},{9,8},{10,11... | collective-permute-start | bytes 6684680 | tf_op jit(solution)/shard_map/reduce_core/ppermute | solution.py:151
  39.2 10.2 %all-to-all-start.1 = ((bf16[4,136,256]{2,1,0:T(8,128)(2,1)}), bf16[4,136,256]{2,1,0:T(8,128)(2,1)S(1)}, u32[]{:S(2)}, u32[]{:S(2)}) async-start(bf16[4,136,256]{2,1,0:T(8,128)(2,1)} %broadcast_in_dim.25), calls=%async_computation.1 | async-start | bytes 557056 | tf_op jit(solution)/shard_map/weight_x/all_to_all | solution.py:149
  44.0 71.3 %all-gather.3.cloned.1.call-start = ((), (), s32[]{:S(2)}) async-start(), calls=%async_computation.5 | async-start | bytes 4734976 | tf_op jit(solution)/shard_map/weight_near/all_gather | solution.py:155
  49.4 0.7 copy-start.7
  50.1 31.2 %all-to-all-start.2 = ((bf16[4,8,136,256]{3,2,1,0:T(8,128)(2,1)}), bf16[4,8,136,256]{3,2,1,0:T(8,128)(2,1)S(1)}, u32[]{:S(2)}, u32[]{:S(2)}) async-start(bf16[4,8,136,256]{3,2,1,0:T(8,128)(2,1)} %add_convert_fusion), calls=%async_computation.2 | async-start | bytes 4456448 | tf_op jit(solution)/shard_map/reduce_x/all_to_all | solution.py:158
  56.0 0.7 copy-start
  56.7 32.8 %copy-start.8 = (s32[528,1]{0,1:T(1,128)S(1)}, s32[528,1]{0,1:T(1,128)}, u32[]{:S(2)}) copy-start(s32[528,1]{0,1:T(1,128)} %constant.19.clone) | copy-start | bytes 6340
  82.4 23.6 %all-to-all-start.3 = ((bf16[8,136,256]{2,1,0:T(8,128)(2,1)}), bf16[8,136,256]{2,1,0:T(8,128)(2,1)S(1)}, u32[]{:S(2)}, u32[]{:S(2)}) async-start(bf16[8,136,256]{2,1,0:T(8,128)(2,1)} %fusion), calls=%async_computation.3 | async-start | bytes 1114112 | tf_op jit(solution)/shard_map/reduce_y/all_to_all | solution.py:170
  106.8 20.0 %all-to-all-start.4 = ((bf16[12,11,256]{2,1,0:T(8,128)(2,1)}), bf16[12,11,256]{2,1,0:T(8,128)(2,1)S(1)}, u32[]{:S(2)}, u32[]{:S(2)}) async-start(bf16[12,11,256]{2,1,0:T(8,128)(2,1)} %reshape.57), calls=%async_computation.4 | async-start | bytes 196608 | tf_op jit(solution)/shard_map/reduce_z/all_to_all | solution.py:176
Sparse Core Ops, SparseCore 0:
  50.3 48.3 all-gather.2

commit v9 on v8

--- a/solution.py
+++ b/solution.py
@@ -39,6 +39,16 @@
 
 def dot(a, b, ca, cb):
     return lax.dot_general(a, b, (((ca,), (cb,)), ((), ())), preferred_element_type=jnp.float32)
+
+
+def dequantize_kernel(codes, scales, copies):
+    n_blocks, width = scales.shape[0], codes.shape[1]
+    rows = lax.broadcasted_iota(jnp.int32, (n_blocks, width), 0)
+    lanes = lax.broadcasted_iota(jnp.int32, (n_blocks, width), 1) // (width // n_blocks)
+    spread = jnp.where(rows == lanes, 1.0, 0.0).astype(jnp.bfloat16)
+    weight = codes[...].astype(jnp.float32) * dot(scales[...], spread, 0, 0)
+    for z in range(copies.shape[0]):
+        copies[z] = weight.astype(jnp.bfloat16)
 
 
 def term_kernel(n_x, place, tokens, gain, cot, order, mine, theirs, cot_grouped, inv):
@@ -67,9 +77,9 @@
     cot[...] = cot_grouped[...].T
 
 
-def main_kernel(tokens, gain, cot, inv, back, w, keys, grad, keys_acc, gh, dots):
+def main_kernel(tokens, gain, cot, inv, back, w, keys, grad, keys_acc, gh, dots, held):
     i = pl.program_id(0)
-    toks, feats = tokens.shape
+    feats = grad.shape[1]
     n_x = w.shape[3]
     r = inv[:, :1]
 
@@ -80,7 +90,8 @@
 
     for x in range(n_x):
         at = pl.ds(pl.multiple_of((i * n_x + x) * COL, COL), COL)
-        v = tokens[:, at].astype(jnp.float32)
+        held[:, at] = tokens[:, x * COL : (x + 1) * COL]
+        v = tokens[:, x * COL : (x + 1) * COL].astype(jnp.float32)
         g = gain[:, at].astype(jnp.float32)
         hid = (v * r * g).astype(jnp.bfloat16)
         weight = jnp.concatenate([w[0, y, c, x] for c in range(2) for y in range(2)], axis=0)
@@ -94,7 +105,7 @@
         keys[...] = dot(back[...], keys_acc[...].astype(jnp.bfloat16), 1, 0).astype(jnp.bfloat16)
         k = r * r * r * (jnp.sum(dots[...], axis=1, keepdims=True) / feats)
         for f in range(0, feats, COL):
-            v = tokens[:, f : f + COL].astype(jnp.float32)
+            v = held[:, f : f + COL].astype(jnp.float32)
             grad[:, f : f + COL] = (r * gh[:, f : f + COL] - v * k).astype(jnp.bfloat16)
 
 
@@ -120,10 +131,14 @@
     cot_t = cotangent.T
 
     with jax.named_scope("weight_far"):
-        scale = jnp.repeat(scales.astype(jnp.float32), width // scales.shape[1], axis=1)
-        own = (codes.astype(jnp.float32) * scale).astype(jnp.bfloat16)
-        spread = jnp.broadcast_to(own[None], (n_z, rows, width))
-        spread, tokens_after = together(spread, tokens)
+        spread = pl.pallas_call(
+            dequantize_kernel,
+            out_shape=jax.ShapeDtypeStruct((n_z, rows, width), jnp.bfloat16),
+            in_specs=[VMEM] * 2,
+            out_specs=VMEM,
+            compiler_params=params(8),
+        )(codes, scales.T)
+        spread, place = together(spread, place)
         spread = lax.all_to_all(spread, "z", split_axis=0, concat_axis=0, tiled=True)
 
     with jax.named_scope("term"):
@@ -140,7 +155,7 @@
             out_specs=(VMEM,) * 4,
             compiler_params=params(20),
             cost_estimate=pl.CostEstimate(flops=3 * toks * outw * feats, bytes_accessed=4 * toks * feats, transcendentals=0),
-        )(place, tokens_after, gain_row, cot_t, jnp.asarray(grouped))
+        )(place, tokens, gain_row, cot_t, jnp.asarray(grouped))
         cot_grouped = cot_grouped.reshape(4 * group, toks)
     with jax.named_scope("weight_x"):
         spread, theirs = together(spread, theirs)
@@ -184,7 +199,7 @@
                 jax.ShapeDtypeStruct((toks, feats), jnp.bfloat16),
             ),
             in_specs=[
-                whole(toks, feats),
+                pl.BlockSpec((toks, n_x * width), lambda i: (0, i)),
                 whole(1, feats),
                 whole(toks, 4 * group),
                 whole(toks, LANE),
@@ -196,6 +211,7 @@
                 pltpu.VMEM((4 * group, toks), jnp.float32),
                 pltpu.VMEM((toks, feats), jnp.float32),
                 pltpu.VMEM((toks, COL), jnp.float32),
+                pltpu.VMEM((toks, feats), jnp.bfloat16),
             ],
             compiler_params=params(60),
             cost_estimate=pl.CostEstimate(flops=5 * toks * outw * feats, bytes_accessed=10 * toks * feats, transcendentals=0),

time: 136 us -> 136 us (level)
    unnamed x20 -> x22, local copies, waits for them, and re-layouts: 6.97 us -> 8.32 us
where the time goes in v9:
time: 136 us; the launch traced here: 134 us
  waiting for transfers between devices  48.4 us (36%)
  starting transfers between devices  43 us (32%)
  between operations  14.2 us (10%)
  Pallas kernels  11.8 us (9%)
  local copies, waits for them, and re-layouts  10.5 us (8%)
  other arithmetic  6.43 us (5%)
    all_to_all x1, waiting for transfers between devices, per_device(): parts = lax.all_to_all(pair, 'x', split_axis=0, concat_axis=0, tiled=True)  24.6 us
    all_to_all x1, waiting for transfers between devices, per_device(): lax.all_to_all(part, ('y_hi', 'y_lo'), split_axis=0, concat_axis=0, tiled...  15.4 us
    all_to_all x1, starting transfers between devices, per_device(): lax.all_to_all(spread, 'z', split_axis=0, concat_axis=0, tiled=True)  15.2 us
    pallas_call x1, Pallas kernels, per_device(): pl.pallas_call(main_kernel, grid=(n_y,), out_shape=(jax.ShapeDtypeStruct(...  8.72 us
    all_to_all x1, starting transfers between devices, per_device(): last = lax.all_to_all(part, 'z', split_axis=0, concat_axis=0, tiled=True)  8.41 us
    unnamed x22, local copies, waits for them, and re-layouts  8.32 us
    all_to_all x1, starting transfers between devices, per_device(): lax.all_to_all(part, ('y_hi', 'y_lo'), split_axis=0, concat_axis=0, tiled...  7.1 us
    all_to_all x1, starting transfers between devices, per_device(): parts = lax.all_to_all(pair, 'x', split_axis=0, concat_axis=0, tiled=True)  5.67 us
  transfers between devices with their start and end apart: 7, of which 5 were waited for; matrix products, arithmetic and copies ran while one was open for 6% of the time, Pallas kernels for 8%

profile of v9, /device:TPU:6, one launch (start us, length us, event | category | flops | bytes accessed | tf_op | source)
XLA Modules:
  0.0 134.3 jit_solution(3064992631334015975)
XLA Ops:
  7.2 0.0 copy-start.2
  7.2 0.7 copy-done.2
  7.9 0.0 copy-start.3
  7.9 0.7 copy-done.3
  8.5 0.8 weight_far.1
  9.3 15.2 %all-to-all-start = ((bf16[12,11,256]{2,1,0:T(8,128)(2,1)}), bf16[12,11,256]{2,1,0:T(8,128)(2,1)S(1)}, u32[]{:S(2)}, u32[]{:S(2)}) async-start(bf16[12,11,256]{2,1,0:T(8,128)(2,1)} %weight_far.1), calls=%async_computation | async-start | bytes 196608 | tf_op jit(solution)/shard_map/weight_far/all_to_all | solution.py:142
  24.5 0.7 reshape.49.refs_2_.gain
  25.2 0.0 copy-start.1
  25.2 0.0 copy-start.5
  25.2 1.6 %copy-done.5 = bf16[256,4096]{1,0:T(8,128)(2,1)S(1)} copy-done((bf16[256,4096]{1,0:T(8,128)(2,1)S(1)}, bf16[256,4096]{1,0:T(8,128)(2,1)}, u32[]{:S(2)}) %copy-start.5) | copy-done | bytes 2097176
  26.8 0.0 copy-start.6
  26.8 1.0 copy-done.6
  27.8 0.0 copy-start.7
  27.8 1.0 copy-done.7
  28.7 2.1 %term.1 = (bf16[4,8,136,256]{3,2,1,0:T(8,128)(2,1)S(1)}, bf16[4,8,136,256]{3,2,1,0:T(8,128)(2,1)S(1)}, bf16[2,272,256]{2,1,0:T(8,128)(2,1)S(1)}, f32[256,128]{1,0:T(8,128)S(1)}) custom-call(s32[1]{0:T(128)} %bitcast.1.refs_0_, bf16[256,4096]{1,0:T(8,128)(2,1)S(1)} %copy-done.5, bf16[1,4096]{1,0:T(2,128)(2,1)S(1)} %reshape.49.refs_2_.gain, ...), custom_call_target="tpu_custom_call" | custom-call | flops 1660944384 | bytes 4194304 | tf_op jit(solution)/shard_map/term/pallas_call | solution.py:146
  30.9 0.0 copy-done.1
  30.9 0.0 copy-start.4
  30.9 1.4 %copy-done.4 = bf16[4,8,136,256]{3,2,1,0:T(8,128)(2,1)} copy-done((bf16[4,8,136,256]{3,2,1,0:T(8,128)(2,1)}, bf16[4,8,136,256]{3,2,1,0:T(8,128)(2,1)S(1)}, u32[]{:S(2)}) %copy-start.4) | copy-done | bytes 2228248
  32.3 0.0 copy-start.8
  32.3 0.7 copy-done.8
  32.9 3.5 %all-to-all-done = bf16[12,11,256]{2,1,0:T(8,128)(2,1)S(1)} async-done(((bf16[12,11,256]{2,1,0:T(8,128)(2,1)}), bf16[12,11,256]{2,1,0:T(8,128)(2,1)S(1)}, u32[]{:S(2)}, u32[]{:S(2)}) %all-to-all-start) | async-done | bytes 67616 | tf_op jit(solution)/shard_map/weight_far/all_to_all | solution.py:142
  36.5 1.9 %collective-permute-start = (bf16[4,8,136,256]{3,2,1,0:T(8,128)(2,1)}, bf16[4,8,136,256]{3,2,1,0:T(8,128)(2,1)}, u32[]{:S(2)}, u32[]{:S(2)}) collective-permute-start(bf16[4,8,136,256]{3,2,1,0:T(8,128)(2,1)} %copy-done.4), channel_id=1, source_target_pairs={{0,1},{1,0},{2,3},{3,2},{4,5},{5,4},{6,7},{7,6},{8,9},{9,8},{10,11... | collective-permute-start | bytes 6684680 | tf_op jit(solution)/shard_map/reduce_core/ppermute | solution.py:166
  38.4 0.7 broadcast_in_dim.14
  39.2 4.8 %all-to-all-start.1 = ((bf16[4,136,256]{2,1,0:T(8,128)(2,1)}), bf16[4,136,256]{2,1,0:T(8,128)(2,1)S(1)}, u32[]{:S(2)}, u32[]{:S(2)}) async-start(bf16[4,136,256]{2,1,0:T(8,128)(2,1)} %broadcast_in_dim.14), calls=%async_computation.1 | async-start | bytes 557056 | tf_op jit(solution)/shard_map/weight_x/all_to_all | solution.py:164
  43.9 0.0 all-gather.3.cloned.1.call-start
  43.9 0.0 collective-permute-done
  44.0 3.5 %add_convert_fusion = bf16[4,8,136,256]{3,2,1,0:T(8,128)(2,1)} fusion(bf16[4,8,136,256]{3,2,1,0:T(8,128)(2,1)} %collective-permute-done, bf16[4,8,136,256]{3,2,1,0:T(8,128)(2,1)S(1)} %get-tuple-element.30), kind=kLoop, calls=%fused_computation | loop fusion | flops 4456448 | bytes 6684672 | tf_op jit(solution)/shard_map/reduce_core/convert_element_type | solution.py:167
  47.5 1.9 %all-to-all-done.1 = bf16[4,136,256]{2,1,0:T(8,128)(2,1)S(1)} async-done(((bf16[4,136,256]{2,1,0:T(8,128)(2,1)}), bf16[4,136,256]{2,1,0:T(8,128)(2,1)S(1)}, u32[]{:S(2)}, u32[]{:S(2)}) %all-to-all-start.1) | async-done | bytes 278560 | tf_op jit(solution)/shard_map/weight_x/all_to_all | solution.py:164
  49.4 0.0 copy-start.9
  49.4 0.7 copy-done.9
  50.1 0.0 all-gather.3.cloned.1.call-update
  50.1 5.7 %all-to-all-start.2 = ((bf16[4,8,136,256]{3,2,1,0:T(8,128)(2,1)}), bf16[4,8,136,256]{3,2,1,0:T(8,128)(2,1)S(1)}, u32[]{:S(2)}, u32[]{:S(2)}) async-start(bf16[4,8,136,256]{3,2,1,0:T(8,128)(2,1)} %add_convert_fusion), calls=%async_computation.2 | async-start | bytes 4456448 | tf_op jit(solution)/shard_map/reduce_x/all_to_all | solution.py:173
  55.8 0.1 reduce_x.1.cot
  55.9 0.0 copy-start
  55.9 0.7 copy-done
  56.7 0.0 copy-start.10
  56.7 24.6 %all-to-all-done.2 = bf16[4,8,136,256]{3,2,1,0:T(8,128)(2,1)S(1)} async-done(((bf16[4,8,136,256]{3,2,1,0:T(8,128)(2,1)}), bf16[4,8,136,256]{3,2,1,0:T(8,128)(2,1)S(1)}, u32[]{:S(2)}, u32[]{:S(2)}) %all-to-all-start.2) | async-done | bytes 2228256 | tf_op jit(solution)/shard_map/reduce_x/all_to_all | solution.py:173
  81.3 1.1 fusion
  82.4 7.1 %all-to-all-start.3 = ((bf16[8,136,256]{2,1,0:T(8,128)(2,1)}), bf16[8,136,256]{2,1,0:T(8,128)(2,1)S(1)}, u32[]{:S(2)}, u32[]{:S(2)}) async-start(bf16[8,136,256]{2,1,0:T(8,128)(2,1)} %fusion), calls=%async_computation.3 | async-start | bytes 1114112 | tf_op jit(solution)/shard_map/reduce_y/all_to_all | solution.py:185
  89.5 0.0 copy-done.10
  89.5 1.0 select_convert_fusion.back
  90.5 15.4 %all-to-all-done.3 = bf16[8,136,256]{2,1,0:T(8,128)(2,1)S(1)} async-done(((bf16[8,136,256]{2,1,0:T(8,128)(2,1)}), bf16[8,136,256]{2,1,0:T(8,128)(2,1)S(1)}, u32[]{:S(2)}, u32[]{:S(2)}) %all-to-all-start.3) | async-done | bytes 557088 | tf_op jit(solution)/shard_map/reduce_y/all_to_all | solution.py:185
  106.1 0.1 fusion.5
  106.1 0.7 reshape.52
  106.8 8.4 %all-to-all-start.4 = ((bf16[12,11,256]{2,1,0:T(8,128)(2,1)}), bf16[12,11,256]{2,1,0:T(8,128)(2,1)S(1)}, u32[]{:S(2)}, u32[]{:S(2)}) async-start(bf16[12,11,256]{2,1,0:T(8,128)(2,1)} %reshape.52), calls=%async_computation.4 | async-start | bytes 196608 | tf_op jit(solution)/shard_map/reduce_z/all_to_all | solution.py:191
  115.2 0.0 all-gather.3.cloned.1.call-done
  115.3 8.7 %main.1 = (bf16[528,256]{1,0:T(8,128)(2,1)}, bf16[256,4096]{1,0:T(8,128)(2,1)}) custom-call(bf16[256,4096]{1,0:T(8,128)(2,1)} %tokens.1, bf16[1,4096]{1,0:T(2,128)(2,1)} %copy-done.1, bf16[256,544]{1,0:T(8,128)(2,1)} %copy-done, f32[256,128]{1,0:T(8,128)} %copy-done.8, bf16[528,544]{1,0:T(8,128)(2,1)} %select_convert_fusion.back, ...), custom_call_target="tpu_custom_call" | custom-call | flops 2768240640 | bytes 10485760 | tf_op jit(solution)/shard_map/main/pallas_call | solution.py:194
  124.0 2.9 %all-to-all-done.4 = bf16[12,11,256]{2,1,0:T(8,128)(2,1)S(1)} async-done(((bf16[12,11,256]{2,1,0:T(8,128)(2,1)}), bf16[12,11,256]{2,1,0:T(8,128)(2,1)S(1)}, u32[]{:S(2)}, u32[]{:S(2)}) %all-to-all-start.4) | async-done | bytes 67616 | tf_op jit(solution)/shard_map/reduce_z/all_to_all | solution.py:191
  126.9 0.6 broadcast_multiply_fusion
  (6 shorter events, 0.1 us)
Async XLA Ops:
  7.2 0.7 copy-start.2
  7.9 0.7 copy-start.3
  9.3 27.1 %all-to-all-start = ((bf16[12,11,256]{2,1,0:T(8,128)(2,1)}), bf16[12,11,256]{2,1,0:T(8,128)(2,1)S(1)}, u32[]{:S(2)}, u32[]{:S(2)}) async-start(bf16[12,11,256]{2,1,0:T(8,128)(2,1)} %weight_far.1), calls=%async_computation | async-start | bytes 196608 | tf_op jit(solution)/shard_map/weight_far/all_to_all | solution.py:142
  25.2 5.6 %copy-start.1 = (bf16[1,4096]{1,0:T(2,128)(2,1)}, bf16[1,4096]{1,0:T(2,128)(2,1)S(1)}, u32[]{:S(2)}) copy-start(bf16[1,4096]{1,0:T(2,128)(2,1)S(1)} %reshape.49.refs_2_.gain) | copy-start | bytes 24580
  25.2 1.6 %copy-start.5 = (bf16[256,4096]{1,0:T(8,128)(2,1)S(1)}, bf16[256,4096]{1,0:T(8,128)(2,1)}, u32[]{:S(2)}) copy-start(bf16[256,4096]{1,0:T(8,128)(2,1)} %tokens.1) | copy-start | bytes 6291460
  26.8 1.0 copy-start.6
  27.8 1.0 copy-start.7
  30.9 1.4 %copy-start.4 = (bf16[4,8,136,256]{3,2,1,0:T(8,128)(2,1)}, bf16[4,8,136,256]{3,2,1,0:T(8,128)(2,1)S(1)}, u32[]{:S(2)}) copy-start(bf16[4,8,136,256]{3,2,1,0:T(8,128)(2,1)S(1)} %get-tuple-element.31) | copy-start | bytes 6684676
  32.3 0.7 copy-start.8
  36.5 7.5 %collective-permute-start = (bf16[4,8,136,256]{3,2,1,0:T(8,128)(2,1)}, bf16[4,8,136,256]{3,2,1,0:T(8,128)(2,1)}, u32[]{:S(2)}, u32[]{:S(2)}) collective-permute-start(bf16[4,8,136,256]{3,2,1,0:T(8,128)(2,1)} %copy-done.4), channel_id=1, source_target_pairs={{0,1},{1,0},{2,3},{3,2},{4,5},{5,4},{6,7},{7,6},{8,9},{9,8},{10,11... | collective-permute-start | bytes 6684680 | tf_op jit(solution)/shard_map/reduce_core/ppermute | solution.py:166
  39.2 10.2 %all-to-all-start.1 = ((bf16[4,136,256]{2,1,0:T(8,128)(2,1)}), bf16[4,136,256]{2,1,0:T(8,128)(2,1)S(1)}, u32[]{:S(2)}, u32[]{:S(2)}) async-start(bf16[4,136,256]{2,1,0:T(8,128)(2,1)} %broadcast_in_dim.14), calls=%async_computation.1 | async-start | bytes 557056 | tf_op jit(solution)/shard_map/weight_x/all_to_all | solution.py:164
  43.9 71.3 %all-gather.3.cloned.1.call-start = ((), (), s32[]{:S(2)}) async-start(), calls=%async_computation.5 | async-start | bytes 4734976 | tf_op jit(solution)/shard_map/weight_near/all_gather | solution.py:170
  49.4 0.7 copy-start.9
  50.1 31.2 %all-to-all-start.2 = ((bf16[4,8,136,256]{3,2,1,0:T(8,128)(2,1)}), bf16[4,8,136,256]{3,2,1,0:T(8,128)(2,1)S(1)}, u32[]{:S(2)}, u32[]{:S(2)}) async-start(bf16[4,8,136,256]{3,2,1,0:T(8,128)(2,1)} %add_convert_fusion), calls=%async_computation.2 | async-start | bytes 4456448 | tf_op jit(solution)/shard_map/reduce_x/all_to_all | solution.py:173
  55.9 0.7 copy-start
  56.7 32.8 %copy-start.10 = (s32[528,1]{0,1:T(1,128)S(1)}, s32[528,1]{0,1:T(1,128)}, u32[]{:S(2)}) copy-start(s32[528,1]{0,1:T(1,128)} %constant.19.clone) | copy-start | bytes 6340
  82.4 23.6 %all-to-all-start.3 = ((bf16[8,136,256]{2,1,0:T(8,128)(2,1)}), bf16[8,136,256]{2,1,0:T(8,128)(2,1)S(1)}, u32[]{:S(2)}, u32[]{:S(2)}) async-start(bf16[8,136,256]{2,1,0:T(8,128)(2,1)} %fusion), calls=%async_computation.3 | async-start | bytes 1114112 | tf_op jit(solution)/shard_map/reduce_y/all_to_all | solution.py:185
  106.8 20.0 %all-to-all-start.4 = ((bf16[12,11,256]{2,1,0:T(8,128)(2,1)}), bf16[12,11,256]{2,1,0:T(8,128)(2,1)S(1)}, u32[]{:S(2)}, u32[]{:S(2)}) async-start(bf16[12,11,256]{2,1,0:T(8,128)(2,1)} %reshape.52), calls=%async_computation.4 | async-start | bytes 196608 | tf_op jit(solution)/shard_map/reduce_z/all_to_all | solution.py:191
Sparse Core Ops, SparseCore 0:
  50.2 48.3 all-gather.2

commit v10 on v7

--- a/solution.py
+++ b/solution.py
@@ -63,8 +63,16 @@
             out[x, 2 * y + 1] = part[group:].astype(jnp.bfloat16)
 
 
-def prep_kernel(cot_grouped, cot):
+def prep_kernel(cot_grouped, order, cot, move):
     cot[...] = cot_grouped[...].T
+    move[...] = pick(order[...], move.shape[1])
+
+
+def sum_kernel(parts, move, out):
+    total = parts[0].astype(jnp.float32)
+    for i in range(1, parts.shape[0]):
+        total = total + parts[i].astype(jnp.float32)
+    out[...] = dot(move[...], total.astype(jnp.bfloat16), 1, 0).astype(jnp.bfloat16)
 
 
 def keys_kernel(order, grouped, keys):
@@ -119,6 +127,9 @@
     toks, feats = tokens.shape
     outw = cotangent.shape[1]
     group, grouped, natural = row_orders(n_z, rows)
+    by_z = np.arange(2 * n_y)[None, :, None] * group + np.arange(n_z * rows).reshape(n_z, 1, rows)
+    by_z = by_z.reshape(-1, 1).astype(np.int32)
+    move_shape = (by_z.shape[0], 2 * n_y * group)
     place = lax.axis_index("core").astype(jnp.int32).reshape(1)
     gain_row = gain.reshape(1, feats)
     cot_t = cotangent.T
@@ -126,9 +137,10 @@
     with jax.named_scope("weight_far"):
         scale = jnp.repeat(scales.astype(jnp.float32), width // scales.shape[1], axis=1)
         own = (codes.astype(jnp.float32) * scale).astype(jnp.bfloat16)
-        spread = jnp.broadcast_to(own[None], (n_x * n_z, rows, width))
+        spread = jnp.broadcast_to(own[None], (n_z, rows, width))
         spread, tokens_after = together(spread, tokens)
-        spread = lax.all_to_all(spread, ("x", "z"), split_axis=0, concat_axis=0, tiled=True)
+        spread = lax.all_to_all(spread, "z", split_axis=0, concat_axis=0, tiled=True)
+
     with jax.named_scope("term"):
         near = jax.ShapeDtypeStruct((n_x, 2 * n_y, group, width), jnp.bfloat16)
         mine, theirs, cot_grouped, inv = pl.pallas_call(
@@ -145,27 +157,41 @@
             cost_estimate=pl.CostEstimate(flops=3 * toks * outw * feats, bytes_accessed=4 * toks * feats, transcendentals=0),
         )(place, tokens_after, gain_row, cot_t, jnp.asarray(grouped))
         cot_grouped = cot_grouped.reshape(4 * group, toks)
-    with jax.named_scope("weight_near"):
+    with jax.named_scope("weight_x"):
+        spread, theirs = together(spread, theirs)
+        strip = jnp.pad(spread.reshape(n_z * rows, width), ((0, group - n_z * rows), (0, 0)))
+        slab = jnp.broadcast_to(strip[None], (n_x, group, width))
+        slab = lax.all_to_all(slab, "x", split_axis=0, concat_axis=0, tiled=True)
+    with jax.named_scope("reduce_core"):
         came = lax.ppermute(theirs, "core", ((0, 1), (1, 0)))
         pair = (mine.astype(jnp.float32) + came.astype(jnp.float32)).astype(jnp.bfloat16)
-        spread, pair = together(spread, pair)
-        slab = jnp.pad(spread.reshape(n_x, n_z * rows, width), ((0, 0), (0, group - n_z * rows), (0, 0)))
+    with jax.named_scope("weight_near"):
+        slab, pair = together(slab, pair)
         w = lax.all_gather(slab, ("y_hi", "y_lo", "core"), axis=0, tiled=False).reshape(n_y, 2, 2, n_x, group, width)
     with jax.named_scope("reduce_x"):
         cot_after, _ = together(cot_grouped, slab)
         parts = lax.all_to_all(pair, "x", split_axis=0, concat_axis=0, tiled=True)
-        cot = pl.pallas_call(
+        cot, move = pl.pallas_call(
             prep_kernel,
-            out_shape=jax.ShapeDtypeStruct((toks, 4 * group), jnp.bfloat16),
-            in_specs=[VMEM],
+            out_shape=(
+                jax.ShapeDtypeStruct((toks, 4 * group), jnp.bfloat16),
+                jax.ShapeDtypeStruct(move_shape, jnp.bfloat16),
+            ),
+            in_specs=[VMEM] * 2,
+            out_specs=(VMEM,) * 2,
+            compiler_params=params(16),
+        )(cot_after, jnp.asarray(by_z))
+        parts, cot, move = together(parts, cot, move)
+        part = pl.pallas_call(
+            sum_kernel,
+            out_shape=jax.ShapeDtypeStruct((move_shape[0], width), jnp.bfloat16),
+            in_specs=[VMEM] * 2,
             out_specs=VMEM,
-            compiler_params=params(8),
-        )(cot_after)
-        parts, cot = together(parts, cot)
-        part = add(parts).astype(jnp.bfloat16)
-    with jax.named_scope("reduce_y"):
-        part, inv = together(part, inv)
-        parts = lax.all_to_all(part, ("y_hi", "y_lo"), split_axis=0, concat_axis=0, tiled=True)
+            compiler_params=params(16),
+        )(parts.reshape(n_x, move_shape[1], width), move)
+    with jax.named_scope("reduce_z"):
+        part, inv = together(part.reshape(n_z, 2 * n_y * rows, width), inv)
+        parts = lax.all_to_all(part, "z", split_axis=0, concat_axis=0, tiled=True)
     with jax.named_scope("main"):
         whole = lambda *shape: pl.BlockSpec(shape, lambda i: (0,) * len(shape))
         keys_grouped, grad_tokens = pl.pallas_call(
@@ -191,11 +217,11 @@
             compiler_params=params(60),
             cost_estimate=pl.CostEstimate(flops=5 * toks * outw * feats, bytes_accessed=10 * toks * feats, transcendentals=0),
         )(tokens, gain_row, cot, inv, w)
-    with jax.named_scope("reduce_z"):
+    with jax.named_scope("reduce_y"):
         parts, grad_tokens = together(parts, grad_tokens)
-        part = add(parts).astype(jnp.bfloat16)[: n_z * rows].reshape(n_z, rows, width)
+        part = add(parts).astype(jnp.bfloat16).reshape(2 * n_y, rows, width)
         part, keys_grouped = together(part, keys_grouped)
-        last = lax.all_to_all(part, "z", split_axis=0, concat_axis=0, tiled=True)
+        last = lax.all_to_all(part, ("y_hi", "y_lo"), split_axis=0, concat_axis=0, tiled=True)
         keys_t = pl.pallas_call(
             keys_kernel,
             out_shape=jax.ShapeDtypeStruct((outw, toks), jnp.bfloat16),

time: 151 us -> 140 us (0.927); the launches traced: 151 us -> 138 us
  waiting for transfers between devices: 62.8 us -> 48.7 us
  local copies, waits for them, and re-layouts: 8.72 us -> 14.8 us
  starting transfers between devices: 45.5 us -> 40.8 us
    all_to_all x2 -> x3, waiting for transfers between devices: 28.2 us -> 15.6 us  [the longest x1 10.1 us: per_device(): parts = lax.all_to_all(part, 'z', split_axis=0, concat_axis=0, tiled=True)]
    all_gather x1, waiting for transfers between devices: 12.3 us -> 4.16 us  [per_device(): lax.all_gather(slab, ('y_hi', 'y_lo', 'core'), axis=0, tiled=False)]
    unnamed x18 -> x28, local copies, waits for them, and re-layouts: 4.9 us -> 11.2 us
    all_to_all x1, waiting for transfers between devices: 0.01 us -> 6.27 us  [per_device(): lax.all_to_all(part, ('y_hi', 'y_lo'), split_axis=0, concat_axis=0, tiled...]
    all_to_all x2 -> x3, starting transfers between devices: 31.7 us -> 26 us  [the longest x1 15.2 us: per_device(): lax.all_to_all(spread, 'z', split_axis=0, concat_axis=0, tiled=True)]
    pallas_call x1 -> x2, Pallas kernels: 0.13 us -> 2.37 us  [the longest x1 1.81 us: per_device(): pl.pallas_call(sum_kernel, out_shape=jax.ShapeDtypeStruct((move_shape[0],...]
  transfers between devices with their start and end apart: 6 -> 7, of which waited for: 4 -> 6; matrix products, arithmetic and copies ran while one was open for 3% -> 4% of each run, Pallas kernels for 6% -> 10%
where the time goes in v10:
time: 140 us; the launch traced here: 138 us
  waiting for transfers between devices  48.7 us (35%)
  starting transfers between devices  40.8 us (29%)
  local copies, waits for them, and re-layouts  14.8 us (11%)
  Pallas kernels  14.2 us (10%)
  between operations  14.2 us (10%)
  other arithmetic  4.94 us (4%)
    all_to_all x1, waiting for transfers between devices, per_device(): parts = lax.all_to_all(pair, 'x', split_axis=0, concat_axis=0, tiled=True)  22.7 us
    all_to_all x1, starting transfers between devices, per_device(): lax.all_to_all(spread, 'z', split_axis=0, concat_axis=0, tiled=True)  15.2 us
    unnamed x28, local copies, waits for them, and re-layouts  11.2 us
    all_to_all x1, waiting for transfers between devices, per_device(): parts = lax.all_to_all(part, 'z', split_axis=0, concat_axis=0, tiled=True)  10.1 us
    pallas_call x1, Pallas kernels, per_device(): pl.pallas_call(main_kernel, grid=(n_y,), out_shape=(jax.ShapeDtypeStruct(...  8.53 us
    all_to_all x1, starting transfers between devices, per_device(): lax.all_to_all(part, ('y_hi', 'y_lo'), split_axis=0, concat_axis=0, tiled...  7.09 us
    all_to_all x1, waiting for transfers between devices, per_device(): lax.all_to_all(part, ('y_hi', 'y_lo'), split_axis=0, concat_axis=0, tiled...  6.27 us
    all_to_all x1, starting transfers between devices, per_device(): parts = lax.all_to_all(part, 'z', split_axis=0, concat_axis=0, tiled=True)  6.03 us
  transfers between devices with their start and end apart: 7, of which 6 were waited for; matrix products, arithmetic and copies ran while one was open for 4% of the time, Pallas kernels for 10%

profile of v10, /device:TPU:6, one launch (start us, length us, event | category | flops | bytes accessed | tf_op | source)
XLA Modules:
  0.0 137.6 jit_solution(1146835779883329443)
XLA Ops:
  7.2 0.8 copy.13
  7.9 0.1 broadcast_in_dim.6
  8.0 0.7 multiply_convert_fusion
  8.7 0.6 broadcast_in_dim.7
  9.4 15.2 %all-to-all-start = ((bf16[12,11,256]{2,1,0:T(8,128)(2,1)}), bf16[12,11,256]{2,1,0:T(8,128)(2,1)S(1)}, u32[]{:S(2)}, u32[]{:S(2)}) async-start(bf16[12,11,256]{2,1,0:T(8,128)(2,1)} %broadcast_in_dim.7), calls=%async_computation | async-start | bytes 196608 | tf_op jit(solution)/shard_map/weight_far/all_to_all | solution.py:142
  24.5 0.7 reshape.70.refs_2_.gain
  25.3 0.0 copy-start.5
  25.3 0.0 copy-start.7
  25.3 1.6 %copy-done.7 = bf16[256,4096]{1,0:T(8,128)(2,1)S(1)} copy-done((bf16[256,4096]{1,0:T(8,128)(2,1)S(1)}, bf16[256,4096]{1,0:T(8,128)(2,1)}, u32[]{:S(2)}) %copy-start.7) | copy-done | bytes 2097176
  26.9 0.0 copy-start.9
  26.9 1.0 copy-done.9
  27.8 0.0 copy-start.10
  27.8 1.0 copy-done.10
  28.8 2.1 %term.1 = (bf16[4,8,136,256]{3,2,1,0:T(8,128)(2,1)S(1)}, bf16[4,8,136,256]{3,2,1,0:T(8,128)(2,1)S(1)}, bf16[2,272,256]{2,1,0:T(8,128)(2,1)S(1)}, f32[256,128]{1,0:T(8,128)S(1)}) custom-call(s32[1]{0:T(128)} %bitcast.refs_0_, bf16[256,4096]{1,0:T(8,128)(2,1)S(1)} %copy-done.7, bf16[1,4096]{1,0:T(2,128)(2,1)S(1)} %reshape.70.refs_2_.gain, ...), custom_call_target="tpu_custom_call" | custom-call | flops 1660944384 | bytes 4194304 | tf_op jit(solution)/shard_map/term/pallas_call | solution.py:146
  30.9 0.0 copy-done.5
  30.9 0.0 copy-start.6
  30.9 1.4 copy-done.6
  32.3 0.0 copy-start.11
  32.3 0.7 copy-done.11
  32.9 3.6 %all-to-all-done = bf16[12,11,256]{2,1,0:T(8,128)(2,1)S(1)} async-done(((bf16[12,11,256]{2,1,0:T(8,128)(2,1)}), bf16[12,11,256]{2,1,0:T(8,128)(2,1)S(1)}, u32[]{:S(2)}, u32[]{:S(2)}) %all-to-all-start) | async-done | bytes 67616 | tf_op jit(solution)/shard_map/weight_far/all_to_all | solution.py:142
  36.5 1.9 %collective-permute-start = (bf16[4,8,136,256]{3,2,1,0:T(8,128)(2,1)}, bf16[4,8,136,256]{3,2,1,0:T(8,128)(2,1)}, u32[]{:S(2)}, u32[]{:S(2)}) collective-permute-start(bf16[4,8,136,256]{3,2,1,0:T(8,128)(2,1)} %copy-done.6), channel_id=1, source_target_pairs={{0,1},{1,0},{2,3},{3,2},{4,5},{5,4},{6,7},{7,6},{8,9},{9,8},{10,11... | collective-permute-start | bytes 6684680 | tf_op jit(solution)/shard_map/reduce_core/ppermute | solution.py:166
  38.5 0.7 broadcast_in_dim.8
  39.2 4.8 %all-to-all-start.1 = ((bf16[4,136,256]{2,1,0:T(8,128)(2,1)}), bf16[4,136,256]{2,1,0:T(8,128)(2,1)S(1)}, u32[]{:S(2)}, u32[]{:S(2)}) async-start(bf16[4,136,256]{2,1,0:T(8,128)(2,1)} %broadcast_in_dim.8), calls=%async_computation.1 | async-start | bytes 557056 | tf_op jit(solution)/shard_map/weight_x/all_to_all | solution.py:164
  44.0 0.0 all-gather.3.cloned.1.call-start
  44.0 0.0 collective-permute-done
  44.0 3.5 %add_convert_fusion = bf16[4,8,136,256]{3,2,1,0:T(8,128)(2,1)} fusion(bf16[4,8,136,256]{3,2,1,0:T(8,128)(2,1)} %collective-permute-done, bf16[4,8,136,256]{3,2,1,0:T(8,128)(2,1)S(1)} %get-tuple-element.33), kind=kLoop, calls=%fused_computation | loop fusion | flops 4456448 | bytes 6684672 | tf_op jit(solution)/shard_map/reduce_core/convert_element_type | solution.py:167
  47.5 1.9 %all-to-all-done.1 = bf16[4,136,256]{2,1,0:T(8,128)(2,1)S(1)} async-done(((bf16[4,136,256]{2,1,0:T(8,128)(2,1)}), bf16[4,136,256]{2,1,0:T(8,128)(2,1)S(1)}, u32[]{:S(2)}, u32[]{:S(2)}) %all-to-all-start.1) | async-done | bytes 278560 | tf_op jit(solution)/shard_map/weight_x/all_to_all | solution.py:164
  49.4 0.0 copy-start.12
  49.4 0.7 copy-done.12
  50.1 0.0 all-gather.3.cloned.1.call-update
  50.2 0.0 copy-start.2
  50.2 5.8 %all-to-all-start.2 = ((bf16[4,8,136,256]{3,2,1,0:T(8,128)(2,1)}), bf16[4,8,136,256]{3,2,1,0:T(8,128)(2,1)S(1)}, u32[]{:S(2)}, u32[]{:S(2)}) async-start(bf16[4,8,136,256]{3,2,1,0:T(8,128)(2,1)} %add_convert_fusion), calls=%async_computation.2 | async-start | bytes 4456448 | tf_op jit(solution)/shard_map/reduce_x/all_to_all | solution.py:173
  56.0 0.0 copy-done.2
  56.0 0.6 reduce_x.2
  56.5 0.0 copy-start
  56.6 1.5 %copy-done = bf16[1056,1088]{1,0:T(8,128)(2,1)} copy-done((bf16[1056,1088]{1,0:T(8,128)(2,1)}, bf16[1056,1088]{1,0:T(8,128)(2,1)S(1)}, u32[]{:S(2)}) %copy-start) | copy-done | bytes 2297880
  58.1 0.0 copy-start.8
  58.1 0.7 copy-done.8
  58.8 22.7 %all-to-all-done.2 = bf16[4,8,136,256]{3,2,1,0:T(8,128)(2,1)S(1)} async-done(((bf16[4,8,136,256]{3,2,1,0:T(8,128)(2,1)}), bf16[4,8,136,256]{3,2,1,0:T(8,128)(2,1)S(1)}, u32[]{:S(2)}, u32[]{:S(2)}) %all-to-all-start.2) | async-done | bytes 2228256 | tf_op jit(solution)/shard_map/reduce_x/all_to_all | solution.py:173
  81.5 0.0 copy-start.1
  81.5 1.7 %copy-done.1 = bf16[1056,1088]{1,0:T(8,128)(2,1)S(1)} copy-done((bf16[1056,1088]{1,0:T(8,128)(2,1)S(1)}, bf16[1056,1088]{1,0:T(8,128)(2,1)}, u32[]{:S(2)}) %copy-start.1) | copy-done | bytes 2297880
  83.2 1.8 %reduce_x.3 = bf16[1056,256]{1,0:T(8,128)(2,1)} custom-call(bf16[4,1088,256]{2,1,0:T(8,128)(2,1)S(1)} %bitcast.10, bf16[1056,1088]{1,0:T(8,128)(2,1)S(1)} %copy-done.1), custom_call_target="tpu_custom_call" | custom-call | tf_op jit(solution)/shard_map/reduce_x/pallas_call | solution.py:185
  85.0 6.0 %all-to-all-start.3 = ((bf16[12,88,256]{2,1,0:T(8,128)(2,1)}), bf16[12,88,256]{2,1,0:T(8,128)(2,1)S(1)}, u32[]{:S(2)}, u32[]{:S(2)}) async-start(bf16[12,88,256]{2,1,0:T(8,128)(2,1)} %bitcast.4), calls=%async_computation.3 | async-start | bytes 1081344 | tf_op jit(solution)/shard_map/reduce_z/all_to_all | solution.py:194
  91.1 4.2 %all-gather.3.cloned.1.call-done = bf16[64,136,256]{2,1,0:T(8,128)(2,1)} async-done(((bf16[4,136,256]{2,1,0:T(8,128)(2,1)}), bf16[64,136,256]{2,1,0:T(8,128)(2,1)}) %all-gather.3.cloned.1.call-update) | async-done | bytes 4456464 | tf_op jit(solution)/shard_map/weight_near/all_gather | solution.py:170
  95.2 0.0 copy-start.4
  95.2 8.5 %main.1 = (bf16[544,256]{1,0:T(8,128)(2,1)}, bf16[256,4096]{1,0:T(8,128)(2,1)}) custom-call(bf16[256,4096]{1,0:T(8,128)(2,1)} %tokens.1, bf16[1,4096]{1,0:T(2,128)(2,1)} %copy-done.5, bf16[256,544]{1,0:T(8,128)(2,1)} %copy-done.8, f32[256,128]{1,0:T(8,128)} %copy-done.11, bf16[4,2,2,4,136,256]{5,4,3,2,1,0:T(8,128)(2,1)} %bitcast.16), custom_call_target="tpu_custom_call" | custom-call | flops 2768240640 | bytes 10485760 | tf_op jit(solution)/shard_map/main/pallas_call | solution.py:197
  103.8 10.1 %all-to-all-done.3 = bf16[12,88,256]{2,1,0:T(8,128)(2,1)S(1)} async-done(((bf16[12,88,256]{2,1,0:T(8,128)(2,1)}), bf16[12,88,256]{2,1,0:T(8,128)(2,1)S(1)}, u32[]{:S(2)}, u32[]{:S(2)}) %all-to-all-start.3) | async-done | bytes 540704 | tf_op jit(solution)/shard_map/reduce_z/all_to_all | solution.py:194
  113.9 0.1 add_convert_fusion.1
  114.0 0.6 reshape.94
  114.6 7.1 %all-to-all-start.4 = ((bf16[8,11,256]{2,1,0:T(8,128)(2,1)}), bf16[8,11,256]{2,1,0:T(8,128)(2,1)S(1)}, u32[]{:S(2)}, u32[]{:S(2)}) async-start(bf16[8,11,256]{2,1,0:T(8,128)(2,1)} %reshape.94), calls=%async_computation.4 | async-start | bytes 131072 | tf_op jit(solution)/shard_map/reduce_y/all_to_all | solution.py:224
  121.7 0.0 copy-done.4
  121.7 0.0 copy-start.3
  121.7 0.9 copy-done.3
  122.7 1.1 reduce_y.1
  123.8 6.3 %all-to-all-done.4 = bf16[8,11,256]{2,1,0:T(8,128)(2,1)S(1)} async-done(((bf16[8,11,256]{2,1,0:T(8,128)(2,1)}), bf16[8,11,256]{2,1,0:T(8,128)(2,1)S(1)}, u32[]{:S(2)}, u32[]{:S(2)}) %all-to-all-start.4) | async-done | bytes 45088 | tf_op jit(solution)/shard_map/reduce_y/all_to_all | solution.py:224
  130.1 0.6 broadcast_multiply_fusion
  (5 shorter events, 0.1 us)
Async XLA Ops:
  9.4 27.1 %all-to-all-start = ((bf16[12,11,256]{2,1,0:T(8,128)(2,1)}), bf16[12,11,256]{2,1,0:T(8,128)(2,1)S(1)}, u32[]{:S(2)}, u32[]{:S(2)}) async-start(bf16[12,11,256]{2,1,0:T(8,128)(2,1)} %broadcast_in_dim.7), calls=%async_computation | async-start | bytes 196608 | tf_op jit(solution)/shard_map/weight_far/all_to_all | solution.py:142
  25.3 5.6 %copy-start.5 = (bf16[1,4096]{1,0:T(2,128)(2,1)}, bf16[1,4096]{1,0:T(2,128)(2,1)S(1)}, u32[]{:S(2)}) copy-start(bf16[1,4096]{1,0:T(2,128)(2,1)S(1)} %reshape.70.refs_2_.gain) | copy-start | bytes 24580
  25.3 1.6 %copy-start.7 = (bf16[256,4096]{1,0:T(8,128)(2,1)S(1)}, bf16[256,4096]{1,0:T(8,128)(2,1)}, u32[]{:S(2)}) copy-start(bf16[256,4096]{1,0:T(8,128)(2,1)} %tokens.1) | copy-start | bytes 6291460
  26.9 1.0 copy-start.9
  27.8 1.0 copy-start.10
  30.9 1.4 copy-start.6
  32.3 0.7 copy-start.11
  36.5 7.5 %collective-permute-start = (bf16[4,8,136,256]{3,2,1,0:T(8,128)(2,1)}, bf16[4,8,136,256]{3,2,1,0:T(8,128)(2,1)}, u32[]{:S(2)}, u32[]{:S(2)}) collective-permute-start(bf16[4,8,136,256]{3,2,1,0:T(8,128)(2,1)} %copy-done.6), channel_id=1, source_target_pairs={{0,1},{1,0},{2,3},{3,2},{4,5},{5,4},{6,7},{7,6},{8,9},{9,8},{10,11... | collective-permute-start | bytes 6684680 | tf_op jit(solution)/shard_map/reduce_core/ppermute | solution.py:166
  39.2 10.2 %all-to-all-start.1 = ((bf16[4,136,256]{2,1,0:T(8,128)(2,1)}), bf16[4,136,256]{2,1,0:T(8,128)(2,1)S(1)}, u32[]{:S(2)}, u32[]{:S(2)}) async-start(bf16[4,136,256]{2,1,0:T(8,128)(2,1)} %broadcast_in_dim.8), calls=%async_computation.1 | async-start | bytes 557056 | tf_op jit(solution)/shard_map/weight_x/all_to_all | solution.py:164
  44.0 51.2 %all-gather.3.cloned.1.call-start = ((), (), s32[]{:S(2)}) async-start(), calls=%async_computation.5 | async-start | bytes 4734976 | tf_op jit(solution)/shard_map/weight_near/all_gather | solution.py:170
  49.4 0.7 copy-start.12
  50.2 5.8 %copy-start.2 = (s32[1056,1]{1,0:T(8,128)S(1)}, s32[1056,1]{1,0:T(8,128)}, u32[]{:S(2)}) copy-start(s32[1056,1]{1,0:T(8,128)} %constant.19.clone.order) | copy-start | bytes 12676
  50.2 31.3 %all-to-all-start.2 = ((bf16[4,8,136,256]{3,2,1,0:T(8,128)(2,1)}), bf16[4,8,136,256]{3,2,1,0:T(8,128)(2,1)S(1)}, u32[]{:S(2)}, u32[]{:S(2)}) async-start(bf16[4,8,136,256]{3,2,1,0:T(8,128)(2,1)} %add_convert_fusion), calls=%async_computation.2 | async-start | bytes 4456448 | tf_op jit(solution)/shard_map/reduce_x/all_to_all | solution.py:173
  56.5 1.5 %copy-start = (bf16[1056,1088]{1,0:T(8,128)(2,1)}, bf16[1056,1088]{1,0:T(8,128)(2,1)S(1)}, u32[]{:S(2)}) copy-start(bf16[1056,1088]{1,0:T(8,128)(2,1)S(1)} %get-tuple-element.42.move) | copy-start | bytes 6893572
  58.1 0.7 copy-start.8
  81.5 1.7 %copy-start.1 = (bf16[1056,1088]{1,0:T(8,128)(2,1)S(1)}, bf16[1056,1088]{1,0:T(8,128)(2,1)}, u32[]{:S(2)}) copy-start(bf16[1056,1088]{1,0:T(8,128)(2,1)} %copy-done) | copy-start | bytes 6893572
  85.0 28.9 %all-to-all-start.3 = ((bf16[12,88,256]{2,1,0:T(8,128)(2,1)}), bf16[12,88,256]{2,1,0:T(8,128)(2,1)S(1)}, u32[]{:S(2)}, u32[]{:S(2)}) async-start(bf16[12,88,256]{2,1,0:T(8,128)(2,1)} %bitcast.4), calls=%async_computation.3 | async-start | bytes 1081344 | tf_op jit(solution)/shard_map/reduce_z/all_to_all | solution.py:194
  95.2 26.5 %copy-start.4 = (s32[528,1]{1,0:T(8,128)S(1)}, s32[528,1]{1,0:T(8,128)}, u32[]{:S(2)}) copy-start(s32[528,1]{1,0:T(8,128)} %constant.20.clone.order) | copy-start | bytes 6340
  114.6 15.5 %all-to-all-start.4 = ((bf16[8,11,256]{2,1,0:T(8,128)(2,1)}), bf16[8,11,256]{2,1,0:T(8,128)(2,1)S(1)}, u32[]{:S(2)}, u32[]{:S(2)}) async-start(bf16[8,11,256]{2,1,0:T(8,128)(2,1)} %reshape.94), calls=%async_computation.4 | async-start | bytes 131072 | tf_op jit(solution)/shard_map/reduce_y/all_to_all | solution.py:224
  121.7 1.0 copy-start.3
Sparse Core Ops, SparseCore 0:
  50.3 44.9 all-gather.2

commit v11 on v7

--- a/solution.py
+++ b/solution.py
@@ -126,9 +126,10 @@
     with jax.named_scope("weight_far"):
         scale = jnp.repeat(scales.astype(jnp.float32), width // scales.shape[1], axis=1)
         own = (codes.astype(jnp.float32) * scale).astype(jnp.bfloat16)
-        spread = jnp.broadcast_to(own[None], (n_x * n_z, rows, width))
+        spread = jnp.broadcast_to(own[None], (n_z, rows, width))
         spread, tokens_after = together(spread, tokens)
-        spread = lax.all_to_all(spread, ("x", "z"), split_axis=0, concat_axis=0, tiled=True)
+        spread = lax.all_to_all(spread, "z", split_axis=0, concat_axis=0, tiled=True)
+
     with jax.named_scope("term"):
         near = jax.ShapeDtypeStruct((n_x, 2 * n_y, group, width), jnp.bfloat16)
         mine, theirs, cot_grouped, inv = pl.pallas_call(
@@ -145,11 +146,16 @@
             cost_estimate=pl.CostEstimate(flops=3 * toks * outw * feats, bytes_accessed=4 * toks * feats, transcendentals=0),
         )(place, tokens_after, gain_row, cot_t, jnp.asarray(grouped))
         cot_grouped = cot_grouped.reshape(4 * group, toks)
-    with jax.named_scope("weight_near"):
+    with jax.named_scope("weight_x"):
+        spread, theirs = together(spread, theirs)
+        strip = jnp.pad(spread.reshape(n_z * rows, width), ((0, group - n_z * rows), (0, 0)))
+        slab = jnp.broadcast_to(strip[None], (n_x, group, width))
+        slab = lax.all_to_all(slab, "x", split_axis=0, concat_axis=0, tiled=True)
+    with jax.named_scope("reduce_core"):
         came = lax.ppermute(theirs, "core", ((0, 1), (1, 0)))
         pair = (mine.astype(jnp.float32) + came.astype(jnp.float32)).astype(jnp.bfloat16)
-        spread, pair = together(spread, pair)
-        slab = jnp.pad(spread.reshape(n_x, n_z * rows, width), ((0, 0), (0, group - n_z * rows), (0, 0)))
+    with jax.named_scope("weight_near"):
+        slab, pair = together(slab, pair)
         w = lax.all_gather(slab, ("y_hi", "y_lo", "core"), axis=0, tiled=False).reshape(n_y, 2, 2, n_x, group, width)
     with jax.named_scope("reduce_x"):
         cot_after, _ = together(cot_grouped, slab)

time: 151 us -> 143 us (0.947)
  waiting for transfers between devices: 62.8 us -> 49.8 us
  starting transfers between devices: 45.5 us -> 49.7 us
  local copies, waits for them, and re-layouts: 8.72 us -> 10.6 us
    all_to_all x1 -> x2, waiting for transfers between devices: 17.6 us -> 5.45 us  [the longest x1 3.56 us: per_device(): lax.all_to_all(spread, 'z', split_axis=0, concat_axis=0, tiled=True)]
    all_gather x1, waiting for transfers between devices: 12.3 us -> 9.11 us  [per_device(): lax.all_gather(slab, ('y_hi', 'y_lo', 'core'), axis=0, tiled=False)]
    all_to_all x1, waiting for transfers between devices: 22.3 us -> 24.6 us  [per_device(): parts = lax.all_to_all(pair, 'x', split_axis=0, concat_axis=0, tiled=True)]
    unnamed x18 -> x22, local copies, waits for them, and re-layouts: 4.9 us -> 7 us
    all_to_all x1, starting transfers between devices: 13.2 us -> 15.1 us  [per_device(): last = lax.all_to_all(part, 'z', split_axis=0, concat_axis=0, tiled=True)]
    all_to_all x1 -> x2, starting transfers between devices: 18.6 us -> 19.9 us  [the longest x1 15.2 us: per_device(): lax.all_to_all(spread, 'z', split_axis=0, concat_axis=0, tiled=True)]
  transfers between devices with their start and end apart: 6 -> 7, of which waited for: 4 -> 5; matrix products, arithmetic and copies ran while one was open for 3% -> 4% of each run, Pallas kernels for 6% -> 8%
where the time goes in v11:
time: 143 us; the launch traced here: 142 us
  waiting for transfers between devices  49.8 us (35%)
  starting transfers between devices  49.7 us (35%)
  between operations  14.2 us (10%)
  Pallas kernels  11.9 us (8%)
  local copies, waits for them, and re-layouts  10.6 us (7%)
  other arithmetic  6.08 us (4%)
    all_to_all x1, waiting for transfers between devices, per_device(): parts = lax.all_to_all(pair, 'x', split_axis=0, concat_axis=0, tiled=True)  24.6 us
    all_to_all x1, starting transfers between devices, per_device(): lax.all_to_all(spread, 'z', split_axis=0, concat_axis=0, tiled=True)  15.2 us
    all_to_all x1, starting transfers between devices, per_device(): last = lax.all_to_all(part, 'z', split_axis=0, concat_axis=0, tiled=True)  15.1 us
    all_to_all x1, waiting for transfers between devices, per_device(): last = lax.all_to_all(part, 'z', split_axis=0, concat_axis=0, tiled=True)  10.6 us
    all_gather x1, waiting for transfers between devices, per_device(): lax.all_gather(slab, ('y_hi', 'y_lo', 'core'), axis=0, tiled=False)  9.11 us
    pallas_call x1, Pallas kernels, per_device(): pl.pallas_call(main_kernel, grid=(n_y,), out_shape=(jax.ShapeDtypeStruct(...  8.48 us
    all_to_all x1, starting transfers between devices, per_device(): lax.all_to_all(part, ('y_hi', 'y_lo'), split_axis=0, concat_axis=0, tiled...  7.1 us
    unnamed x22, local copies, waits for them, and re-layouts  7 us
  transfers between devices with their start and end apart: 7, of which 5 were waited for; matrix products, arithmetic and copies ran while one was open for 4% of the time, Pallas kernels for 8%

profile of v11, /device:TPU:6, one launch (start us, length us, event | category | flops | bytes accessed | tf_op | source)
XLA Modules:
  0.0 142.3 jit_solution(9232027433864660612)
XLA Ops:
  7.2 0.8 copy.12
  7.9 0.1 broadcast_in_dim.6
  8.0 0.7 multiply_convert_fusion
  8.7 0.6 broadcast_in_dim.7
  9.4 15.2 %all-to-all-start = ((bf16[12,11,256]{2,1,0:T(8,128)(2,1)}), bf16[12,11,256]{2,1,0:T(8,128)(2,1)S(1)}, u32[]{:S(2)}, u32[]{:S(2)}) async-start(bf16[12,11,256]{2,1,0:T(8,128)(2,1)} %broadcast_in_dim.7), calls=%async_computation | async-start | bytes 196608 | tf_op jit(solution)/shard_map/weight_far/all_to_all | solution.py:131
  24.5 0.7 reshape.54.refs_2_.gain
  25.3 0.0 copy-start.3
  25.3 0.0 copy-start.5
  25.3 1.6 %copy-done.5 = bf16[256,4096]{1,0:T(8,128)(2,1)S(1)} copy-done((bf16[256,4096]{1,0:T(8,128)(2,1)S(1)}, bf16[256,4096]{1,0:T(8,128)(2,1)}, u32[]{:S(2)}) %copy-start.5) | copy-done | bytes 2097176
  26.9 0.0 copy-start.6
  26.9 1.0 copy-done.6
  27.8 0.0 copy-start.7
  27.8 1.0 copy-done.7
  28.8 2.1 %term.1 = (bf16[4,8,136,256]{3,2,1,0:T(8,128)(2,1)S(1)}, bf16[4,8,136,256]{3,2,1,0:T(8,128)(2,1)S(1)}, bf16[2,272,256]{2,1,0:T(8,128)(2,1)S(1)}, f32[256,128]{1,0:T(8,128)S(1)}) custom-call(s32[1]{0:T(128)} %bitcast.refs_0_, bf16[256,4096]{1,0:T(8,128)(2,1)S(1)} %copy-done.5, bf16[1,4096]{1,0:T(2,128)(2,1)S(1)} %reshape.54.refs_2_.gain, ...), custom_call_target="tpu_custom_call" | custom-call | flops 1660944384 | bytes 4194304 | tf_op jit(solution)/shard_map/term/pallas_call | solution.py:135
  30.9 0.0 copy-done.3
  30.9 0.0 copy-start.4
  30.9 1.4 copy-done.4
  32.3 0.0 copy-start.8
  32.3 0.7 copy-done.8
  32.9 3.6 %all-to-all-done = bf16[12,11,256]{2,1,0:T(8,128)(2,1)S(1)} async-done(((bf16[12,11,256]{2,1,0:T(8,128)(2,1)}), bf16[12,11,256]{2,1,0:T(8,128)(2,1)S(1)}, u32[]{:S(2)}, u32[]{:S(2)}) %all-to-all-start) | async-done | bytes 67616 | tf_op jit(solution)/shard_map/weight_far/all_to_all | solution.py:131
  36.5 1.9 %collective-permute-start = (bf16[4,8,136,256]{3,2,1,0:T(8,128)(2,1)}, bf16[4,8,136,256]{3,2,1,0:T(8,128)(2,1)}, u32[]{:S(2)}, u32[]{:S(2)}) collective-permute-start(bf16[4,8,136,256]{3,2,1,0:T(8,128)(2,1)} %copy-done.4), channel_id=1, source_target_pairs={{0,1},{1,0},{2,3},{3,2},{4,5},{5,4},{6,7},{7,6},{8,9},{9,8},{10,11... | collective-permute-start | bytes 6684680 | tf_op jit(solution)/shard_map/reduce_core/ppermute | solution.py:155
  38.5 0.7 broadcast_in_dim.8
  39.2 4.8 %all-to-all-start.1 = ((bf16[4,136,256]{2,1,0:T(8,128)(2,1)}), bf16[4,136,256]{2,1,0:T(8,128)(2,1)S(1)}, u32[]{:S(2)}, u32[]{:S(2)}) async-start(bf16[4,136,256]{2,1,0:T(8,128)(2,1)} %broadcast_in_dim.8), calls=%async_computation.1 | async-start | bytes 557056 | tf_op jit(solution)/shard_map/weight_x/all_to_all | solution.py:153
  44.0 0.0 all-gather.3.cloned.1.call-start
  44.0 0.0 collective-permute-done
  44.0 3.5 %add_convert_fusion = bf16[4,8,136,256]{3,2,1,0:T(8,128)(2,1)} fusion(bf16[4,8,136,256]{3,2,1,0:T(8,128)(2,1)} %collective-permute-done, bf16[4,8,136,256]{3,2,1,0:T(8,128)(2,1)S(1)} %get-tuple-element.30), kind=kLoop, calls=%fused_computation | loop fusion | flops 4456448 | bytes 6684672 | tf_op jit(solution)/shard_map/reduce_core/convert_element_type | solution.py:156
  47.5 1.9 %all-to-all-done.1 = bf16[4,136,256]{2,1,0:T(8,128)(2,1)S(1)} async-done(((bf16[4,136,256]{2,1,0:T(8,128)(2,1)}), bf16[4,136,256]{2,1,0:T(8,128)(2,1)S(1)}, u32[]{:S(2)}, u32[]{:S(2)}) %all-to-all-start.1) | async-done | bytes 278560 | tf_op jit(solution)/shard_map/weight_x/all_to_all | solution.py:153
  49.4 0.0 copy-start.9
  49.4 0.7 copy-done.9
  50.1 0.0 all-gather.3.cloned.1.call-update
  50.2 5.7 %all-to-all-start.2 = ((bf16[4,8,136,256]{3,2,1,0:T(8,128)(2,1)}), bf16[4,8,136,256]{3,2,1,0:T(8,128)(2,1)S(1)}, u32[]{:S(2)}, u32[]{:S(2)}) async-start(bf16[4,8,136,256]{3,2,1,0:T(8,128)(2,1)} %add_convert_fusion), calls=%async_computation.2 | async-start | bytes 4456448 | tf_op jit(solution)/shard_map/reduce_x/all_to_all | solution.py:162
  55.8 0.1 reduce_x.1.cot
  56.0 0.0 copy-start
  56.0 0.7 copy-done
  56.7 24.6 %all-to-all-done.2 = bf16[4,8,136,256]{3,2,1,0:T(8,128)(2,1)S(1)} async-done(((bf16[4,8,136,256]{3,2,1,0:T(8,128)(2,1)}), bf16[4,8,136,256]{3,2,1,0:T(8,128)(2,1)S(1)}, u32[]{:S(2)}, u32[]{:S(2)}) %all-to-all-start.2) | async-done | bytes 2228256 | tf_op jit(solution)/shard_map/reduce_x/all_to_all | solution.py:162
  81.3 1.1 fusion
  82.4 7.1 %all-to-all-start.3 = ((bf16[8,136,256]{2,1,0:T(8,128)(2,1)}), bf16[8,136,256]{2,1,0:T(8,128)(2,1)S(1)}, u32[]{:S(2)}, u32[]{:S(2)}) async-start(bf16[8,136,256]{2,1,0:T(8,128)(2,1)} %fusion), calls=%async_computation.3 | async-start | bytes 1114112 | tf_op jit(solution)/shard_map/reduce_y/all_to_all | solution.py:174
  89.5 9.1 %all-gather.3.cloned.1.call-done = bf16[64,136,256]{2,1,0:T(8,128)(2,1)} async-done(((bf16[4,136,256]{2,1,0:T(8,128)(2,1)}), bf16[64,136,256]{2,1,0:T(8,128)(2,1)}) %all-gather.3.cloned.1.call-update) | async-done | bytes 4456464 | tf_op jit(solution)/shard_map/weight_near/all_gather | solution.py:159
  98.6 8.5 %main.1 = (bf16[544,256]{1,0:T(8,128)(2,1)}, bf16[256,4096]{1,0:T(8,128)(2,1)}) custom-call(bf16[256,4096]{1,0:T(8,128)(2,1)} %tokens.1, bf16[1,4096]{1,0:T(2,128)(2,1)} %copy-done.3, bf16[256,544]{1,0:T(8,128)(2,1)} %copy-done, f32[256,128]{1,0:T(8,128)} %copy-done.8, bf16[4,2,2,4,136,256]{5,4,3,2,1,0:T(8,128)(2,1)} %bitcast.15), custom_call_target="tpu_custom_call" | custom-call | flops 2768240640 | bytes 10485760 | tf_op jit(solution)/shard_map/main/pallas_call | solution.py:177
  107.1 0.0 copy-start.1
  107.1 0.0 copy-start.2
  107.1 0.0 all-to-all-done.3
  107.2 0.1 fusion.5
  107.3 0.7 reshape.58
  107.9 15.1 %all-to-all-start.4 = ((bf16[12,11,256]{2,1,0:T(8,128)(2,1)}), bf16[12,11,256]{2,1,0:T(8,128)(2,1)S(1)}, u32[]{:S(2)}, u32[]{:S(2)}) async-start(bf16[12,11,256]{2,1,0:T(8,128)(2,1)} %reshape.58), calls=%async_computation.4 | async-start | bytes 196608 | tf_op jit(solution)/shard_map/reduce_z/all_to_all | solution.py:204
  123.1 0.0 copy-done.1
  123.1 0.0 copy-done.2
  123.1 1.1 reduce_z.1
  124.2 10.6 %all-to-all-done.4 = bf16[12,11,256]{2,1,0:T(8,128)(2,1)S(1)} async-done(((bf16[12,11,256]{2,1,0:T(8,128)(2,1)}), bf16[12,11,256]{2,1,0:T(8,128)(2,1)S(1)}, u32[]{:S(2)}, u32[]{:S(2)}) %all-to-all-start.4) | async-done | bytes 67616 | tf_op jit(solution)/shard_map/reduce_z/all_to_all | solution.py:204
  134.8 0.6 broadcast_multiply_fusion
  (7 shorter events, 0.1 us)
Async XLA Ops:
  9.4 27.1 %all-to-all-start = ((bf16[12,11,256]{2,1,0:T(8,128)(2,1)}), bf16[12,11,256]{2,1,0:T(8,128)(2,1)S(1)}, u32[]{:S(2)}, u32[]{:S(2)}) async-start(bf16[12,11,256]{2,1,0:T(8,128)(2,1)} %broadcast_in_dim.7), calls=%async_computation | async-start | bytes 196608 | tf_op jit(solution)/shard_map/weight_far/all_to_all | solution.py:131
  25.3 5.6 %copy-start.3 = (bf16[1,4096]{1,0:T(2,128)(2,1)}, bf16[1,4096]{1,0:T(2,128)(2,1)S(1)}, u32[]{:S(2)}) copy-start(bf16[1,4096]{1,0:T(2,128)(2,1)S(1)} %reshape.54.refs_2_.gain) | copy-start | bytes 24580
  25.3 1.6 %copy-start.5 = (bf16[256,4096]{1,0:T(8,128)(2,1)S(1)}, bf16[256,4096]{1,0:T(8,128)(2,1)}, u32[]{:S(2)}) copy-start(bf16[256,4096]{1,0:T(8,128)(2,1)} %tokens.1) | copy-start | bytes 6291460
  26.9 1.0 copy-start.6
  27.8 1.0 copy-start.7
  30.9 1.4 copy-start.4
  32.3 0.7 copy-start.8
  36.5 7.5 %collective-permute-start = (bf16[4,8,136,256]{3,2,1,0:T(8,128)(2,1)}, bf16[4,8,136,256]{3,2,1,0:T(8,128)(2,1)}, u32[]{:S(2)}, u32[]{:S(2)}) collective-permute-start(bf16[4,8,136,256]{3,2,1,0:T(8,128)(2,1)} %copy-done.4), channel_id=1, source_target_pairs={{0,1},{1,0},{2,3},{3,2},{4,5},{5,4},{6,7},{7,6},{8,9},{9,8},{10,11... | collective-permute-start | bytes 6684680 | tf_op jit(solution)/shard_map/reduce_core/ppermute | solution.py:155
  39.2 10.2 %all-to-all-start.1 = ((bf16[4,136,256]{2,1,0:T(8,128)(2,1)}), bf16[4,136,256]{2,1,0:T(8,128)(2,1)S(1)}, u32[]{:S(2)}, u32[]{:S(2)}) async-start(bf16[4,136,256]{2,1,0:T(8,128)(2,1)} %broadcast_in_dim.8), calls=%async_computation.1 | async-start | bytes 557056 | tf_op jit(solution)/shard_map/weight_x/all_to_all | solution.py:153
  44.0 54.7 %all-gather.3.cloned.1.call-start = ((), (), s32[]{:S(2)}) async-start(), calls=%async_computation.5 | async-start | bytes 4734976 | tf_op jit(solution)/shard_map/weight_near/all_gather | solution.py:159
  49.4 0.7 copy-start.9
  50.2 31.2 %all-to-all-start.2 = ((bf16[4,8,136,256]{3,2,1,0:T(8,128)(2,1)}), bf16[4,8,136,256]{3,2,1,0:T(8,128)(2,1)S(1)}, u32[]{:S(2)}, u32[]{:S(2)}) async-start(bf16[4,8,136,256]{3,2,1,0:T(8,128)(2,1)} %add_convert_fusion), calls=%async_computation.2 | async-start | bytes 4456448 | tf_op jit(solution)/shard_map/reduce_x/all_to_all | solution.py:162
  56.0 0.8 copy-start
  82.4 24.7 %all-to-all-start.3 = ((bf16[8,136,256]{2,1,0:T(8,128)(2,1)}), bf16[8,136,256]{2,1,0:T(8,128)(2,1)S(1)}, u32[]{:S(2)}, u32[]{:S(2)}) async-start(bf16[8,136,256]{2,1,0:T(8,128)(2,1)} %fusion), calls=%async_computation.3 | async-start | bytes 1114112 | tf_op jit(solution)/shard_map/reduce_y/all_to_all | solution.py:174
  107.1 16.0 %copy-start.1 = (bf16[544,256]{1,0:T(8,128)(2,1)S(1)}, bf16[544,256]{1,0:T(8,128)(2,1)}, u32[]{:S(2)}) copy-start(bf16[544,256]{1,0:T(8,128)(2,1)} %get-tuple-element.45.grouped) | copy-start | bytes 835588
  107.1 16.0 %copy-start.2 = (s32[528,1]{1,0:T(8,128)S(1)}, s32[528,1]{1,0:T(8,128)}, u32[]{:S(2)}) copy-start(s32[528,1]{1,0:T(8,128)} %constant.17.clone.order) | copy-start | bytes 6340
  107.9 26.9 %all-to-all-start.4 = ((bf16[12,11,256]{2,1,0:T(8,128)(2,1)}), bf16[12,11,256]{2,1,0:T(8,128)(2,1)S(1)}, u32[]{:S(2)}, u32[]{:S(2)}) async-start(bf16[12,11,256]{2,1,0:T(8,128)(2,1)} %reshape.58), calls=%async_computation.4 | async-start | bytes 196608 | tf_op jit(solution)/shard_map/reduce_z/all_to_all | solution.py:204
Sparse Core Ops, SparseCore 0:
  50.3 48.3 all-gather.2
